TPU v7x, 32 devices: a whole 2x2x4 slice. The times are simulated.
32 devices in a mesh: section: 2 (over core), dp: 16 (over z, y, x).
Axes of the slice: x: 2, y: 2, z: 4, core: 2. Of those that a mesh axis runs over, the one named last changes fastest.
Arguments:
- tokens: bfloat16 [32, 1024, 768], P('dp'), may hold values from -6 to 6
- segments: int32 [32, 1024], P('dp'), may hold values from 0 to 3, never falling along the last dimension, each value on 1 to 512 neighbouring positions
- cotangent: bfloat16 [32, 1024, 768], P('dp'), may hold values from -6 to 6
- gain_attn: float32 [2, 768], P('section', 'dp'), may hold values from 0.1 to 1.9
- gain_ffn: float32 [2, 768], P('section', 'dp'), may hold values from 0.1 to 1.9
- w_query: float32 [2, 768, 768], P('section', 'dp'), may hold values from -0.21875 to 0.21875
- w_key: float32 [2, 768, 768], P('section', 'dp'), may hold values from -0.21875 to 0.21875
- w_value: float32 [2, 768, 768], P('section', 'dp'), may hold values from -0.21875 to 0.21875
- w_out: float32 [2, 768, 768], P('section', None, 'dp'), may hold values from -0.875 to 0.875
- w_in: float32 [2, 768, 3072], P('section', 'dp'), may hold values from -0.21875 to 0.21875
- w_back: float32 [2, 3072, 768], P('section', None, 'dp'), may hold values from -0.15625 to 0.15625
- mix_logits: float32 [2, 12, 12], P('section'), may hold values from -1.75 to 1.75
- mix_weights: float32 [2, 12, 12], P('section'), may hold values from -1.75 to 1.75
Outputs:
- section_out: bfloat16 [2, 32, 1024, 768], P('section', 'dp')
- section_grad: bfloat16 [2, 32, 1024, 768], P('section', 'dp')
- grad_gain_attn: float32 [2, 768], P('section', 'dp')
- grad_gain_ffn: float32 [2, 768], P('section', 'dp')
- grad_query: float32 [2, 768, 768], P('section', 'dp')
- grad_key: float32 [2, 768, 768], P('section', 'dp')
- grad_value: float32 [2, 768, 768], P('section', 'dp')
- grad_out: float32 [2, 768, 768], P('section', None, 'dp')
- grad_in: float32 [2, 768, 3072], P('section', 'dp')
- grad_back: float32 [2, 3072, 768], P('section', None, 'dp')
- grad_mix_logits: float32 [2, 12, 12], P('section')
- grad_mix_weights: float32 [2, 12, 12], P('section')
Inputs may be any that keep to these rules, and one draw needn't show every extreme that they name: `segments`: along each row the segment number never falls; each segment covers at most 512 positions.
All inputs are finite; a program needn't handle non-finite values.
Results may differ from a plain program's by a relative error of at most 0.035.
The roundings to bfloat16 on the way count: a program that leaves them out, or rounds other values in their place, can miss the bound.
Values may be sent and summed in bfloat16 or wider, within the bound.
No kernel may reach another device: no remote copies, remote signals or barrier semaphores. Data moves between devices by JAX's collectives and lax.ppermute only.
A program may use at most 640 MiB of HBM per device.

v0:
```python
import jax
import jax.numpy as jnp
from jax import lax
from jax.sharding import PartitionSpec as P

MICRO = 2


EPS = 1e-06
HIGH = lax.Precision.HIGHEST
NEGATIVE = -1e30


def shifted(x, axis, by):
    size = lax.axis_size(axis)
    pairs = [(i, i + by) for i in range(size) if 0 <= i + by < size]
    return lax.ppermute(x, axis, pairs)


def rms_scale(values, gain):
    return values * lax.rsqrt(jnp.mean(values * values, axis=-1, keepdims=True) + EPS) * gain


def flat_dot(left, right):
    result = jnp.dot(left.reshape(-1, left.shape[-1]), right, preferred_element_type=jnp.float32)
    return result.reshape(left.shape[:-1] + (right.shape[-1],))


def weight_grad(left, right):
    return jnp.einsum("rtd,rth->dh", left, right, preferred_element_type=jnp.float32)


def back_dot(grad_rows, weight):
    return jnp.einsum("rth,dh->rtd", grad_rows, weight, preferred_element_type=jnp.float32)


def block_scores(
    query_block, key_block, segment_query, segment_key, first_row, mix_logits, head_count
):
    rows_query = query_block.shape[0]
    rows_key = key_block.shape[0]
    head_size = query_block.shape[1] // head_count
    query_heads = query_block.reshape(rows_query, head_count, head_size)
    key_heads = key_block.reshape(rows_key, head_count, head_size)
    scores = jnp.einsum(
        "qhe,khe->hqk", query_heads, key_heads, preferred_element_type=jnp.float32
    ) * head_size ** (-0.5)
    premixed = jnp.einsum("hqk,hg->gqk", scores, mix_logits, precision=HIGH)
    place_query = first_row + jnp.arange(rows_query)
    place_key = jnp.arange(rows_key)
    allowed = (segment_query[:, None] == segment_key[None, :]) & (
        place_key[None, :] <= place_query[:, None]
    )
    return (scores, jnp.where(allowed[None], premixed, NEGATIVE))


def attend_row(queries, keys_all, values_all, segment, mix_logits, mix_weights):
    length = queries.shape[0]
    head_count = mix_logits.shape[0]
    head_size = queries.shape[1] // head_count
    block_rows = min(512, length)
    outputs = []
    totals = []
    for block_index in range(length // block_rows):
        first_row = block_index * block_rows
        finish = first_row + block_rows
        scores, premixed = block_scores(
            queries[first_row:finish],
            keys_all[:finish],
            segment[first_row:finish],
            segment[:finish],
            first_row,
            mix_logits,
            head_count,
        )
        largest = jnp.max(premixed, axis=-1, keepdims=True)
        exponent = jnp.exp(premixed - largest)
        summed = jnp.sum(exponent, axis=-1, keepdims=True)
        softened = exponent / summed
        totals.append((largest + jnp.log(summed))[:, :, 0])
        remixed = jnp.einsum("gqk,gh->hqk", softened, mix_weights, precision=HIGH).astype(
            jnp.bfloat16
        )
        value_heads = values_all[:finish].reshape(finish, head_count, head_size)
        attended = jnp.einsum(
            "hqk,khe->qhe", remixed, value_heads, preferred_element_type=jnp.float32
        )
        outputs.append(attended.reshape(block_rows, head_count * head_size).astype(jnp.bfloat16))
    return (jnp.concatenate(outputs, 0), jnp.concatenate(totals, 1))


def attend_row_back(
    queries, keys_all, values_all, segment, totals, grad_attended, mix_logits, mix_weights
):
    length = queries.shape[0]
    head_count = mix_logits.shape[0]
    head_size = queries.shape[1] // head_count
    scale = head_size ** (-0.5)
    block_rows = min(512, length)
    grad_keys = jnp.zeros((length, head_count, head_size), jnp.float32)
    grad_values = jnp.zeros((length, head_count, head_size), jnp.float32)
    grad_logit_mix = jnp.zeros((head_count, head_count), jnp.float32)
    grad_weight_mix = jnp.zeros((head_count, head_count), jnp.float32)
    grad_queries = []
    for block_index in range(length // block_rows):
        first_row = block_index * block_rows
        finish = first_row + block_rows
        scores, premixed = block_scores(
            queries[first_row:finish],
            keys_all[:finish],
            segment[first_row:finish],
            segment[:finish],
            first_row,
            mix_logits,
            head_count,
        )
        softened = jnp.exp(premixed - totals[:, first_row:finish, None])
        remixed = jnp.einsum("gqk,gh->hqk", softened, mix_weights, precision=HIGH).astype(
            jnp.bfloat16
        )
        out_heads = grad_attended[first_row:finish].reshape(block_rows, head_count, head_size)
        value_heads = values_all[:finish].reshape(finish, head_count, head_size)
        key_heads = keys_all[:finish].reshape(finish, head_count, head_size)
        query_heads = queries[first_row:finish].reshape(block_rows, head_count, head_size)
        grad_remixed = jnp.einsum(
            "qhe,khe->hqk", out_heads, value_heads, preferred_element_type=jnp.float32
        )
        grad_values = grad_values.at[:finish].add(
            jnp.einsum("hqk,qhe->khe", remixed, out_heads, preferred_element_type=jnp.float32)
        )
        grad_weight_mix = grad_weight_mix + jnp.einsum(
            "gqk,hqk->gh", softened, grad_remixed, precision=HIGH
        )
        grad_softened = jnp.einsum("hqk,gh->gqk", grad_remixed, mix_weights, precision=HIGH)
        grad_premixed = softened * (
            grad_softened - jnp.sum(grad_softened * softened, axis=-1, keepdims=True)
        )
        grad_logit_mix = grad_logit_mix + jnp.einsum(
            "hqk,gqk->hg", scores, grad_premixed, precision=HIGH
        )
        grad_scores = jnp.einsum("gqk,hg->hqk", grad_premixed, mix_logits, precision=HIGH).astype(
            jnp.bfloat16
        )
        block_grad = (
            jnp.einsum("hqk,khe->qhe", grad_scores, key_heads, preferred_element_type=jnp.float32)
            * scale
        )
        grad_queries.append(block_grad.reshape(block_rows, head_count * head_size))
        grad_keys = grad_keys.at[:finish].add(
            jnp.einsum("hqk,qhe->khe", grad_scores, query_heads, preferred_element_type=jnp.float32)
            * scale
        )
    all_queries = jnp.concatenate(grad_queries, 0).astype(jnp.bfloat16)
    all_keys = grad_keys.reshape(length, head_count * head_size).astype(jnp.bfloat16)
    all_values = grad_values.reshape(length, head_count * head_size).astype(jnp.bfloat16)
    return (all_queries, all_keys, all_values, grad_logit_mix, grad_weight_mix)


def layer_forward(inputs_low, segment_rows, weights, mixes):
    gain_attn, gain_ffn, w_query, w_key, w_value, w_out, w_in, w_back = weights
    mix_logits, mix_weights = mixes
    inputs = inputs_low.astype(jnp.float32)
    normed = rms_scale(inputs, gain_attn.astype(jnp.float32)).astype(jnp.bfloat16)
    queries = flat_dot(normed, w_query).astype(jnp.bfloat16)
    keys_all = flat_dot(normed, w_key).astype(jnp.bfloat16)
    values_all = flat_dot(normed, w_value).astype(jnp.bfloat16)

    def row_attend(row_parts):
        return attend_row(
            row_parts[0], row_parts[1], row_parts[2], row_parts[3], mix_logits, mix_weights
        )

    attended, totals = lax.map(row_attend, (queries, keys_all, values_all, segment_rows))
    middle = inputs + flat_dot(attended, w_out)
    normed_two = rms_scale(middle, gain_ffn.astype(jnp.float32)).astype(jnp.bfloat16)
    before = flat_dot(normed_two, w_in)
    hidden = jax.nn.gelu(before).astype(jnp.bfloat16)
    result = middle + flat_dot(hidden, w_back)
    kept = (
        inputs_low,
        normed,
        queries,
        keys_all,
        values_all,
        totals,
        attended,
        middle,
        normed_two,
        before,
        hidden,
    )
    return (result.astype(jnp.bfloat16), kept)


def layer_backward(grad_result, segment_rows, kept, weights, mixes):
    gain_attn, gain_ffn, w_query, w_key, w_value, w_out, w_in, w_back = weights
    mix_logits, mix_weights = mixes
    (
        inputs_low,
        normed,
        queries,
        keys_all,
        values_all,
        totals,
        attended,
        middle,
        normed_two,
        before,
        hidden,
    ) = kept
    grad_branch = grad_result.astype(jnp.bfloat16)
    grad_back = weight_grad(hidden, grad_branch)
    grad_hidden = back_dot(grad_branch, w_back)
    grad_before = jax.vjp(jax.nn.gelu, before)[1](grad_hidden)[0].astype(jnp.bfloat16)
    grad_in = weight_grad(normed_two, grad_before)
    grad_normed_two = back_dot(grad_before, w_in)
    grad_middle_norm, grad_gain_ffn = jax.vjp(rms_scale, middle, gain_ffn.astype(jnp.float32))[1](
        grad_normed_two
    )
    grad_middle = grad_result + grad_middle_norm
    grad_attn_branch = grad_middle.astype(jnp.bfloat16)
    grad_out = weight_grad(attended, grad_attn_branch)
    grad_attended = back_dot(grad_attn_branch, w_out).astype(jnp.bfloat16)

    def row_back(row_parts):
        return attend_row_back(
            row_parts[0],
            row_parts[1],
            row_parts[2],
            row_parts[3],
            row_parts[4],
            row_parts[5],
            mix_logits,
            mix_weights,
        )

    grad_queries, grad_keys, grad_values, logit_rows, weight_rows = lax.map(
        row_back, (queries, keys_all, values_all, segment_rows, totals, grad_attended)
    )
    grad_query = weight_grad(normed, grad_queries)
    grad_key = weight_grad(normed, grad_keys)
    grad_value = weight_grad(normed, grad_values)
    grad_normed = (
        back_dot(grad_queries, w_query)
        + back_dot(grad_keys, w_key)
        + back_dot(grad_values, w_value)
    )
    inputs = inputs_low.astype(jnp.float32)
    grad_inputs_norm, grad_gain_attn = jax.vjp(rms_scale, inputs, gain_attn.astype(jnp.float32))[1](
        grad_normed
    )
    grad_inputs = grad_middle + grad_inputs_norm
    layer_grads = (
        grad_gain_attn,
        grad_gain_ffn,
        grad_query,
        grad_key,
        grad_value,
        grad_out,
        grad_in,
        grad_back,
    )
    mix_grads = (jnp.sum(logit_rows, axis=0), jnp.sum(weight_rows, axis=0))
    return (grad_inputs.astype(jnp.bfloat16), layer_grads, mix_grads)


def on_device(
    tokens,
    segments,
    cotangent,
    gain_attn,
    gain_ffn,
    w_query,
    w_key,
    w_value,
    w_out,
    w_in,
    w_back,
    mix_logits,
    mix_weights,
):
    section = lax.axis_index("section")
    rows_dev = tokens.shape[0]
    length = tokens.shape[1]
    width = tokens.shape[2]
    per_batch = rows_dev // MICRO
    head_count = mix_logits.shape[1]
    hidden_width = w_query.shape[2]
    ffn_width = w_in.shape[2]
    mixes = (mix_logits[0], mix_weights[0])
    gathered = (
        lax.all_gather(gain_attn.astype(jnp.bfloat16), "dp", axis=1, tiled=True),
        lax.all_gather(gain_ffn.astype(jnp.bfloat16), "dp", axis=1, tiled=True),
        lax.all_gather(w_query.astype(jnp.bfloat16), "dp", axis=1, tiled=True),
        lax.all_gather(w_key.astype(jnp.bfloat16), "dp", axis=1, tiled=True),
        lax.all_gather(w_value.astype(jnp.bfloat16), "dp", axis=1, tiled=True),
        lax.all_gather(w_out.astype(jnp.bfloat16), "dp", axis=2, tiled=True),
        lax.all_gather(w_in.astype(jnp.bfloat16), "dp", axis=1, tiled=True),
        lax.all_gather(w_back.astype(jnp.bfloat16), "dp", axis=2, tiled=True),
    )
    weights = tuple((piece[0] for piece in gathered))

    def buffer(columns, dtype):
        return jnp.zeros((MICRO, per_batch, length, columns), dtype)

    store = (
        buffer(width, jnp.bfloat16),
        buffer(width, jnp.bfloat16),
        buffer(width, jnp.bfloat16),
        buffer(hidden_width, jnp.bfloat16),
        buffer(hidden_width, jnp.bfloat16),
        buffer(hidden_width, jnp.bfloat16),
        jnp.zeros((MICRO, per_batch, head_count, length), jnp.float32),
        buffer(hidden_width, jnp.bfloat16),
        buffer(width, jnp.float32),
        buffer(width, jnp.bfloat16),
        buffer(ffn_width, jnp.float32),
        buffer(ffn_width, jnp.bfloat16),
    )
    received = jnp.zeros((per_batch, length, width), jnp.bfloat16)
    for micro_turn in range(MICRO + 1):
        slot_raw = micro_turn - section
        active = (slot_raw >= 0) & (slot_raw < MICRO)
        slot_index = jnp.clip(slot_raw, 0, MICRO - 1)
        first_local = min(micro_turn, MICRO - 1) * per_batch
        layer_inputs = jnp.where(
            section == 0, tokens[first_local : first_local + per_batch], received
        )
        segment_rows = lax.dynamic_slice_in_dim(segments, slot_index * per_batch, per_batch, 0)

        def run_forward(current):
            result, kept = layer_forward(layer_inputs, segment_rows, weights, mixes)
            return tuple(
                (
                    lax.dynamic_update_index_in_dim(holder, value, slot_index, 0)
                    for holder, value in zip(current, (result,) + kept)
                )
            )

        store = lax.cond(active, run_forward, lambda current: current, store)
        if micro_turn < MICRO:
            outgoing = lax.dynamic_index_in_dim(store[0], slot_index, 0, keepdims=False)
            received = shifted(outgoing, "section", 1)
    carried = tuple((jnp.zeros(piece.shape, jnp.float32) for piece in weights))
    carried = carried + (
        jnp.zeros((head_count, head_count), jnp.float32),
        jnp.zeros((head_count, head_count), jnp.float32),
        buffer(width, jnp.bfloat16),
    )
    incoming = jnp.zeros((per_batch, length, width), jnp.bfloat16)
    for micro_turn in range(MICRO + 1):
        slot_raw = micro_turn - 1 + section
        active = (slot_raw >= 0) & (slot_raw < MICRO)
        slot_index = jnp.clip(slot_raw, 0, MICRO - 1)
        first_local = min(micro_turn, MICRO - 1) * per_batch
        grad_rows = jnp.where(
            section == 1, cotangent[first_local : first_local + per_batch], incoming
        )
        segment_rows = lax.dynamic_slice_in_dim(segments, slot_index * per_batch, per_batch, 0)

        def run_backward(current):
            kept = tuple(
                (
                    lax.dynamic_index_in_dim(holder, slot_index, 0, keepdims=False)
                    for holder in store[1:]
                )
            )
            grad_inputs, layer_grads, mix_grads = layer_backward(
                grad_rows.astype(jnp.float32), segment_rows, kept, weights, mixes
            )
            summed = tuple(
                (left + right for left, right in zip(current[:10], layer_grads + mix_grads))
            )
            return summed + (
                lax.dynamic_update_index_in_dim(current[10], grad_inputs, slot_index, 0),
            )

        carried = lax.cond(active, run_backward, lambda current: current, carried)
        if micro_turn < MICRO:
            outgoing = lax.dynamic_index_in_dim(carried[10], slot_index, 0, keepdims=False)
            incoming = shifted(outgoing, "section", -1)
    sharded = (
        lax.psum_scatter(carried[0][None], "dp", scatter_dimension=1, tiled=True),
        lax.psum_scatter(carried[1][None], "dp", scatter_dimension=1, tiled=True),
        lax.psum_scatter(carried[2][None], "dp", scatter_dimension=1, tiled=True),
        lax.psum_scatter(carried[3][None], "dp", scatter_dimension=1, tiled=True),
        lax.psum_scatter(carried[4][None], "dp", scatter_dimension=1, tiled=True),
        lax.psum_scatter(carried[5][None], "dp", scatter_dimension=2, tiled=True),
        lax.psum_scatter(carried[6][None], "dp", scatter_dimension=1, tiled=True),
        lax.psum_scatter(carried[7][None], "dp", scatter_dimension=2, tiled=True),
    )
    mix_sums = lax.psum((carried[8], carried[9]), "dp")
    section_out = store[0].reshape((1, rows_dev, length, width))
    section_grad = carried[10].reshape((1, rows_dev, length, width))
    return (
        section_out,
        section_grad,
        sharded[0],
        sharded[1],
        sharded[2],
        sharded[3],
        sharded[4],
        sharded[5],
        sharded[6],
        sharded[7],
        mix_sums[0][None],
        mix_sums[1][None],
    )


def solution(mesh):
    return jax.shard_map(
        on_device,
        mesh=mesh,
        in_specs=(
            P("dp", None, None),
            P("dp", None),
            P("dp", None, None),
            P("section", "dp"),
            P("section", "dp"),
            P("section", "dp", None),
            P("section", "dp", None),
            P("section", "dp", None),
            P("section", None, "dp"),
            P("section", "dp", None),
            P("section", None, "dp"),
            P("section", None, None),
            P("section", None, None),
        ),
        out_specs=(
            P("section", "dp", None, None),
            P("section", "dp", None, None),
            P("section", "dp"),
            P("section", "dp"),
            P("section", "dp", None),
            P("section", "dp", None),
            P("section", "dp", None),
            P("section", None, "dp"),
            P("section", "dp", None),
            P("section", None, "dp"),
            P("section", None, None),
            P("section", None, None),
        ),
        check_vma=False,
    )
```

profile of v0, /device:TPU:1, one launch (start us, length us, event | category | flops | bytes accessed | tf_op | source)
XLA Modules:
  0.0 5155.2 jit_solution(2225544202347755530)
XLA Ops:
  243.5 83.2 %all-gather.15.cloned.1.call-done = bf16[1,768,3072]{2,1,0:T(8,128)(2,1)} async-done(((bf16[1,48,3072]{2,1,0:T(8,128)(2,1)}), bf16[1,768,3072]{2,1,0:T(8,128)(2,1)}) %all-gather.15.cloned.1.call-update) | async-done | bytes 4718608 | tf_op jit(solution)/shard_map/all_gather | solution.py:298
  326.7 82.3 %all-gather.17.cloned.1.call-done = bf16[1,3072,768]{1,2,0:T(8,128)(2,1)} async-done(((bf16[1,3072,48]{1,2,0:T(8,128)(2,1)}), bf16[1,3072,768]{1,2,0:T(8,128)(2,1)}) %all-gather.17.cloned.1.call-update) | async-done | bytes 4718608 | tf_op jit(solution)/shard_map/all_gather | solution.py:299
  459.7 321.7 %collective-permute-done = bf16[1,1024,768]{2,1,0:T(8,128)(2,1)} collective-permute-done((bf16[1,1024,768]{2,1,0:T(8,128)(2,1)}, bf16[1,1024,768]{2,1,0:T(8,128)(2,1)}, u32[]{:S(2)}, u32[]{:S(2)}) %collective-permute-start) | collective-permute-done | bytes 1572896 | tf_op jit(solution)/shard_map/ppermute | solution.py:17
  782.5 325.7 %conditional.7 = ((bf16[2,1,1024,768]{2,3,1,0:T(8,128)(2,1)}, bf16[2,1,1024,768]{2,3,1,0:T(8,128)(2,1)}, bf16[2,1,1024,768]{2,3,1,0:T(8,128)(2,1)S(1)}, bf16[2,1...) conditional(s32[]{:T(128)} %convert_element_type.623, ...), branch_computations={%region_8.9_spmd, %region_9.16_spmd.clone} | conditional | flops 19817304064 | bytes 520608832 | solution.py:340
  908.4 81.4 %bitcast_reduce_fusion.4 = (f32[12,512]{0,1:T(8,128)S(1)}, f32[512,1024,12]{1,2,0:T(8,128)}) fusion(pred[512,1024]{1,0:T(8,128)(4,1)S(1)} %copy-done.104, f32[12,12]{1,0:T(8,128)S(1)} %get-tuple-element.2357, f32[12,512,1024]{2,1,0:T(8,128)} %broadcast_multiply_fusion.8), kind=kOutput, calls=%fused_computation.524 | convolution fusion | flops 918546432 | bytes 50881088 | tf_op jit(solution)/shard_map/cond/branch_1_fun/while/body/eval_jaxpr/hqk,hg->gqk/dot_general | solution.py:48
  1116.5 333.4 %conditional.8 = (bf16[2,1,1024,768]{2,3,1,0:T(8,128)(2,1)}, bf16[2,1,1024,768]{2,3,1,0:T(8,128)(2,1)S(1)}, bf16[2,1,1024,768]{2,3,1,0:T(8,128)(2,1)}, bf16[2,1,...) conditional(s32[]{:T(128)} %convert_element_type.622, ...), branch_computations={%region_16.17_spmd, %region_17.24_spmd} | conditional | flops 19817304064 | bytes 527571968 | solution.py:340
  1240.8 81.4 %bitcast_reduce_fusion.2 = (f32[12,512]{0,1:T(8,128)S(1)}, f32[512,1024,12]{1,2,0:T(8,128)}) fusion(pred[512,1024]{1,0:T(8,128)(4,1)S(1)} %copy-done.102, f32[12,12]{1,0:T(8,128)S(1)} %get-tuple-element.2222, f32[12,512,1024]{2,1,0:T(8,128)} %broadcast_multiply_fusion.2), kind=kOutput, calls=%fused_computation.92 | convolution fusion | flops 918546432 | bytes 50881088 | tf_op jit(solution)/shard_map/cond/branch_1_fun/while/body/eval_jaxpr/hqk,hg->gqk/dot_general | solution.py:48
  1451.7 842.7 %conditional.9 = (f32[768]{0:T(1024)S(1)}, f32[768]{0:T(1024)}, f32[768,768]{1,0:T(8,128)}, f32[768,768]{1,0:T(8,128)}, f32[768,768]{1,0:T(8,128)}, /*index=5*/f...) conditional(s32[]{:T(128)} %convert_element_type.635, ...), branch_computations={%region_24.25_spmd, %region_25.34_spmd} | conditional | flops 43446042624 | bytes 1588861184 | solution.py:378
  1789.5 59.8 %fusion.140 = f32[512,1024,12]{1,2,0:T(8,128)} fusion(f32[12,512,1024]{2,1,0:T(8,128)} %broadcast_multiply_fusion.4, f32[12,12]{1,0:T(8,128)S(1)} %get-tuple-element.1258), kind=kOutput, calls=%fused_computation.190 | convolution fusion | flops 905969664 | bytes 50332224 | tf_op jit(solution)/shard_map/cond/branch_1_fun/while/body/eval_jaxpr/hqk,hg->gqk/dot_general | solution.py:48
  2002.8 87.1 %fusion.142 = (f32[12,512]{0,1:T(8,128)S(1)}, f32[512,1024,12]{1,2,0:T(8,128)}) fusion(f32[12,512]{0,1:T(8,128)} %get-tuple-element.2549, f32[512,1024,12]{1,2,0:T(8,128)} %fusion.140, pred[512,1024]{1,0:T(8,128)(4,1)S(1)} %copy-done.25, f32[12,12]{0,1:T(8,128)S(1)} %get-tuple-element.1268, f32[12,512,1024]{2,1,0:T(8,128)} %fusion.765), kind=kOutput, calls=%fused_computation.194 | convolution fusion | flops 931129344 | bytes 76071488 | tf_op jit(solution)/shard_map/cond/branch_1_fun/while/body/eval_jaxpr/hqk,gh->gqk/dot_general | solution.py:134
  2176.5 62.3 %fusion.269 = f32[12,12]{1,0:T(8,128)} fusion(f32[12,12]{1,0:T(8,128)S(1)} %copy-done.205, f32[12,512,1024]{2,1,0:T(8,128)} %broadcast_multiply_fusion.4, f32[12,512,1024]{2,0,1:T(8,128)} %fusion.907), kind=kOutput, calls=%fused_computation.309 | convolution fusion | flops 905969792 | bytes 50332800 | tf_op jit(solution)/shard_map/cond/branch_1_fun/while/body/eval_jaxpr/hqk,gqk->hg/dot_general | solution.py:138
  2301.9 852.1 %conditional.10 = ((f32[768]{0:T(1024)}, f32[768]{0:T(1024)}, f32[768,768]{1,0:T(8,128)}, f32[768,768]{1,0:T(8,128)}, f32[768,768]{1,0:T(8,128)}, /*index=5*/f32...) conditional(s32[]{:T(128)} %convert_element_type.634, ...), branch_computations={%region_34.35_spmd, %region_35.44_spmd.clone.clone} | conditional | flops 43453906944 | bytes 1606224640 | solution.py:378
  2647.9 59.6 %fusion.565 = f32[512,1024,12]{1,2,0:T(8,128)} fusion(f32[12,512,1024]{2,1,0:T(8,128)} %broadcast_multiply_fusion.10, f32[12,12]{1,0:T(8,128)S(1)} %get-tuple-element.2413), kind=kOutput, calls=%fused_computation.622 | convolution fusion | flops 905969664 | bytes 50332224 | tf_op jit(solution)/shard_map/cond/branch_1_fun/while/body/eval_jaxpr/hqk,hg->gqk/dot_general | solution.py:48
  2862.4 87.3 %fusion.567 = (f32[12,512]{0,1:T(8,128)S(1)}, f32[512,1024,12]{1,2,0:T(8,128)}) fusion(f32[12,512]{0,1:T(8,128)} %get-tuple-element.2611, f32[512,1024,12]{1,2,0:T(8,128)} %fusion.565, pred[512,1024]{1,0:T(8,128)(4,1)S(1)} %copy-done.27, f32[12,12]{0,1:T(8,128)S(1)} %get-tuple-element.2423, f32[12,512,1024]{2,1,0:T(8,128)} %fusion.771), kind=kOutput, calls=%fused_computation.626 | convolution fusion | flops 931129344 | bytes 76071488 | tf_op jit(solution)/shard_map/cond/branch_1_fun/while/body/eval_jaxpr/hqk,gh->gqk/dot_general | solution.py:134
  3036.3 61.4 %fusion.715 = f32[12,12]{1,0:T(8,128)S(1)} fusion(f32[12,12]{1,0:T(8,128)S(1)} %copy-done.170, f32[12,12]{1,0:T(8,128)S(1)} %copy-done.206, f32[12,512,1024]{2,1,0:T(8,128)} %broadcast_multiply_fusion.10, f32[12,512,1024]{2,0,1:T(8,128)} %fusion.913), kind=kOutput, calls=%fused_computation.748 | convolution fusion | flops 905969920 | bytes 50333376 | tf_op jit(solution)/shard_map/cond/branch_1_fun/while/body/eval_jaxpr/hqk,gqk->hg/dot_general | solution.py:138
  3185.6 60.2 %all-reduce.8 = (f32[1,12,12]{2,0,1:T(1,128)}, f32[1,12,12]{2,0,1:T(1,128)}) all-reduce(f32[1,12,12]{2,0,1:T(1,128)S(1)} %broadcast_in_dim.641, f32[1,12,12]{2,0,1:T(1,128)S(1)} %broadcast_in_dim.642), channel_id=1, replica_groups=mesh['section'=2,'dp'=16] {'dp'}, use_global_device_ids=true, to_apply=%region_62.63 | all-reduce | flops 288 | bytes 2304 | tf_op jit(solution)/shard_map/psum | solution.py:392
  3245.8 891.9 %reduce-scatter.25.cloned.1.call-done = f32[48,1]{1,0:T(8,128)} async-done(((f32[768,1]{1,0:T(8,128)}), f32[48,1]{1,0:T(8,128)}) %reduce-scatter.25.cloned.1.call-update) | async-done | bytes 208
  4139.0 124.7 %reduce-scatter.27.cloned.1.call-done = f32[48,1]{1,0:T(8,128)} async-done(((f32[768,1]{1,0:T(8,128)}), f32[48,1]{1,0:T(8,128)}) %reduce-scatter.27.cloned.1.call-update) | async-done | bytes 208
  4265.1 130.9 %reduce-scatter.13.cloned.1.call-done = f32[1,48,768]{2,1,0:T(8,128)} async-done(((f32[1,768,768]{2,1,0:T(8,128)}), f32[1,48,768]{2,1,0:T(8,128)}) %reduce-scatter.13.cloned.1.call-update) | async-done | bytes 147472 | tf_op jit(solution)/shard_map/reduce_scatter | solution.py:385
  4396.0 132.7 %reduce-scatter.15.cloned.1.call-done = f32[1,48,768]{2,1,0:T(8,128)} async-done(((f32[1,768,768]{2,1,0:T(8,128)}), f32[1,48,768]{2,1,0:T(8,128)}) %reduce-scatter.15.cloned.1.call-update) | async-done | bytes 147472 | tf_op jit(solution)/shard_map/reduce_scatter | solution.py:386
  4528.7 132.3 %reduce-scatter.17.cloned.1.call-done = f32[1,48,768]{2,1,0:T(8,128)} async-done(((f32[1,768,768]{2,1,0:T(8,128)}), f32[1,48,768]{2,1,0:T(8,128)}) %reduce-scatter.17.cloned.1.call-update) | async-done | bytes 147472 | tf_op jit(solution)/shard_map/reduce_scatter | solution.py:387
  4661.0 132.7 %reduce-scatter.19.cloned.1.call-done = f32[1,768,48]{1,2,0:T(8,128)} async-done(((f32[1,768,768]{1,2,0:T(8,128)}), f32[1,768,48]{1,2,0:T(8,128)}) %reduce-scatter.19.cloned.1.call-update) | async-done | bytes 147472 | tf_op jit(solution)/shard_map/reduce_scatter | solution.py:388
  4793.8 177.2 %reduce-scatter.21.cloned.1.call-done = f32[1,48,3072]{2,1,0:T(8,128)} async-done(((f32[1,768,3072]{2,1,0:T(8,128)}), f32[1,48,3072]{2,1,0:T(8,128)}) %reduce-scatter.21.cloned.1.call-update) | async-done | bytes 589840 | tf_op jit(solution)/shard_map/reduce_scatter | solution.py:389
  4971.0 177.4 %reduce-scatter.23.cloned.1.call-done = f32[1,3072,48]{1,2,0:T(8,128)} async-done(((f32[1,3072,768]{1,2,0:T(8,128)}), f32[1,3072,48]{1,2,0:T(8,128)}) %reduce-scatter.23.cloned.1.call-update) | async-done | bytes 589840 | tf_op jit(solution)/shard_map/reduce_scatter | solution.py:390
  (696 shorter events, 2146.8 us)
Async XLA Ops:
  7.3 61.1 %all-gather.9.cloned.1.call-start = ((), (), s32[]{:S(2)}) async-start(), calls=%async_computation.9 | async-start | bytes 1253376 | tf_op jit(solution)/shard_map/all_gather | solution.py:294
  9.0 117.7 %all-gather.11.cloned.1.call-start = ((), (), s32[]{:S(2)}) async-start(), calls=%async_computation.10 | async-start | bytes 1253376 | tf_op jit(solution)/shard_map/all_gather | solution.py:295
  10.7 174.5 %all-gather.7.cloned.1.call-start = ((), (), s32[]{:S(2)}) async-start(), calls=%async_computation.8 | async-start | bytes 1253376 | tf_op jit(solution)/shard_map/all_gather | solution.py:296
  12.3 231.2 %all-gather.13.cloned.1.call-start = ((), (), s32[]{:S(2)}) async-start(), calls=%async_computation.11 | async-start | bytes 1253376 | tf_op jit(solution)/shard_map/all_gather | solution.py:297
  13.9 312.8 %all-gather.15.cloned.1.call-start = ((), (), s32[]{:S(2)}) async-start(), calls=%async_computation.12 | async-start | bytes 5013504 | tf_op jit(solution)/shard_map/all_gather | solution.py:298
  15.8 393.2 %all-gather.17.cloned.1.call-start = ((), (), s32[]{:S(2)}) async-start(), calls=%async_computation.13 | async-start | bytes 5013504 | tf_op jit(solution)/shard_map/all_gather | solution.py:299
  17.7 4120.0 %reduce-scatter.25.cloned.1.call-start = ((), (), s32[]{:S(2)}) async-start(), calls=%async_computation.20 | async-start | bytes 417792
  55.4 353.6 %copy-start.175 = (bf16[768]{0:T(1024)(128)(2,1)}, bf16[768]{0:T(1024)(128)(2,1)S(1)}, u32[]{:S(2)}) copy-start(bf16[768]{0:T(1024)(128)(2,1)S(1)} %get-tuple-element.2816) | copy-start | bytes 4612
  55.4 353.6 %copy-start.180 = (bf16[768]{0:T(1024)(128)(2,1)}, bf16[768]{0:T(1024)(128)(2,1)S(1)}, u32[]{:S(2)}) copy-start(bf16[768]{0:T(1024)(128)(2,1)S(1)} %get-tuple-element.2793) | copy-start | bytes 4612
  453.1 329.4 %copy-start.159 = (s32[2,1024]{1,0:T(2,128)S(1)}, s32[2,1024]{1,0:T(2,128)}, u32[]{:S(2)}) copy-start(s32[2,1024]{1,0:T(2,128)} %param.62) | copy-start | bytes 24580
  453.2 329.4 %copy-start.176 = (bf16[768]{0:T(1024)(128)(2,1)S(1)}, bf16[768]{0:T(1024)(128)(2,1)}, u32[]{:S(2)}) copy-start(bf16[768]{0:T(1024)(128)(2,1)} %copy-done.175) | copy-start | bytes 4612
  453.2 329.4 %copy-start.181 = (bf16[768]{0:T(1024)(128)(2,1)S(1)}, bf16[768]{0:T(1024)(128)(2,1)}, u32[]{:S(2)}) copy-start(bf16[768]{0:T(1024)(128)(2,1)} %copy-done.180) | copy-start | bytes 4612
  458.4 323.0 %collective-permute-start = (bf16[1,1024,768]{2,1,0:T(8,128)(2,1)}, bf16[1,1024,768]{2,1,0:T(8,128)(2,1)}, u32[]{:S(2)}, u32[]{:S(2)}) collective-permute-start(bf16[1,1024,768]{2,1,0:T(8,128)(2,1)} %bitcast.1453), channel_id=1, source_target_pairs={{0,16},{1,17},{2,18},{3,19},{4,20},{5,21},{6,22},{7,23},{8,24},{9,... | collective-permute-start | bytes 4718600 | tf_op jit(solution)/shard_map/ppermute | solution.py:17
  1110.9 5.6 collective-permute-start.1
  2141.1 97.7 %slice-start.33 = ((s8[16777216]{0:T(1024)(128)(4,1)}), s8[4194304]{0:T(1024)(128)(4,1)S(1)}, s32[]{:S(2)}) async-start(s8[16777216]{0:T(1024)(128)(4,1)} %bitcast.1359), calls=%async_computation.55 | async-start | bytes 8388608 | tf_op jit(solution)/shard_map/cond
  2297.3 4.6 collective-permute-start.2
  3156.9 5.6 collective-permute-start.3
  3167.5 1096.3 %reduce-scatter.27.cloned.1.call-start = ((), (), s32[]{:S(2)}) async-start(), calls=%async_computation.21 | async-start | bytes 417792
  3169.2 1226.8 %reduce-scatter.13.cloned.1.call-start = ((), (), s32[]{:S(2)}) async-start(), calls=%async_computation.14 | async-start | bytes 2506752 | tf_op jit(solution)/shard_map/reduce_scatter | solution.py:385
  3169.9 1358.8 %reduce-scatter.15.cloned.1.call-start = ((), (), s32[]{:S(2)}) async-start(), calls=%async_computation.15 | async-start | bytes 2506752 | tf_op jit(solution)/shard_map/reduce_scatter | solution.py:386
  3170.5 1490.5 %reduce-scatter.17.cloned.1.call-start = ((), (), s32[]{:S(2)}) async-start(), calls=%async_computation.16 | async-start | bytes 2506752 | tf_op jit(solution)/shard_map/reduce_scatter | solution.py:387
  3171.3 1622.5 %reduce-scatter.19.cloned.1.call-start = ((), (), s32[]{:S(2)}) async-start(), calls=%async_computation.17 | async-start | bytes 2506752 | tf_op jit(solution)/shard_map/reduce_scatter | solution.py:388
  3174.4 1796.6 %reduce-scatter.21.cloned.1.call-start = ((), (), s32[]{:S(2)}) async-start(), calls=%async_computation.18 | async-start | bytes 10027008 | tf_op jit(solution)/shard_map/reduce_scatter | solution.py:389
  3175.1 1973.3 %reduce-scatter.23.cloned.1.call-start = ((), (), s32[]{:S(2)}) async-start(), calls=%async_computation.19 | async-start | bytes 10027008 | tf_op jit(solution)/shard_map/reduce_scatter | solution.py:390
  (192 other events, 3308.6 us)
Sparse Core Ops, SparseCore 0:
  11.5 56.8 all-gather.8
  71.7 54.9 all-gather.10
  130.1 54.9 all-gather.6
  188.4 54.9 all-gather.12
  246.7 79.9 all-gather.14
  329.9 79.0 all-gather.16
  3167.6 970.0 reduce-scatter.24
  4143.1 120.6 reduce-scatter.26
  4269.3 126.6 reduce-scatter.12
  4402.1 126.5 reduce-scatter.14
  4534.2 126.7 reduce-scatter.16
  4667.1 126.5 reduce-scatter.18
  4800.0 170.9 reduce-scatter.20
  4978.1 170.2 reduce-scatter.22
where the time goes:
time: 5160 us
  waiting for transfers between devices  2580 us (50%)
  matrix products  2000 us (39%)
  other arithmetic  250 us (5%)
  local copies, waits for them, and re-layouts  195 us (4%)
  blocking collectives  96 us (2%)
    unnamed x16, waiting for transfers between devices  1020 us
    dot_general x8, matrix products, block_scores(): premixed = jnp.einsum('hqk,hg->gqk', scores, mix_logits, precision=HIGH)  457 us
    ppermute x4, waiting for transfers between devices, shifted(): return lax.ppermute(x, axis, pairs)  327 us
    dot_general x4, matrix products, attend_row_back(): jnp.einsum('hqk,gh->gqk', grad_remixed, mix_weights, precision=HIGH)  253 us
    dot_general x4, matrix products, attend_row_back(): jnp.einsum('hqk,gqk->hg', scores, grad_premixed, precision=HIGH)  193 us
    reduce_scatter x1, waiting for transfers between devices, on_device(): lax.psum_scatter(carried[7][None], 'dp', scatter_dimension=2, tiled=True)  177 us
    reduce_scatter x1, waiting for transfers between devices, on_device(): lax.psum_scatter(carried[6][None], 'dp', scatter_dimension=1, tiled=True)  177 us
    dot_general x4, matrix products, attend_row_back(): jnp.einsum('gqk,hqk->gh', softened, grad_remixed, precision=HIGH)  172 us
  transfers between devices with their start and end apart: 18, of which 18 were waited for; matrix products, arithmetic and copies ran while one was open for 1% of the time, Pallas kernels for 0%

commit v1 on v0

v1 whole, which is shorter than its diff:
```python
import functools
import math

import jax
import jax.numpy as jnp
from jax import lax
from jax.experimental import pallas as pl
from jax.experimental.pallas import tpu as pltpu
from jax.sharding import PartitionSpec as P

EPS = 1e-06
NEGATIVE = -1e30
LOG2E = math.log2(math.e)
BF = jnp.bfloat16
F32 = jnp.float32
QB = 128
REACH = 512
ROWB = 256
VMEM = 60 * 1024 * 1024

SMEM_SPEC = pl.BlockSpec(memory_space=pltpu.SMEM)


def dot(left, right):
    return jnp.dot(left, right, preferred_element_type=F32)


def dot_t(left, right):
    return lax.dot_general(left, right, (((1,), (1,)), ((), ())), preferred_element_type=F32)


def whole(shape):
    return pl.BlockSpec(shape, lambda *_: (0,) * len(shape))


def column(shape, place):
    return pl.BlockSpec(shape, lambda *_: (0, place))


def params():
    return pltpu.CompilerParams(vmem_limit_bytes=VMEM)


def project_kernel(x_ref, gain_ref, wq_ref, wk_ref, wv_ref, normed_ref, q_ref, qt_ref, k_ref, kt_ref, v_ref, vt_ref):
    x = x_ref[...].astype(F32)
    scale = lax.rsqrt(jnp.mean(x * x, axis=-1, keepdims=True) + EPS)
    normed = (x * scale * gain_ref[...]).astype(BF)
    normed_ref[...] = normed
    for w_ref, y_ref, yt_ref in ((wq_ref, q_ref, qt_ref), (wk_ref, k_ref, kt_ref), (wv_ref, v_ref, vt_ref)):
        y = dot(normed, w_ref[...])
        y_ref[...] = y.astype(BF)
        yt_ref[...] = y.T.astype(BF)


def project(x, gain, w, places):
    length, width = x.shape
    rows = pl.BlockSpec((ROWB, width), lambda i: (i, 0))
    cols = pl.BlockSpec((width, ROWB), lambda i: (0, i))
    flat = jax.ShapeDtypeStruct((length, width), BF)
    turned = jax.ShapeDtypeStruct((width, length), BF)
    return pl.pallas_call(
        project_kernel,
        grid=(length // ROWB,),
        in_specs=[rows, whole((1, width))] + [column((width, width), p) for p in places],
        out_specs=[rows, rows, cols, rows, cols, rows, cols],
        out_shape=[flat, flat, turned, flat, turned, flat, turned],
        compiler_params=params(),
        cost_estimate=pl.CostEstimate(flops=6 * length * width * width, bytes_accessed=16 * length * width, transcendentals=0),
        name="project",
    )(x, gain, w, w, w)


def attend_kernel(
    heads, start_ref, mw_ref, ml_ref, qt_ref, k_ref, vt_ref, segc_ref, segr_ref, o_ref, a_ref, mixed_ref, out_acc
):
    block = pl.program_id(0)
    start = start_ref[block]
    size = qt_ref.shape[0] // heads

    def body(blocks):
        span = blocks * QB
        offset = pl.multiple_of(start * QB, QB)
        keys = k_ref[pl.ds(offset, span), :]
        values = vt_ref[:, pl.ds(offset, span)]
        place_k = offset + lax.broadcasted_iota(jnp.int32, (span, QB), 0)
        place_q = block * QB + lax.broadcasted_iota(jnp.int32, (span, QB), 1)
        allowed = (segc_ref[pl.ds(offset, span), :] == segr_ref[...]) & (place_k <= place_q)
        bias = jnp.where(allowed, 0.0, NEGATIVE)
        bias = jnp.concatenate([bias, bias], 1)
        for pair in range(heads // 2):
            parts = []
            for g in (2 * pair, 2 * pair + 1):
                parts.append(
                    jnp.concatenate(
                        [
                            (qt_ref[h * size : (h + 1) * size, :].astype(F32) * ml_ref[h, g]).astype(BF)
                            for h in range(heads)
                        ],
                        0,
                    )
                )
            scores = dot(keys, jnp.concatenate(parts, 1)) + bias
            powers = jnp.exp2(scores - jnp.max(scores, axis=0, keepdims=True))
            soft = (powers * (1.0 / jnp.sum(powers, axis=0, keepdims=True))).astype(BF)
            a_ref[0, pair, 0:span, :] = soft
            mixed = dot(values, soft)
            mixed_ref[2 * pair] = mixed[:, :QB].astype(BF)
            mixed_ref[2 * pair + 1] = mixed[:, QB:].astype(BF)
            for h in range(heads):
                own = slice(h * size, (h + 1) * size)
                term = mixed[own, :QB] * mw_ref[2 * pair, h] + mixed[own, QB:] * mw_ref[2 * pair + 1, h]
                if pair == 0:
                    out_acc[own, :] = term
                else:
                    out_acc[own, :] += term
        o_ref[...] = out_acc[...].T.astype(BF)

    for blocks in range(1, REACH // QB + 2):
        pl.when(block - start + 1 == blocks)(functools.partial(body, blocks))


def attend(start, mw, ml, qt, k, vt, segc, segr):
    width, length = qt.shape
    heads = mw.shape[0]
    steps = length // QB
    most = REACH + QB
    rows = pl.BlockSpec((QB, width), lambda i, s: (i, 0))
    cols = pl.BlockSpec((width, QB), lambda i, s: (0, i))
    return pl.pallas_call(
        functools.partial(attend_kernel, heads),
        grid_spec=pltpu.PrefetchScalarGridSpec(
            num_scalar_prefetch=1,
            grid=(steps,),
            in_specs=[
                SMEM_SPEC,
                SMEM_SPEC,
                cols,
                whole((length, width)),
                whole((width, length)),
                whole((length, 1)),
                pl.BlockSpec((1, QB), lambda i, s: (0, i)),
            ],
            out_specs=[
                rows,
                pl.BlockSpec((1, heads // 2, most, 2 * QB), lambda i, s: (i, 0, 0, 0)),
                pl.BlockSpec((heads, width, QB), lambda i, s: (0, 0, i)),
            ],
            scratch_shapes=[pltpu.VMEM((width, QB), F32)],
        ),
        out_shape=[
            jax.ShapeDtypeStruct((length, width), BF),
            jax.ShapeDtypeStruct((steps, heads // 2, most, 2 * QB), BF),
            jax.ShapeDtypeStruct((heads, width, length), BF),
        ],
        compiler_params=params(),
        cost_estimate=pl.CostEstimate(
            flops=4 * length * most * width * heads, bytes_accessed=40 << 20, transcendentals=length * most * heads
        ),
        name="attend",
    )(start, mw, ml, qt, k, vt, segc, segr)


def attend_back_kernel(
    heads,
    start_ref,
    mw_ref,
    ml_ref,
    mlx_ref,
    mwx_ref,
    q_ref,
    qt_ref,
    do_ref,
    dot_ref,
    kt_ref,
    v_ref,
    a_ref,
    mixed_ref,
    dq_ref,
    dk_ref,
    dv_ref,
    gml_ref,
    gmw_ref,
    dk_acc,
    dv_acc,
    dqt_acc,
    dz_all,
    a_all,
    q_all,
    do_all,
):
    block = pl.program_id(0)
    start = start_ref[block]
    size = qt_ref.shape[0] // heads
    head_rows = [slice(h * size, (h + 1) * size) for h in range(heads)]

    @pl.when(block == 0)
    def _():
        for ref in (dk_acc, dv_acc, gml_ref, gmw_ref):
            ref[...] = jnp.zeros_like(ref)

    def body(blocks):
        span = blocks * QB
        offset = pl.multiple_of(start * QB, QB)
        values = v_ref[pl.ds(offset, span), :]
        keys = kt_ref[:, pl.ds(offset, span)]
        q = q_ref[...].astype(F32)
        do = do_ref[...].astype(F32)
        for pair in range(heads // 2):
            both = (2 * pair, 2 * pair + 1)
            lanes = slice(2 * QB * pair, 2 * QB * (pair + 1))
            parts = []
            for g in both:
                parts.append(
                    jnp.concatenate([(dot_ref[own, :].astype(F32) * mw_ref[g, h]).astype(BF) for h, own in enumerate(head_rows)], 0)
                )
            dsoft = dot(values, jnp.concatenate(parts, 1))
            soft = a_ref[0, pair, 0:span, :]
            wide = soft.astype(F32)
            product = wide * dsoft
            dz = (product - wide * jnp.sum(product, axis=0, keepdims=True)).astype(BF)
            dz_all[0:span, lanes] = dz
            a_all[0:span, lanes] = soft
            for t, g in enumerate(both):
                at = slice((2 * pair + t) * QB, (2 * pair + t + 1) * QB)
                q_all[at, :] = (q * mlx_ref[g : g + 1, :]).astype(BF)
                do_all[at, :] = (do * mwx_ref[g : g + 1, :]).astype(BF)
            side = dot(keys, dz)
            for h, own in enumerate(head_rows):
                terms = (side[own, :QB], side[own, QB:])
                term = terms[0] * ml_ref[h, both[0]] + terms[1] * ml_ref[h, both[1]]
                if pair == 0:
                    dqt_acc[own, :] = term
                else:
                    dqt_acc[own, :] += term
                qth = qt_ref[own, :].astype(F32)
                doth = dot_ref[own, :].astype(F32)
                for g, piece in zip(both, terms):
                    gml_ref[g, h] += jnp.sum((qth * piece).reshape(size // 8, 8, QB), axis=0)
                    gmw_ref[g, h] += jnp.sum((doth * mixed_ref[g, own, :].astype(F32)).reshape(size // 8, 8, QB), axis=0)
        dv_acc[pl.ds(offset, span), :] += dot(a_all[0:span, :], do_all[...])
        dk_acc[pl.ds(offset, span), :] += dot(dz_all[0:span, :], q_all[...])
        dq_ref[...] = dqt_acc[...].T.astype(BF)

    for blocks in range(1, REACH // QB + 2):
        pl.when(block - start + 1 == blocks)(functools.partial(body, blocks))

    @pl.when(block == pl.num_programs(0) - 1)
    def _():
        dk_ref[...] = dk_acc[...].astype(BF)
        dv_ref[...] = dv_acc[...].astype(BF)


def attend_back(start, mw, ml, mlx, mwx, q, qt, do, dot_, kt, v, soft, mixed):
    length, width = q.shape
    heads = mw.shape[0]
    steps = length // QB
    most = REACH + QB
    rows = pl.BlockSpec((QB, width), lambda i, s: (i, 0))
    cols = pl.BlockSpec((width, QB), lambda i, s: (0, i))
    flat = jax.ShapeDtypeStruct((length, width), BF)
    sums = jax.ShapeDtypeStruct((heads, heads, 8, QB), F32)
    return pl.pallas_call(
        functools.partial(attend_back_kernel, heads),
        grid_spec=pltpu.PrefetchScalarGridSpec(
            num_scalar_prefetch=1,
            grid=(steps,),
            in_specs=[
                SMEM_SPEC,
                SMEM_SPEC,
                whole((heads, width)),
                whole((heads, width)),
                rows,
                cols,
                rows,
                cols,
                whole((width, length)),
                whole((length, width)),
                pl.BlockSpec((1, heads // 2, most, 2 * QB), lambda i, s: (i, 0, 0, 0)),
                pl.BlockSpec((heads, width, QB), lambda i, s: (0, 0, i)),
            ],
            out_specs=[rows, whole((length, width)), whole((length, width)), whole(sums.shape), whole(sums.shape)],
            scratch_shapes=[
                pltpu.VMEM((length, width), F32),
                pltpu.VMEM((length, width), F32),
                pltpu.VMEM((width, QB), F32),
                pltpu.VMEM((most, heads * QB), BF),
                pltpu.VMEM((most, heads * QB), BF),
                pltpu.VMEM((heads * QB, width), BF),
                pltpu.VMEM((heads * QB, width), BF),
            ],
        ),
        out_shape=[flat, flat, flat, sums, sums],
        compiler_params=params(),
        cost_estimate=pl.CostEstimate(
            flops=8 * length * most * width * heads, bytes_accessed=50 << 20, transcendentals=0
        ),
        name="attend_back",
    )(start, mw, ml, mlx, mwx, q, qt, do, dot_, kt, v, soft, mixed)


def gelu_both(b):
    root = math.sqrt(2.0 / math.pi)
    square = b * b
    t = jnp.tanh(root * (b + 0.044715 * (square * b)))
    half = 0.5 * (1.0 + t)
    slope = half + 0.5 * b * (1.0 - t * t) * (root * (1.0 + 3.0 * 0.044715 * square))
    return b * half, slope


def feed_kernel(x_ref, o_ref, gain_ref, wo_ref, wi_ref, wb_ref, y_ref, middle_ref, normed_ref, slope_ref, hidden_ref):
    middle = x_ref[...].astype(F32) + dot_t(o_ref[...], wo_ref[...])
    middle_ref[...] = middle
    scale = lax.rsqrt(jnp.mean(middle * middle, axis=-1, keepdims=True) + EPS)
    normed = (middle * scale * gain_ref[...]).astype(BF)
    normed_ref[...] = normed
    wide = wi_ref.shape[1]
    part = wide // 4
    for c in range(4):
        own = slice(c * part, (c + 1) * part)
        hidden, slope = gelu_both(dot(normed, wi_ref[:, own]))
        hidden_ref[:, own] = hidden.astype(BF)
        slope_ref[:, own] = slope.astype(BF)
    y_ref[...] = (middle + dot_t(hidden_ref[...], wb_ref[...])).astype(BF)


def feed(x, o, gain, w, place_out, place_in, place_back):
    length, width = x.shape
    wide = 4 * width
    rows = pl.BlockSpec((ROWB, width), lambda i: (i, 0))
    rows_wide = pl.BlockSpec((ROWB, wide), lambda i: (i, 0))
    flat = jax.ShapeDtypeStruct((length, width), BF)
    flat_wide = jax.ShapeDtypeStruct((length, wide), BF)
    return pl.pallas_call(
        feed_kernel,
        grid=(length // ROWB,),
        in_specs=[
            rows,
            rows,
            whole((1, width)),
            column((width, width), place_out),
            column((width, wide), place_in),
            column((width, wide), place_back),
        ],
        out_specs=[rows, rows, rows, rows_wide, rows_wide],
        out_shape=[flat, jax.ShapeDtypeStruct((length, width), F32), flat, flat_wide, flat_wide],
        compiler_params=params(),
        cost_estimate=pl.CostEstimate(
            flops=18 * length * width * width, bytes_accessed=30 << 20, transcendentals=length * wide
        ),
        name="feed",
    )(x, o, gain, w, w, w)


def norm_back(values, gain, grad):
    scale = lax.rsqrt(jnp.mean(values * values, axis=-1, keepdims=True) + EPS)
    unit = values * scale
    dn = grad * gain
    back = scale * (dn - unit * jnp.mean(dn * unit, axis=-1, keepdims=True))
    return back, jnp.sum(grad * unit, axis=0, keepdims=True)


def feed_back_kernel(
    dy_ref, slope_ref, middle_ref, gain_ref, wo_ref, wi_ref, wb_ref, gf_ref, dmiddle_ref, ga_ref, do_ref, dot_ref, gg_ref
):
    @pl.when(pl.program_id(0) == 0)
    def _():
        gg_ref[...] = jnp.zeros_like(gg_ref)

    dy = dy_ref[...]
    wide = wi_ref.shape[1]
    part = wide // 4
    for c in range(4):
        own = slice(c * part, (c + 1) * part)
        gf_ref[:, own] = (dot(dy, wb_ref[:, own]) * slope_ref[:, own].astype(F32)).astype(BF)
    dnormed = dot_t(gf_ref[...], wi_ref[...])
    back, gg = norm_back(middle_ref[...], gain_ref[...], dnormed)
    gg_ref[...] += gg
    dmiddle = dy.astype(F32) + back
    dmiddle_ref[...] = dmiddle
    ga = dmiddle.astype(BF)
    ga_ref[...] = ga
    do = dot(ga, wo_ref[...])
    do_ref[...] = do.astype(BF)
    dot_ref[...] = do.T.astype(BF)


def feed_back(dy, slope, middle, gain, w, place_out, place_in, place_back):
    length, width = dy.shape
    wide = 4 * width
    rows = pl.BlockSpec((ROWB, width), lambda i: (i, 0))
    rows_wide = pl.BlockSpec((ROWB, wide), lambda i: (i, 0))
    flat = jax.ShapeDtypeStruct((length, width), BF)
    return pl.pallas_call(
        feed_back_kernel,
        grid=(length // ROWB,),
        in_specs=[
            rows,
            rows_wide,
            rows,
            whole((1, width)),
            column((width, width), place_out),
            column((width, wide), place_in),
            column((width, wide), place_back),
        ],
        out_specs=[rows_wide, rows, rows, rows, pl.BlockSpec((width, ROWB), lambda i: (0, i)), whole((1, width))],
        out_shape=[
            jax.ShapeDtypeStruct((length, wide), BF),
            jax.ShapeDtypeStruct((length, width), F32),
            flat,
            flat,
            jax.ShapeDtypeStruct((width, length), BF),
            jax.ShapeDtypeStruct((1, width), F32),
        ],
        compiler_params=params(),
        cost_estimate=pl.CostEstimate(flops=18 * length * width * width, bytes_accessed=40 << 20, transcendentals=0),
        name="feed_back",
    )(dy, slope, middle, gain, w, w, w)


def project_back_kernel(dq_ref, dk_ref, dv_ref, x_ref, dmiddle_ref, gain_ref, wq_ref, wk_ref, wv_ref, dx_ref, gg_ref):
    @pl.when(pl.program_id(0) == 0)
    def _():
        gg_ref[...] = jnp.zeros_like(gg_ref)

    dnormed = dot_t(dq_ref[...], wq_ref[...]) + dot_t(dk_ref[...], wk_ref[...]) + dot_t(dv_ref[...], wv_ref[...])
    back, gg = norm_back(x_ref[...].astype(F32), gain_ref[...], dnormed)
    gg_ref[...] += gg
    dx_ref[...] = (dmiddle_ref[...] + back).astype(BF)


def project_back(dq, dk, dv, x, dmiddle, gain, w, places):
    length, width = x.shape
    rows = pl.BlockSpec((ROWB, width), lambda i: (i, 0))
    return pl.pallas_call(
        project_back_kernel,
        grid=(length // ROWB,),
        in_specs=[rows] * 5 + [whole((1, width))] + [column((width, width), p) for p in places],
        out_specs=[rows, whole((1, width))],
        out_shape=[jax.ShapeDtypeStruct((length, width), BF), jax.ShapeDtypeStruct((1, width), F32)],
        compiler_params=params(),
        cost_estimate=pl.CostEstimate(flops=6 * length * width * width, bytes_accessed=18 << 20, transcendentals=0),
        name="project_back",
    )(dq, dk, dv, x, dmiddle, gain, w, w, w)


def weight_grad(left, right):
    return lax.dot_general(left, right, (((0,), (0,)), ((), ())), preferred_element_type=F32).astype(BF)


def mix_tables(mix_logits, mix_weights, size):
    scaled = mix_logits * (LOG2E * size ** (-0.5))
    wide_logits = jnp.repeat(scaled.T, size, axis=1)
    wide_weights = jnp.repeat(mix_weights, size, axis=1)
    return scaled, mix_logits * size ** (-0.5), wide_logits, wide_weights


def layer_forward(x, seg, weights, tables):
    gains, w_qkv, at_qkv, w_rest, at_rest = weights
    start, segc, segr = seg
    scaled, _, _, mix_weights = tables[:4]
    normed, q, qt, k, kt, v, vt = project(x, gains[0], w_qkv, at_qkv)
    o, soft, mixed = attend(start, tables[4], scaled, qt, k, vt, segc, segr)
    y, middle, normed_two, slope, hidden = feed(x, o, gains[1], w_rest, *at_rest)
    return y, (x, normed, q, qt, kt, v, o, soft, mixed, middle, normed_two, slope, hidden)


def layer_backward(dy, seg, kept, weights, tables):
    gains, w_qkv, at_qkv, w_rest, at_rest = weights
    x, normed, q, qt, kt, v, o, soft, mixed, middle, normed_two, slope, hidden = kept
    start = seg[0]
    _, plain, wide_logits, wide_weights, mix_weights = tables
    gf, dmiddle, ga, do, dot_, gg_ffn = feed_back(dy, slope, middle, gains[1], w_rest, *at_rest)
    grad_back = weight_grad(dy, hidden)
    grad_in = weight_grad(normed_two, gf)
    grad_out = weight_grad(ga, o)
    size = q.shape[1] // mix_weights.shape[0]
    unscaled = wide_logits * (1.0 / LOG2E)
    dq, dk, dv, gml, gmw = attend_back(
        start, mix_weights, plain, unscaled, wide_weights, q, qt, do, dot_, kt, v, soft, mixed
    )
    grads_qkv = [weight_grad(normed, g) for g in (dq, dk, dv)]
    dx, gg_attn = project_back(dq, dk, dv, x, dmiddle, gains[0], w_qkv, at_qkv)
    gml = jnp.sum(gml, axis=(2, 3)).T * size ** (-0.5)
    gmw = jnp.sum(gmw, axis=(2, 3))
    return dx, (grad_in, grad_back, grad_out), grads_qkv, (gg_attn, gg_ffn, gml, gmw)


def windows(seg):
    length = seg.shape[0]
    last = seg[QB - 1 :: QB]
    first = seg[::QB]
    start = jnp.sum((last[None, :] < first[:, None]).astype(jnp.int32), axis=1)
    return start, seg[:, None], seg[None, :]


AXES = ("dp", "section")


def swap(x):
    return lax.ppermute(x, "section", [(0, 1), (1, 0)])


def on_device(
    tokens,
    segments,
    cotangent,
    gain_attn,
    gain_ffn,
    w_query,
    w_key,
    w_value,
    w_out,
    w_in,
    w_back,
    mix_logits,
    mix_weights,
):
    section = lax.axis_index("section")
    first = section == 0
    width = tokens.shape[2]
    heads = mix_logits.shape[1]
    size = width // heads
    share = w_query.shape[1]
    half = share // 2

    x0 = lax.dynamic_index_in_dim(tokens, section, 0, keepdims=False)
    seg = windows(lax.dynamic_index_in_dim(segments, section, 0, keepdims=False))
    cot = lax.dynamic_index_in_dim(cotangent, section, 0, keepdims=False)

    gains = jnp.concatenate([gain_attn, gain_ffn], 0).astype(BF)
    gains = jnp.pad(gains.T, ((0, 0), (0, 126)))
    qkv = jnp.concatenate([w_query[0], w_key[0], w_value[0]], 1).astype(BF)
    early = jnp.concatenate([qkv, gains], 1)
    late = jnp.concatenate([w_in[0].astype(BF), w_back[0].T.astype(BF), w_out[0].T.astype(BF)], 1)

    def halves(own):
        other = swap(jnp.where(first, own[half:], own[:half]))
        return jnp.where(first, own[:half], other), jnp.where(first, other, own[half:])

    early0, early1 = halves(early)
    early_all0 = lax.all_gather(early0, AXES, axis=0, tiled=True)
    late0, late1 = halves(late)
    wide = w_in.shape[2]
    rest = jnp.concatenate(
        [late0[:, : 2 * wide], late1[:, : 2 * wide], late0[:, 2 * wide :], late1[:, 2 * wide :], early1], 1
    )
    rest_all = lax.all_gather(rest, AXES, axis=0, tiled=True)

    own_mix = jnp.concatenate([mix_logits, mix_weights], 0)
    other_mix = swap(own_mix)
    mix0 = jnp.where(first, own_mix, other_mix)
    mix1 = jnp.where(first, other_mix, own_mix)

    def gain_rows(columns):
        rows = columns[:, :2].astype(F32).T
        return rows[0:1], rows[1:2]

    tables = [mix_tables(m[0], m[1], size) + (m[1],) for m in (mix0, mix1)]
    at = 4 * wide // width
    weights0 = (gain_rows(early_all0[:, 3 * width :]), early_all0, (0, 1, 2), rest_all, (at, 0, 1))
    end = 4 * wide + 5 * width
    weights1 = (gain_rows(rest_all[:, end:]), rest_all, (at + 2, at + 3, at + 4), rest_all, (at + 1, 2, 3))

    y0, kept0 = layer_forward(x0, seg, weights0, tables[0])
    y1, kept1 = layer_forward(y0, seg, weights1, tables[1])

    dx1, ffn1, qkv1, small1 = layer_backward(cot, seg, kept1, weights1, tables[1])
    dx0, ffn0, qkv0, small0 = layer_backward(dx1, seg, kept0, weights0, tables[0])

    def scatter(pieces):
        packed = jnp.concatenate(pieces, 1)
        return lax.psum_scatter(packed, AXES, scatter_dimension=0, tiled=True)

    sums1 = scatter(list(ffn1) + qkv1)
    sums0 = jnp.concatenate([scatter(list(ffn0)), scatter(qkv0)], 1)
    other = swap(jnp.where(first, sums1, sums0))
    mine = jnp.where(first, jnp.concatenate([sums0, other], 0), jnp.concatenate([other, sums1], 0)).astype(F32)
    grad_in = mine[:, :wide]
    grad_back = mine[:, wide : 2 * wide].T
    grad_out = mine[:, 2 * wide : 2 * wide + width].T
    grads = [mine[:, 2 * wide + i * width : 2 * wide + (i + 1) * width] for i in (1, 2, 3)]

    small = jnp.stack([jnp.concatenate([s.reshape(-1) for s in parts]) for parts in (small0, small1)])
    small = lax.psum(small, AXES)
    small = jnp.where(first, small[0], small[1])
    place = lax.axis_index("dp") * share
    gg_attn = lax.dynamic_slice_in_dim(small, place, share)[None]
    gg_ffn = lax.dynamic_slice_in_dim(small, width + place, share)[None]
    gml = small[2 * width : 2 * width + heads * heads].reshape(1, heads, heads)
    gmw = small[2 * width + heads * heads :].reshape(1, heads, heads)

    def outputs(own0, own1):
        other = swap(jnp.where(first, own1, own0))
        return jnp.where(first, jnp.stack([own0, other]), jnp.stack([other, own1]))[None]

    return (
        outputs(y0, y1),
        outputs(dx0, dx1),
        gg_attn,
        gg_ffn,
        grads[0][None],
        grads[1][None],
        grads[2][None],
        grad_out[None],
        grad_in[None],
        grad_back[None],
        gml,
        gmw,
    )


def solution(mesh):
    rows = P("dp", None, None)
    by_row = P("section", "dp", None)
    by_column = P("section", None, "dp")
    shared = P("section", None, None)
    gain = P("section", "dp")
    return jax.shard_map(
        on_device,
        mesh=mesh,
        in_specs=(
            rows,
            P("dp", None),
            rows,
            gain,
            gain,
            by_row,
            by_row,
            by_row,
            by_column,
            by_row,
            by_column,
            shared,
            shared,
        ),
        out_specs=(
            P("section", "dp", None, None),
            P("section", "dp", None, None),
            gain,
            gain,
            by_row,
            by_row,
            by_row,
            by_column,
            by_row,
            by_column,
            shared,
            shared,
        ),
        check_vma=False,
    )
```

time: 5160 us -> 903 us (0.17)
  waiting for transfers between devices: 2580 us -> 432 us
  matrix products: 2000 us -> 56.9 us
  Pallas kernels: 0 us -> 280 us
  other arithmetic: 250 us -> 38.1 us
  local copies, waits for them, and re-layouts: 195 us -> 25.6 us
    dot_general x96 -> x12, matrix products: 2000 us -> 56.9 us  [weight_grad(): lax.dot_general(left, right, (((0,), (0,)), ((), ())), preferred_element_...]
    unnamed x16 -> x5, waiting for transfers between devices: 1020 us -> 0.76 us
    reduce_scatter x6 -> x3, waiting for transfers between devices: 883 us -> 262 us  [scatter(): return lax.psum_scatter(packed, AXES, scatter_dimension=0, tiled=True)]
    ppermute x4 -> x6, waiting for transfers between devices: 327 us -> 0.02 us  [swap(): return lax.ppermute(x, 'section', [(0, 1), (1, 0)])]
    pallas_call x0 -> x12, Pallas kernels: none -> 280 us  [the longest x2 89.8 us: attend_back(): pl.pallas_call(functools.partial(attend_back_kernel, heads), grid_spec=pl...]
    all_gather x6 -> x2, waiting for transfers between devices: 351 us -> 169 us  [the longest x1 116 us: on_device(): rest_all = lax.all_gather(rest, AXES, axis=0, tiled=True)]
    dot_general x4 -> x0, other arithmetic: 125 us -> none  [the longest x2 70.7 us: attend_row_back(): jnp.einsum('hqk,gqk->hg', scores, grad_premixed, precision=HIGH)]
    another operation x24 -> x2, local copies, waits for them, and re-layouts: 73.3 us -> 0.02 us  [on_device(): jnp.stack([jnp.concatenate([s.reshape(-1) for s in parts]) for parts in (...]
  transfers between devices with their start and end apart: 18 -> 11, of which waited for: 18 -> 4; matrix products, arithmetic and copies ran while one was open for 1% -> 8% of each run, Pallas kernels for 0% -> 10%
where the time goes in v1:
time: 903 us; the launch traced here: 899 us
  waiting for transfers between devices  432 us (48%)
  Pallas kernels  280 us (31%)
  matrix products  56.9 us (6%)
  blocking collectives  47.3 us (5%)
  other arithmetic  38.1 us (4%)
  local copies, waits for them, and re-layouts  25.6 us (3%)
  between operations  14.7 us (2%)
    reduce_scatter x3, waiting for transfers between devices, scatter(): return lax.psum_scatter(packed, AXES, scatter_dimension=0, tiled=True)  262 us
    all_gather x1, waiting for transfers between devices, on_device(): rest_all = lax.all_gather(rest, AXES, axis=0, tiled=True)  116 us
    pallas_call x2, Pallas kernels, attend_back(): pl.pallas_call(functools.partial(attend_back_kernel, heads), grid_spec=pl...  89.8 us
    dot_general x12, matrix products, weight_grad(): lax.dot_general(left, right, (((0,), (0,)), ((), ())), preferred_element_...  56.9 us
    pallas_call x2, Pallas kernels, attend(): pl.pallas_call(functools.partial(attend_kernel, heads), grid_spec=pltpu.P...  56.9 us
    all_gather x1, waiting for transfers between devices, on_device(): early_all0 = lax.all_gather(early0, AXES, axis=0, tiled=True)  53.1 us
    pallas_call x2, Pallas kernels, feed(): pl.pallas_call(feed_kernel, grid=(length // ROWB,), in_specs=[rows, rows,...  52.2 us
    psum x1, blocking collectives, on_device(): small = lax.psum(small, AXES)  47.3 us
  transfers between devices with their start and end apart: 11, of which 4 were waited for; matrix products, arithmetic and copies ran while one was open for 8% of the time, Pallas kernels for 10%

profile of v1, /device:TPU:1, one launch (start us, length us, event | category | flops | bytes accessed | tf_op | source)
XLA Modules:
  0.0 898.6 jit_solution(12131512867599409571)
XLA Ops:
  29.2 53.1 %all-gather.3.cloned.1.call-done.wq_ref.wk_ref.wv_ref = bf16[768,2432]{1,0:T(8,128)(2,1)} async-done(((bf16[24,2432]{1,0:T(8,128)(2,1)}), bf16[768,2432]{1,0:T(8,128)(2,1)}) %all-gather.3.cloned.1.call-update) | async-done | bytes 3735568 | tf_op jit(solution)/shard_map/all_gather | solution.py:541
  84.8 8.4 project.2
  93.2 28.6 %attend.2 = (bf16[1024,768]{1,0:T(8,128)(2,1)}, bf16[8,6,640,256]{3,2,1,0:T(8,128)(2,1)}, bf16[12,768,1024]{2,1,0:T(8,128)(2,1)}) custom-call(s32[8]{0:T(128)} %convert_reduce_fusion.start_ref, f32[12,12]{1,0:T(8,128)} %get-tuple-element.144.mw_ref, f32[12,12]{1,0:T(8,128)} %get-tuple-element.143.ml_ref, bf16[768,1024]{1,0:T(8,128)(2,1)} %get-tuple-element.68.qt_ref, ...), custom_call_target="tpu_custom_call" | custom-call | flops 24159191040 | bytes 41943040 | tf_op jit(solution)/shard_map/attend/pallas_call | solution.py:129
  121.8 116.0 %all-gather.5.cloned.1.call-done.wo_ref.wi_ref.wb_ref.wq_ref.wk_ref.wv_ref = bf16[768,16256]{1,0:T(8,128)(2,1)} async-done(((bf16[24,16256]{1,0:T(8,128)(2,1)}), bf16[768,16256]{1,0:T(8,128)(2,1)}) %all-gather.5.cloned.1.call-update) | async-done | bytes 24969232 | tf_op jit(solution)/shard_map/all_gather | solution.py:547
  240.3 26.1 %feed.2 = (bf16[1024,768]{1,0:T(8,128)(2,1)}, f32[1024,768]{1,0:T(8,128)}, bf16[1024,768]{1,0:T(8,128)(2,1)}, bf16[1024,3072]{1,0:T(8,128)(2,1)}, bf16[1024,3072]{1,0:T(8,128)(2,1)}) custom-call(bf16[1024,768]{1,0:T(8,128)(2,1)} %dynamic-slice_bitcast_fusion.1.x_ref, bf16[1024,768]{1,0:T(8,128)(2,1)} %get-tuple-element.71.o_ref, f32[1,768]{1,0:T(1,128)} %copy.101.gain_ref, ...), custom_call_target="tpu_custom_call" | custom-call | flops 10871635968 | bytes 31457280 | tf_op jit(solution)/shard_map/feed/pallas_call | solution.py:333
  266.4 8.4 project.3
  274.8 28.3 %attend.3 = (bf16[1024,768]{1,0:T(8,128)(2,1)}, bf16[8,6,640,256]{3,2,1,0:T(8,128)(2,1)}, bf16[12,768,1024]{2,1,0:T(8,128)(2,1)}) custom-call(s32[8]{0:T(128)} %convert_reduce_fusion.start_ref, f32[12,12]{1,0:T(8,128)} %copy-done.28, f32[12,12]{1,0:T(8,128)} %get-tuple-element.146.ml_ref, bf16[768,1024]{1,0:T(8,128)(2,1)} %get-tuple-element.73.qt_ref, ...), custom_call_target="tpu_custom_call" | custom-call | flops 24159191040 | bytes 41943040 | tf_op jit(solution)/shard_map/attend/pallas_call | solution.py:129
  303.1 26.1 %feed.3 = (bf16[1024,768]{1,0:T(8,128)(2,1)}, f32[1024,768]{1,0:T(8,128)}, bf16[1024,768]{1,0:T(8,128)(2,1)}, bf16[1024,3072]{1,0:T(8,128)(2,1)}, bf16[1024,3072]{1,0:T(8,128)(2,1)}) custom-call(bf16[1024,768]{1,0:T(8,128)(2,1)} %get-tuple-element.72.x_ref, bf16[1024,768]{1,0:T(8,128)(2,1)} %get-tuple-element.76.o_ref, f32[1,768]{1,0:T(1,128)} %copy.104.gain_ref, ...), custom_call_target="tpu_custom_call" | custom-call | flops 10871635968 | bytes 31457280 | tf_op jit(solution)/shard_map/feed/pallas_call | solution.py:333
  329.3 22.3 %feed_back.2 = (bf16[1024,3072]{1,0:T(8,128)(2,1)}, f32[1024,768]{1,0:T(8,128)}, bf16[1024,768]{1,0:T(8,128)(2,1)}, bf16[1024,768]{1,0:T(8,128)(2,1)}, bf16[768,1024]{1,0:T(8,128)(2,1)}, /*index=5*/f32[1,768]{1,0:T(1,128)}) custom-call(bf16[1024,768]{1,0:T(8,128)(2,1)} %dynamic-slice_bitcast_fusion.dy_ref, bf16[1024,3072]{1,0:T(8,128)(2,1)} %get-tuple-element.80.slope_ref, ...), custom_call_target="tpu_custom_call" | custom-call | flops 10871635968 | bytes 41943040 | tf_op jit(solution)/shard_map/feed_back/pallas_call | solution.py:393
  351.6 44.8 %attend_back.2 = (bf16[1024,768]{1,0:T(8,128)(2,1)}, bf16[1024,768]{1,0:T(8,128)(2,1)}, bf16[1024,768]{1,0:T(8,128)(2,1)}, f32[12,12,8,128]{3,2,1,0:T(8,128)}, f32[12,12,8,128]{3,2,1,0:T(8,128)}) custom-call(s32[8]{0:T(128)} %convert_reduce_fusion.start_ref, f32[12,12]{1,0:T(8,128)} %copy-done.28, f32[12,12]{1,0:T(8,128)} %get-tuple-element.145.ml_ref, ...), custom_call_target="tpu_custom_call" | custom-call | flops 48318382080 | bytes 52428800 | tf_op jit(solution)/shard_map/attend_back/pallas_call | solution.py:262
  396.4 9.6 %project_back.2 = (bf16[1024,768]{1,0:T(8,128)(2,1)}, f32[1,768]{1,0:T(1,128)}) custom-call(bf16[1024,768]{1,0:T(8,128)(2,1)} %get-tuple-element.88.dq_ref, bf16[1024,768]{1,0:T(8,128)(2,1)} %get-tuple-element.89.dk_ref, bf16[1024,768]{1,0:T(8,128)(2,1)} %get-tuple-element.90.dv_ref, bf16[1024,768]{1,0:T(8,128)(2,1)} %get-tuple-element.72.x_ref, ...), custom_call_target="tpu_custom_call" | custom-call | flops 3623878656 | bytes 18874368 | tf_op jit(solution)/shard_map/project_back/pallas_call | solution.py:434
  406.0 9.2 %convolution_convert_fusion.2 = bf16[768,3072]{1,0:T(8,128)(2,1)} fusion(bf16[1024,768]{1,0:T(8,128)(2,1)} %get-tuple-element.92.dy_ref, bf16[1024,3072]{1,0:T(8,128)(2,1)} %get-tuple-element.116), kind=kOutput, calls=%fused_computation.5 | convolution fusion | flops 4834197504 | bytes 12582912 | tf_op jit(solution)/shard_map/dot_general | solution.py:447
  415.1 22.5 %feed_back.3 = (bf16[1024,3072]{1,0:T(8,128)(2,1)}, f32[1024,768]{1,0:T(8,128)}, bf16[1024,768]{1,0:T(8,128)(2,1)}, bf16[1024,768]{1,0:T(8,128)(2,1)}, bf16[768,1024]{1,0:T(8,128)(2,1)}, /*index=5*/f32[1,768]{1,0:T(1,128)}) custom-call(bf16[1024,768]{1,0:T(8,128)(2,1)} %get-tuple-element.92.dy_ref, bf16[1024,3072]{1,0:T(8,128)(2,1)} %get-tuple-element.93.slope_ref, ...), custom_call_target="tpu_custom_call" | custom-call | flops 10871635968 | bytes 41943040 | tf_op jit(solution)/shard_map/feed_back/pallas_call | solution.py:393
  440.6 8.2 convolution_convert_fusion.3
  448.9 8.0 pad_maximum_fusion
  459.2 45.0 %attend_back.3 = (bf16[1024,768]{1,0:T(8,128)(2,1)}, bf16[1024,768]{1,0:T(8,128)(2,1)}, bf16[1024,768]{1,0:T(8,128)(2,1)}, f32[12,12,8,128]{3,2,1,0:T(8,128)}, f32[12,12,8,128]{3,2,1,0:T(8,128)}) custom-call(s32[8]{0:T(128)} %convert_reduce_fusion.start_ref, f32[12,12]{1,0:T(8,128)} %get-tuple-element.144.mw_ref, f32[12,12]{1,0:T(8,128)} %get-tuple-element.142.ml_ref, ...), custom_call_target="tpu_custom_call" | custom-call | flops 48318382080 | bytes 52428800 | tf_op jit(solution)/shard_map/attend_back/pallas_call | solution.py:262
  513.5 10.7 %fusion.1 = bf16[768,9216]{1,0:T(8,128)(2,1)} fusion(bf16[1024,768]{1,0:T(8,128)(2,1)S(1)} %copy-done.37, bf16[1024,3072]{1,0:T(8,128)(2,1)} %get-tuple-element.120), kind=kOutput, calls=%fused_computation.4 | convolution fusion | flops 4834197504 | bytes 12582912 | tf_op jit(solution)/shard_map/dot_general | solution.py:447
  524.2 9.8 %fusion = bf16[768,9216]{1,0:T(8,128)(2,1)} fusion(bf16[768,9216]{1,0:T(8,128)(2,1)} %fusion.1, bf16[1024,768]{1,0:T(8,128)(2,1)S(1)} %copy-done.6, bf16[1024,3072]{1,0:T(8,128)(2,1)} %get-tuple-element.121), kind=kOutput, calls=%fused_computation.2 | convolution fusion | flops 4834197504 | bytes 12582912 | tf_op jit(solution)/shard_map/dot_general | solution.py:447
  546.2 10.1 %project_back.3 = (bf16[1024,768]{1,0:T(8,128)(2,1)}, f32[1,768]{1,0:T(1,128)}) custom-call(bf16[1024,768]{1,0:T(8,128)(2,1)} %get-tuple-element.101.dq_ref, bf16[1024,768]{1,0:T(8,128)(2,1)} %get-tuple-element.102.dk_ref, bf16[1024,768]{1,0:T(8,128)(2,1)} %get-tuple-element.103.dv_ref, bf16[1024,768]{1,0:T(8,128)(2,1)} %dynamic-slice_bitcast_fusion.1.x_ref, ...), custom_call_target="tpu_custom_call" | custom-call | flops 3623878656 | bytes 18874368 | tf_op jit(solution)/shard_map/project_back/pallas_call | solution.py:434
  558.1 47.3 %psum.7 = f32[2,1824]{1,0:T(2,128)S(1)} all-reduce(f32[2,1824]{1,0:T(2,128)S(1)} %pad_maximum_fusion.3), channel_id=1, replica_groups=mesh['section'=2,'dp'=16] {'dp','section'}, use_global_device_ids=true, to_apply=%region_5.6 | all-reduce | flops 3648 | bytes 29184 | tf_op jit(solution)/shard_map/psum | solution.py:584
  614.5 95.6 %reduce-scatter.6.cloned.1.call-done = bf16[24,2304]{1,0:T(8,128)(2,1)} async-done(((bf16[768,2304]{1,0:T(8,128)(2,1)}), bf16[24,2304]{1,0:T(8,128)(2,1)}) %reduce-scatter.6.cloned.1.call-update) | async-done | bytes 110608 | tf_op jit(solution)/shard_map/reduce_scatter | solution.py:572
  711.7 166.5 %reduce-scatter.8.cloned.1.call-done = bf16[24,9216]{1,0:T(8,128)(2,1)} async-done(((bf16[768,9216]{1,0:T(8,128)(2,1)}), bf16[24,9216]{1,0:T(8,128)(2,1)}) %reduce-scatter.8.cloned.1.call-update) | async-done | bytes 442384 | tf_op jit(solution)/shard_map/reduce_scatter | solution.py:572
  881.2 4.3 maximum_select_fusion.1
  885.6 3.7 maximum_select_fusion
  (208 shorter events, 71.6 us)
Async XLA Ops:
  7.2 13.8 %copy-start = (bf16[2,1024,768]{2,1,0:T(8,128)(2,1)S(1)}, bf16[2,1024,768]{2,1,0:T(8,128)(2,1)}, u32[]{:S(2)}) copy-start(bf16[2,1024,768]{2,1,0:T(8,128)(2,1)} %param.13) | copy-start | bytes 9437188
  7.2 75.0 %all-gather.3.cloned.1.call-start = ((), (), s32[]{:S(2)}) async-start(), calls=%async_computation.3 | async-start | bytes 3852288 | tf_op jit(solution)/shard_map/all_gather | solution.py:541
  12.3 3.9 collective-permute-start.2
  15.7 1.7 collective-permute-start.1
  19.0 218.8 %all-gather.5.cloned.1.call-start = ((), (), s32[]{:S(2)}) async-start(), calls=%async_computation.4 | async-start | bytes 25749504 | tf_op jit(solution)/shard_map/all_gather | solution.py:547
  19.7 593.1 %reduce-scatter.4.cloned.1.call-start = ((), (), s32[]{:S(2)}) async-start(), calls=%async_computation.5 | async-start | bytes 10948608 | tf_op jit(solution)/shard_map/reduce_scatter | solution.py:572
  19.8 5.9 collective-permute-start
  27.8 57.1 %copy-start.28 = (f32[12,12]{1,0:T(8,128)}, f32[12,12]{1,0:T(8,128)S(1)}, u32[]{:S(2)}) copy-start(f32[12,12]{1,0:T(8,128)S(1)} %get-tuple-element.147.mw_ref) | copy-start | bytes 1732
  415.1 22.5 %copy-start.17 = (bf16[1024,768]{1,0:T(8,128)(2,1)S(1)}, bf16[1024,768]{1,0:T(8,128)(2,1)}, u32[]{:S(2)}) copy-start(bf16[1024,768]{1,0:T(8,128)(2,1)} %get-tuple-element.71.o_ref) | copy-start | bytes 4718596
  437.6 11.2 %slice-start = ((s8[4718592]{0:T(1024)(128)(4,1)}), s8[4194304]{0:T(1024)(128)(4,1)S(1)}, s32[]{:S(2)}) async-start(s8[4718592]{0:T(1024)(128)(4,1)} %bitcast.102), calls=%async_computation.8 | async-start | bytes 8388608
  456.9 253.3 %reduce-scatter.6.cloned.1.call-start = ((), (), s32[]{:S(2)}) async-start(), calls=%async_computation.6 | async-start | bytes 3649536 | tf_op jit(solution)/shard_map/reduce_scatter | solution.py:572
  459.2 45.0 %copy-start.41 = (bf16[1024,768]{1,0:T(8,128)(2,1)S(1)}, bf16[1024,768]{1,0:T(8,128)(2,1)}, u32[]{:S(2)}) copy-start(bf16[1024,768]{1,0:T(8,128)(2,1)} %get-tuple-element.118) | copy-start | bytes 4718596
  512.2 366.0 %reduce-scatter.8.cloned.1.call-start = ((), (), s32[]{:S(2)}) async-start(), calls=%async_computation.7 | async-start | bytes 14598144 | tf_op jit(solution)/shard_map/reduce_scatter | solution.py:572
  513.5 10.7 %copy-start.6 = (bf16[1024,768]{1,0:T(8,128)(2,1)S(1)}, bf16[1024,768]{1,0:T(8,128)(2,1)}, u32[]{:S(2)}) copy-start(bf16[1024,768]{1,0:T(8,128)(2,1)} %dynamic-slice_bitcast_fusion.dy_ref) | copy-start | bytes 4718596
  524.2 9.8 %copy-start.38 = (bf16[1024,768]{1,0:T(8,128)(2,1)S(1)}, bf16[1024,768]{1,0:T(8,128)(2,1)}, u32[]{:S(2)}) copy-start(bf16[1024,768]{1,0:T(8,128)(2,1)} %get-tuple-element.122) | copy-start | bytes 4718596
  546.1 10.8 %copy-start.35 = (f32[1,768]{1,0:T(1,128)S(1)}, f32[1,768]{1,0:T(1,128)}, u32[]{:S(2)}) copy-start(f32[1,768]{1,0:T(1,128)} %get-tuple-element.107) | copy-start | bytes 9220
  546.1 10.9 %copy-start.34 = (f32[1,768]{1,0:T(1,128)S(1)}, f32[1,768]{1,0:T(1,128)}, u32[]{:S(2)}) copy-start(f32[1,768]{1,0:T(1,128)} %get-tuple-element.110) | copy-start | bytes 9220
  546.2 11.0 %copy-start.21 = (f32[12,12,8,128]{3,2,1,0:T(8,128)S(1)}, f32[12,12,8,128]{3,2,1,0:T(8,128)}, u32[]{:S(2)}) copy-start(f32[12,12,8,128]{3,2,1,0:T(8,128)} %get-tuple-element.112) | copy-start | bytes 1769476
  546.2 11.4 %copy-start.20 = (f32[12,12,8,128]{3,2,1,0:T(8,128)S(1)}, f32[12,12,8,128]{3,2,1,0:T(8,128)}, u32[]{:S(2)}) copy-start(f32[12,12,8,128]{3,2,1,0:T(8,128)} %get-tuple-element.113) | copy-start | bytes 1769476
  546.2 11.8 %copy-start.33 = (f32[1,768]{1,0:T(1,128)S(1)}, f32[1,768]{1,0:T(1,128)}, u32[]{:S(2)}) copy-start(f32[1,768]{1,0:T(1,128)} %get-tuple-element.111) | copy-start | bytes 9220
  546.2 60.7 %copy-start.3 = (bf16[1024,768]{1,0:T(8,128)(2,1)S(1)}, bf16[1024,768]{1,0:T(8,128)(2,1)}, u32[]{:S(2)}) copy-start(bf16[1024,768]{1,0:T(8,128)(2,1)} %get-tuple-element.92.dy_ref) | copy-start | bytes 4718596
  609.8 271.4 %collective-permute-start.4 = (bf16[1024,768]{1,0:T(8,128)(2,1)}, bf16[1024,768]{1,0:T(8,128)(2,1)}, u32[]{:S(2)}, u32[]{:S(2)}) collective-permute-start(bf16[1024,768]{1,0:T(8,128)(2,1)} %broadcast_select_fusion), channel_id=1, source_target_pairs={{0,16},{16,0},{1,17},{17,1},{2,18},{18,2},{3,19},{19,3},{4,20},{20... | collective-permute-start | bytes 4718600 | tf_op jit(solution)/shard_map/ppermute | solution.py:500
  611.2 274.4 %collective-permute-start.3 = (bf16[1024,768]{1,0:T(8,128)(2,1)}, bf16[1024,768]{1,0:T(8,128)(2,1)}, u32[]{:S(2)}, u32[]{:S(2)}) collective-permute-start(bf16[1024,768]{1,0:T(8,128)(2,1)} %broadcast_select_fusion.1), channel_id=1, source_target_pairs={{0,16},{16,0},{1,17},{17,1},{2,18},{18,2},{3,19},{19,3},{4,20},{20... | collective-permute-start | bytes 4718600 | tf_op jit(solution)/shard_map/ppermute | solution.py:500
  879.2 10.1 %collective-permute-start.5 = (bf16[24,9216]{1,0:T(8,128)(2,1)S(1)}, bf16[24,9216]{1,0:T(8,128)(2,1)S(1)}, u32[]{:S(2)}, u32[]{:S(2)}) collective-permute-start(bf16[24,9216]{1,0:T(8,128)(2,1)S(1)} %broadcast_select_fusion.2), channel_id=1, source_target_pairs={{0,16},{16,0},{1,17},{17,1},{2,18},{18,2},{3,19},{19,3},{4,20},{20... | collective-permute-start | bytes 1327112 | tf_op jit(solution)/shard_map/ppermute | solution.py:500
  (32 other events, 89.1 us)
Sparse Core Ops, SparseCore 0:
  19.1 63.1 all-gather.2
  85.2 152.5 all-gather.4
  457.0 144.5 reduce-scatter.3
  606.8 103.2 reduce-scatter.5
  716.0 162.0 reduce-scatter.7

commit v2 on v1

--- a/solution.py
+++ b/solution.py
@@ -41,33 +41,67 @@
     return pltpu.CompilerParams(vmem_limit_bytes=VMEM)
 
 
-def project_kernel(x_ref, gain_ref, wq_ref, wk_ref, wv_ref, normed_ref, q_ref, qt_ref, k_ref, kt_ref, v_ref, vt_ref):
+def two_weights(width, low_ref, high_ref):
+    return [
+        [(0, low_ref, 0, width)],
+        [(0, low_ref, width, width // 2), (width // 2, high_ref, 0, width // 2)],
+        [(0, high_ref, width // 2, width)],
+    ]
+
+
+def with_weights(count, width, refs, body):
+    if count == 3:
+        body([[(0, ref, 0, width)] for ref in refs])
+        return
+    section_ref, own_ref, other_ref = refs
+    pl.when(section_ref[0] == 0)(lambda: body(two_weights(width, own_ref, other_ref)))
+    pl.when(section_ref[0] != 0)(lambda: body(two_weights(width, other_ref, own_ref)))
+
+
+def weight_specs(weights, width):
+    kind, operands, places = weights
+    if kind == 3:
+        return [column((width, width), p) for p in places], list(operands)
+    section, own, other = operands
+    return [SMEM_SPEC, whole(own.shape), whole(other.shape)], [section, own, other]
+
+
+def project_kernel(count, *refs):
+    x_ref, gain_ref = refs[:2]
+    normed_ref, q_ref, qt_ref, k_ref, kt_ref, v_ref, vt_ref = refs[-7:]
+    width = x_ref.shape[1]
     x = x_ref[...].astype(F32)
     scale = lax.rsqrt(jnp.mean(x * x, axis=-1, keepdims=True) + EPS)
     normed = (x * scale * gain_ref[...]).astype(BF)
     normed_ref[...] = normed
-    for w_ref, y_ref, yt_ref in ((wq_ref, q_ref, qt_ref), (wk_ref, k_ref, kt_ref), (wv_ref, v_ref, vt_ref)):
-        y = dot(normed, w_ref[...])
-        y_ref[...] = y.astype(BF)
-        yt_ref[...] = y.T.astype(BF)
-
-
-def project(x, gain, w, places):
+
+    def body(pieces):
+        for own, y_ref, yt_ref in zip(pieces, (q_ref, k_ref, v_ref), (qt_ref, kt_ref, vt_ref)):
+            for at, w_ref, start, columns in own:
+                y = dot(normed, w_ref[:, start : start + columns])
+                y_ref[:, at : at + columns] = y.astype(BF)
+                yt_ref[at : at + columns, :] = y.T.astype(BF)
+
+    with_weights(count, width, refs[2:-7], body)
+
+
+def project(x, gain, weights):
     length, width = x.shape
     rows = pl.BlockSpec((ROWB, width), lambda i: (i, 0))
     cols = pl.BlockSpec((width, ROWB), lambda i: (0, i))
     flat = jax.ShapeDtypeStruct((length, width), BF)
     turned = jax.ShapeDtypeStruct((width, length), BF)
+    specs, operands = weight_specs(weights, width)
     return pl.pallas_call(
-        project_kernel,
+        functools.partial(project_kernel, weights[0]),
         grid=(length // ROWB,),
-        in_specs=[rows, whole((1, width))] + [column((width, width), p) for p in places],
+        in_specs=[rows, whole((1, width))] + specs,
         out_specs=[rows, rows, cols, rows, cols, rows, cols],
         out_shape=[flat, flat, turned, flat, turned, flat, turned],
         compiler_params=params(),
         cost_estimate=pl.CostEstimate(flops=6 * length * width * width, bytes_accessed=16 * length * width, transcendentals=0),
         name="project",
-    )(x, gain, w, w, w)
+    )(x, gain, *operands)
 
 
 def attend_kernel(
@@ -175,9 +209,7 @@
     v_ref,
     a_ref,
     mixed_ref,
-    dq_ref,
-    dk_ref,
-    dv_ref,
+    dqkv_ref,
     gml_ref,
     gmw_ref,
     dk_acc,
@@ -190,7 +222,8 @@
 ):
     block = pl.program_id(0)
     start = start_ref[block]
-    size = qt_ref.shape[0] // heads
+    width = qt_ref.shape[0]
+    size = width // heads
     head_rows = [slice(h * size, (h + 1) * size) for h in range(heads)]
 
     @pl.when(block == 0)
@@ -239,15 +272,15 @@
                     gmw_ref[g, h] += jnp.sum((doth * mixed_ref[g, own, :].astype(F32)).reshape(size // 8, 8, QB), axis=0)
         dv_acc[pl.ds(offset, span), :] += dot(a_all[0:span, :], do_all[...])
         dk_acc[pl.ds(offset, span), :] += dot(dz_all[0:span, :], q_all[...])
-        dq_ref[...] = dqt_acc[...].T.astype(BF)
+        dqkv_ref[pl.ds(pl.multiple_of(block * QB, QB), QB), 0:width] = dqt_acc[...].T.astype(BF)
 
     for blocks in range(1, REACH // QB + 2):
         pl.when(block - start + 1 == blocks)(functools.partial(body, blocks))
 
     @pl.when(block == pl.num_programs(0) - 1)
     def _():
-        dk_ref[...] = dk_acc[...].astype(BF)
-        dv_ref[...] = dv_acc[...].astype(BF)
+        dqkv_ref[:, width : 2 * width] = dk_acc[...].astype(BF)
+        dqkv_ref[:, 2 * width :] = dv_acc[...].astype(BF)
 
 
 def attend_back(start, mw, ml, mlx, mwx, q, qt, do, dot_, kt, v, soft, mixed):
@@ -257,7 +290,6 @@
     most = REACH + QB
     rows = pl.BlockSpec((QB, width), lambda i, s: (i, 0))
     cols = pl.BlockSpec((width, QB), lambda i, s: (0, i))
-    flat = jax.ShapeDtypeStruct((length, width), BF)
     sums = jax.ShapeDtypeStruct((heads, heads, 8, QB), F32)
     return pl.pallas_call(
         functools.partial(attend_back_kernel, heads),
@@ -278,7 +310,7 @@
                 pl.BlockSpec((1, heads // 2, most, 2 * QB), lambda i, s: (i, 0, 0, 0)),
                 pl.BlockSpec((heads, width, QB), lambda i, s: (0, 0, i)),
             ],
-            out_specs=[rows, whole((length, width)), whole((length, width)), whole(sums.shape), whole(sums.shape)],
+            out_specs=[whole((length, 3 * width)), whole(sums.shape), whole(sums.shape)],
             scratch_shapes=[
                 pltpu.VMEM((length, width), F32),
                 pltpu.VMEM((length, width), F32),
@@ -289,7 +321,7 @@
                 pltpu.VMEM((heads * QB, width), BF),
             ],
         ),
-        out_shape=[flat, flat, flat, sums, sums],
+        out_shape=[jax.ShapeDtypeStruct((length, 3 * width), BF), sums, sums],
         compiler_params=params(),
         cost_estimate=pl.CostEstimate(
             flops=8 * length * most * width * heads, bytes_accessed=50 << 20, transcendentals=0
@@ -355,17 +387,12 @@
     scale = lax.rsqrt(jnp.mean(values * values, axis=-1, keepdims=True) + EPS)
     unit = values * scale
     dn = grad * gain
-    back = scale * (dn - unit * jnp.mean(dn * unit, axis=-1, keepdims=True))
-    return back, jnp.sum(grad * unit, axis=0, keepdims=True)
+    return scale * (dn - unit * jnp.mean(dn * unit, axis=-1, keepdims=True))
 
 
 def feed_back_kernel(
-    dy_ref, slope_ref, middle_ref, gain_ref, wo_ref, wi_ref, wb_ref, gf_ref, dmiddle_ref, ga_ref, do_ref, dot_ref, gg_ref
+    dy_ref, slope_ref, middle_ref, gain_ref, wo_ref, wi_ref, wb_ref, gf_ref, dmiddle_ref, ga_ref, do_ref, dot_ref
 ):
-    @pl.when(pl.program_id(0) == 0)
-    def _():
-        gg_ref[...] = jnp.zeros_like(gg_ref)
-
     dy = dy_ref[...]
     wide = wi_ref.shape[1]
     part = wide // 4
@@ -373,9 +400,7 @@
         own = slice(c * part, (c + 1) * part)
         gf_ref[:, own] = (dot(dy, wb_ref[:, own]) * slope_ref[:, own].astype(F32)).astype(BF)
     dnormed = dot_t(gf_ref[...], wi_ref[...])
-    back, gg = norm_back(middle_ref[...], gain_ref[...], dnormed)
-    gg_ref[...] += gg
-    dmiddle = dy.astype(F32) + back
+    dmiddle = dy.astype(F32) + norm_back(middle_ref[...], gain_ref[...], dnormed)
     dmiddle_ref[...] = dmiddle
     ga = dmiddle.astype(BF)
     ga_ref[...] = ga
@@ -402,14 +427,13 @@
             column((width, wide), place_in),
             column((width, wide), place_back),
         ],
-        out_specs=[rows_wide, rows, rows, rows, pl.BlockSpec((width, ROWB), lambda i: (0, i)), whole((1, width))],
+        out_specs=[rows_wide, rows, rows, rows, pl.BlockSpec((width, ROWB), lambda i: (0, i))],
         out_shape=[
             jax.ShapeDtypeStruct((length, wide), BF),
             jax.ShapeDtypeStruct((length, width), F32),
             flat,
             flat,
             jax.ShapeDtypeStruct((width, length), BF),
-            jax.ShapeDtypeStruct((1, width), F32),
         ],
         compiler_params=params(),
         cost_estimate=pl.CostEstimate(flops=18 * length * width * width, bytes_accessed=40 << 20, transcendentals=0),
@@ -417,72 +441,54 @@
     )(dy, slope, middle, gain, w, w, w)
 
 
-def project_back_kernel(dq_ref, dk_ref, dv_ref, x_ref, dmiddle_ref, gain_ref, wq_ref, wk_ref, wv_ref, dx_ref, gg_ref):
-    @pl.when(pl.program_id(0) == 0)
-    def _():
-        gg_ref[...] = jnp.zeros_like(gg_ref)
-
-    dnormed = dot_t(dq_ref[...], wq_ref[...]) + dot_t(dk_ref[...], wk_ref[...]) + dot_t(dv_ref[...], wv_ref[...])
-    back, gg = norm_back(x_ref[...].astype(F32), gain_ref[...], dnormed)
-    gg_ref[...] += gg
-    dx_ref[...] = (dmiddle_ref[...] + back).astype(BF)
-
-
-def project_back(dq, dk, dv, x, dmiddle, gain, w, places):
+def project_back_kernel(count, dqkv_ref, x_ref, dmiddle_ref, gain_ref, *refs):
+    dx_ref = refs[-1]
+    width = x_ref.shape[1]
+
+    def body(pieces):
+        dnormed = None
+        for i, own in enumerate(pieces):
+            for at, w_ref, start, columns in own:
+                first = i * width + at
+                term = dot_t(dqkv_ref[:, first : first + columns], w_ref[:, start : start + columns])
+                dnormed = term if dnormed is None else dnormed + term
+        dx_ref[...] = (dmiddle_ref[...] + norm_back(x_ref[...].astype(F32), gain_ref[...], dnormed)).astype(BF)
+
+    with_weights(count, width, refs[:-1], body)
+
+
+def project_back(dqkv, x, dmiddle, gain, weights):
     length, width = x.shape
     rows = pl.BlockSpec((ROWB, width), lambda i: (i, 0))
+    specs, operands = weight_specs(weights, width)
     return pl.pallas_call(
-        project_back_kernel,
+        functools.partial(project_back_kernel, weights[0]),
         grid=(length // ROWB,),
-        in_specs=[rows] * 5 + [whole((1, width))] + [column((width, width), p) for p in places],
-        out_specs=[rows, whole((1, width))],
-        out_shape=[jax.ShapeDtypeStruct((length, width), BF), jax.ShapeDtypeStruct((1, width), F32)],
+        in_specs=[pl.BlockSpec((ROWB, 3 * width), lambda i: (i, 0)), rows, rows, whole((1, width))] + specs,
+        out_specs=rows,
+        out_shape=jax.ShapeDtypeStruct((length, width), BF),
         compiler_params=params(),
         cost_estimate=pl.CostEstimate(flops=6 * length * width * width, bytes_accessed=18 << 20, transcendentals=0),
         name="project_back",
-    )(dq, dk, dv, x, dmiddle, gain, w, w, w)
+    )(dqkv, x, dmiddle, gain, *operands)
 
 
 def weight_grad(left, right):
-    return lax.dot_general(left, right, (((0,), (0,)), ((), ())), preferred_element_type=F32).astype(BF)
+    return lax.dot_general(left, right, (((0,), (0,)), ((), ())), preferred_element_type=F32)
 
 
 def mix_tables(mix_logits, mix_weights, size):
-    scaled = mix_logits * (LOG2E * size ** (-0.5))
-    wide_logits = jnp.repeat(scaled.T, size, axis=1)
-    wide_weights = jnp.repeat(mix_weights, size, axis=1)
-    return scaled, mix_logits * size ** (-0.5), wide_logits, wide_weights
+    plain = mix_logits * size ** (-0.5)
+    return mix_weights, plain * LOG2E, plain, jnp.repeat(plain.T, size, axis=1), jnp.repeat(mix_weights, size, axis=1)
 
 
 def layer_forward(x, seg, weights, tables):
-    gains, w_qkv, at_qkv, w_rest, at_rest = weights
+    gains, w_qkv, w_rest, places = weights
     start, segc, segr = seg
-    scaled, _, _, mix_weights = tables[:4]
-    normed, q, qt, k, kt, v, vt = project(x, gains[0], w_qkv, at_qkv)
-    o, soft, mixed = attend(start, tables[4], scaled, qt, k, vt, segc, segr)
-    y, middle, normed_two, slope, hidden = feed(x, o, gains[1], w_rest, *at_rest)
+    normed, q, qt, k, kt, v, vt = project(x, gains[0], w_qkv)
+    o, soft, mixed = attend(start, tables[0], tables[1], qt, k, vt, segc, segr)
+    y, middle, normed_two, slope, hidden = feed(x, o, gains[1], w_rest, *places)
     return y, (x, normed, q, qt, kt, v, o, soft, mixed, middle, normed_two, slope, hidden)
-
-
-def layer_backward(dy, seg, kept, weights, tables):
-    gains, w_qkv, at_qkv, w_rest, at_rest = weights
-    x, normed, q, qt, kt, v, o, soft, mixed, middle, normed_two, slope, hidden = kept
-    start = seg[0]
-    _, plain, wide_logits, wide_weights, mix_weights = tables
-    gf, dmiddle, ga, do, dot_, gg_ffn = feed_back(dy, slope, middle, gains[1], w_rest, *at_rest)
-    grad_back = weight_grad(dy, hidden)
-    grad_in = weight_grad(normed_two, gf)
-    grad_out = weight_grad(ga, o)
-    size = q.shape[1] // mix_weights.shape[0]
-    unscaled = wide_logits * (1.0 / LOG2E)
-    dq, dk, dv, gml, gmw = attend_back(
-        start, mix_weights, plain, unscaled, wide_weights, q, qt, do, dot_, kt, v, soft, mixed
-    )
-    grads_qkv = [weight_grad(normed, g) for g in (dq, dk, dv)]
-    dx, gg_attn = project_back(dq, dk, dv, x, dmiddle, gains[0], w_qkv, at_qkv)
-    gml = jnp.sum(gml, axis=(2, 3)).T * size ** (-0.5)
-    gmw = jnp.sum(gmw, axis=(2, 3))
-    return dx, (grad_in, grad_back, grad_out), grads_qkv, (gg_attn, gg_ffn, gml, gmw)
 
 
 def windows(seg):
@@ -498,6 +504,52 @@
 
 def swap(x):
     return lax.ppermute(x, "section", [(0, 1), (1, 0)])
+
+
+def partners(x, mask):
+    return lax.ppermute(x, "dp", [(i, i ^ mask) for i in range(lax.axis_size("dp"))])
+
+
+def bit_groups():
+    bits = lax.axis_size("dp").bit_length() - 1
+    return [(at, 1 << min(2, bits - at)) for at in range(0, bits, 2)]
+
+
+def gather_rows(own):
+    share, columns = own.shape
+    place = lax.axis_index("dp")
+    done = own[None]
+    for shift, members in reversed(bit_groups()):
+        me = (place >> shift) & (members - 1)
+        out = jnp.zeros((done.shape[0], members, share, columns), own.dtype)
+        for other in range(members):
+            piece = done if other == 0 else partners(done, other << shift)
+            out = lax.dynamic_update_slice(out, piece[:, None], (0, me ^ other, 0, 0))
+        done = out.reshape(-1, share, columns)
+    return done.reshape(-1, columns)
+
+
+def reduce_rows(whole_rows):
+    size = lax.axis_size("dp")
+    columns = whole_rows.shape[1]
+    share = whole_rows.shape[0] // size
+    place = lax.axis_index("dp")
+    held = whole_rows.reshape(size, share, columns)
+    for shift, members in bit_groups():
+        me = (place >> shift) & (members - 1)
+        held = held.astype(BF).reshape(-1, members, share, columns)
+        total = lax.dynamic_index_in_dim(held, me, 1, keepdims=False).astype(F32)
+        for other in range(1, members):
+            piece = lax.dynamic_index_in_dim(held, me ^ other, 1, keepdims=False)
+            total = total + partners(piece, other << shift).astype(F32)
+        held = total
+    return held.reshape(share, columns)
+
+
+def sum_everywhere(x):
+    for bit in range(lax.axis_size("dp").bit_length() - 1):
+        x = x + partners(x, 1 << bit)
+    return x + swap(x)
 
 
 def on_device(
@@ -522,72 +574,116 @@
     size = width // heads
     share = w_query.shape[1]
     half = share // 2
+    wide = w_in.shape[2]
+    middle = 3 * width // 2
 
     x0 = lax.dynamic_index_in_dim(tokens, section, 0, keepdims=False)
     seg = windows(lax.dynamic_index_in_dim(segments, section, 0, keepdims=False))
     cot = lax.dynamic_index_in_dim(cotangent, section, 0, keepdims=False)
 
     gains = jnp.concatenate([gain_attn, gain_ffn], 0).astype(BF)
-    gains = jnp.pad(gains.T, ((0, 0), (0, 126)))
+    gain_columns = jnp.pad(gains.T, ((0, 0), (0, 126)))
     qkv = jnp.concatenate([w_query[0], w_key[0], w_value[0]], 1).astype(BF)
-    early = jnp.concatenate([qkv, gains], 1)
+    low = jnp.concatenate([qkv[:, :middle], gain_columns], 1)
+    high = jnp.concatenate([qkv[:, middle:], gain_columns], 1)
+    from_first = swap(high)
+    own_half = gather_rows(jnp.where(first, low, from_first))
+    other_half = swap(own_half)
+
     late = jnp.concatenate([w_in[0].astype(BF), w_back[0].T.astype(BF), w_out[0].T.astype(BF)], 1)
 
     def halves(own):
         other = swap(jnp.where(first, own[half:], own[:half]))
         return jnp.where(first, own[:half], other), jnp.where(first, other, own[half:])
 
-    early0, early1 = halves(early)
-    early_all0 = lax.all_gather(early0, AXES, axis=0, tiled=True)
     late0, late1 = halves(late)
-    wide = w_in.shape[2]
-    rest = jnp.concatenate(
-        [late0[:, : 2 * wide], late1[:, : 2 * wide], late0[:, 2 * wide :], late1[:, 2 * wide :], early1], 1
-    )
-    rest_all = lax.all_gather(rest, AXES, axis=0, tiled=True)
+    early1 = halves(jnp.concatenate([qkv, gain_columns], 1))[1]
+    second = lax.all_gather(jnp.concatenate([late0, early1], 1), AXES, axis=0, tiled=True)
+    third = lax.all_gather(late1, AXES, axis=0, tiled=True)
 
     own_mix = jnp.concatenate([mix_logits, mix_weights], 0)
     other_mix = swap(own_mix)
     mix0 = jnp.where(first, own_mix, other_mix)
     mix1 = jnp.where(first, other_mix, own_mix)
+    tables = [mix_tables(m[0], m[1], size) for m in (mix0, mix1)]
 
     def gain_rows(columns):
         rows = columns[:, :2].astype(F32).T
         return rows[0:1], rows[1:2]
 
-    tables = [mix_tables(m[0], m[1], size) + (m[1],) for m in (mix0, mix1)]
-    at = 4 * wide // width
-    weights0 = (gain_rows(early_all0[:, 3 * width :]), early_all0, (0, 1, 2), rest_all, (at, 0, 1))
-    end = 4 * wide + 5 * width
-    weights1 = (gain_rows(rest_all[:, end:]), rest_all, (at + 2, at + 3, at + 4), rest_all, (at + 1, 2, 3))
+    at_out = 2 * wide // width
+    end = 2 * wide + 4 * width
+    qkv0 = (2, (section.astype(jnp.int32).reshape(1), own_half, other_half), ())
+    qkv1 = (3, (second,) * 3, (at_out + 1, at_out + 2, at_out + 3))
+    weights0 = (gain_rows(own_half[:, middle:]), qkv0, second, (at_out, 0, 1))
+    weights1 = (gain_rows(second[:, end:]), qkv1, third, (at_out, 0, 1))
 
     y0, kept0 = layer_forward(x0, seg, weights0, tables[0])
     y1, kept1 = layer_forward(y0, seg, weights1, tables[1])
 
-    dx1, ffn1, qkv1, small1 = layer_backward(cot, seg, kept1, weights1, tables[1])
-    dx0, ffn0, qkv0, small0 = layer_backward(dx1, seg, kept0, weights0, tables[0])
-
-    def scatter(pieces):
-        packed = jnp.concatenate(pieces, 1)
-        return lax.psum_scatter(packed, AXES, scatter_dimension=0, tiled=True)
-
-    sums1 = scatter(list(ffn1) + qkv1)
-    sums0 = jnp.concatenate([scatter(list(ffn0)), scatter(qkv0)], 1)
-    other = swap(jnp.where(first, sums1, sums0))
-    mine = jnp.where(first, jnp.concatenate([sums0, other], 0), jnp.concatenate([other, sums1], 0)).astype(F32)
-    grad_in = mine[:, :wide]
-    grad_back = mine[:, wide : 2 * wide].T
-    grad_out = mine[:, 2 * wide : 2 * wide + width].T
-    grads = [mine[:, 2 * wide + i * width : 2 * wide + (i + 1) * width] for i in (1, 2, 3)]
-
-    small = jnp.stack([jnp.concatenate([s.reshape(-1) for s in parts]) for parts in (small0, small1)])
-    small = lax.psum(small, AXES)
-    small = jnp.where(first, small[0], small[1])
-    place = lax.axis_index("dp") * share
-    gg_attn = lax.dynamic_slice_in_dim(small, place, share)[None]
-    gg_ffn = lax.dynamic_slice_in_dim(small, width + place, share)[None]
-    gml = small[2 * width : 2 * width + heads * heads].reshape(1, heads, heads)
-    gmw = small[2 * width + heads * heads :].reshape(1, heads, heads)
+    def back_feed(dy, kept, weights):
+        slope, middle_rows = kept[11], kept[9]
+        return feed_back(dy, slope, middle_rows, weights[0][1], weights[2], *weights[3])
+
+    def back_attend(do, dot_, kept, table):
+        _, _, q, qt, kt, v, _, soft, mixed = kept[:9]
+        mix, _, plain, wide_logits, wide_weights = table
+        dqkv, gml, gmw = attend_back(
+            seg[0], mix, plain, wide_logits, wide_weights, q, qt, do, dot_, kt, v, soft, mixed
+        )
+        return dqkv, jnp.stack([jnp.sum(gml, axis=(2, 3)).T * size ** (-0.5), jnp.sum(gmw, axis=(2, 3))])
+
+    gf, dmiddle, ga, do, dot_ = back_feed(cot, kept1, weights1)
+    grads1 = [weight_grad(cot, kept1[12]), weight_grad(kept1[10], gf), weight_grad(ga, kept1[6])]
+    grads1 = [grads1[1], grads1[0], grads1[2]]
+    dqkv, mix_sums1 = back_attend(do, dot_, kept1, tables[1])
+    grads1.append(weight_grad(kept1[1], dqkv))
+    packed1 = jnp.concatenate([g.astype(BF) for g in grads1], 1)
+    dx1 = project_back(dqkv, kept1[0], dmiddle, weights1[0][0], qkv1)
+    dx1, packed1 = lax.optimization_barrier((dx1, packed1))
+    sums1 = lax.psum_scatter(packed1, AXES, scatter_dimension=0, tiled=True)
+
+    def shared_grad(left, right):
+        columns = right.shape[1] // 2
+        away = lax.dynamic_slice_in_dim(right, (1 - section) * columns, columns, 1)
+        here = lax.dynamic_slice_in_dim(right, section * columns, columns, 1)
+        arrived = swap(weight_grad(left, away).astype(BF))
+        return (weight_grad(left, here) + arrived.astype(F32)).astype(BF)
+
+    gf, dmiddle, ga, do, dot_ = back_feed(dx1, kept0, weights0)
+    packed0 = jnp.concatenate(
+        [shared_grad(kept0[10], gf), shared_grad(dx1, kept0[12]), shared_grad(ga, kept0[6])], 1
+    )
+    do, packed0 = lax.optimization_barrier((do, packed0))
+    ffn0 = reduce_rows(packed0)
+    dqkv, mix_sums0 = back_attend(do, dot_, kept0, tables[0])
+    proj0 = reduce_rows(shared_grad(kept0[1], dqkv))
+    dx0 = project_back(dqkv, kept0[0], dmiddle, weights0[0][0], qkv0)
+
+    ffn0_other = lax.ppermute(ffn0, "section", [(1, 0)])
+    proj0_other = lax.ppermute(proj0, "section", [(1, 0)])
+    sums1_other = lax.ppermute(sums1, "section", [(0, 1)])
+    sums1 = jnp.concatenate([sums1_other, sums1], 0).astype(F32)
+    cuts = (0, wide // 2, wide, wide + width // 2)
+
+    def join(i):
+        return jnp.concatenate([ffn0[:, cuts[i] : cuts[i + 1]], ffn0_other[:, cuts[i] : cuts[i + 1]]], 1)
+
+    grad_in = jnp.where(first, join(0), sums1[:, :wide])
+    grad_back = jnp.where(first, join(1), sums1[:, wide : 2 * wide])
+    grad_out = jnp.where(first, join(2), sums1[:, 2 * wide : 2 * wide + width])
+    grad_qkv = jnp.where(first, jnp.concatenate([proj0, proj0_other], 1), sums1[:, 2 * wide + width :])
+
+    def gain_grad(pairs, gain):
+        total = sum(jnp.sum(w.astype(BF).astype(F32) * g, axis=1) for w, g in pairs)
+        return (total / gain[0].astype(BF).astype(F32))[None]
+
+    parts = [grad_qkv[:, i * width : (i + 1) * width] for i in range(3)]
+    gg_attn = gain_grad(list(zip((w_query[0], w_key[0], w_value[0]), parts)), gain_attn)
+    gg_ffn = gain_grad([(w_in[0], grad_in)], gain_ffn)
+
+    mix_sums = sum_everywhere(jnp.stack([mix_sums0, mix_sums1]))
+    mix_sums = jnp.where(first, mix_sums[0], mix_sums[1])
 
     def outputs(own0, own1):
         other = swap(jnp.where(first, own1, own0))
@@ -598,14 +694,14 @@
         outputs(dx0, dx1),
         gg_attn,
         gg_ffn,
-        grads[0][None],
-        grads[1][None],
-        grads[2][None],
-        grad_out[None],
+        parts[0][None],
+        parts[1][None],
+        parts[2][None],
+        grad_out.T[None],
         grad_in[None],
-        grad_back[None],
-        gml,
-        gmw,
+        grad_back.T[None],
+        mix_sums[0][None],
+        mix_sums[1][None],
     )
 
 

time: 903 us -> 658 us (0.73)
  waiting for transfers between devices: 432 us -> 124 us
  starting transfers between devices: 4.1 us -> 69.1 us
  blocking collectives: 47.3 us -> 0 us
  Pallas kernels: 280 us -> 303 us
  other arithmetic: 38.1 us -> 54.8 us
    reduce_scatter x3 -> x1, waiting for transfers between devices: 262 us -> 0.01 us  [on_device(): sums1 = lax.psum_scatter(packed1, AXES, scatter_dimension=0, tiled=True)]
    all_gather x2, waiting for transfers between devices: 169 us -> 32.1 us  [the longest x1 24.4 us: on_device(): third = lax.all_gather(late1, AXES, axis=0, tiled=True)]
    ppermute x0 -> x25, waiting for transfers between devices: none -> 88.9 us  [the longest x22 86.4 us: partners(): lax.ppermute(x, 'dp', [(i, i ^ mask) for i in range(lax.axis_size('dp'))])]
    ppermute x0 -> x25, starting transfers between devices: none -> 49.4 us  [the longest x22 40.6 us: partners(): lax.ppermute(x, 'dp', [(i, i ^ mask) for i in range(lax.axis_size('dp'))])]
    psum x1 -> x0, blocking collectives: 47.3 us -> none  [on_device(): small = lax.psum(small, AXES)]
    ppermute x6 -> x12, starting transfers between devices: 3.9 us -> 19.6 us  [swap(): return lax.ppermute(x, 'section', [(0, 1), (1, 0)])]
    pallas_call x2, Pallas kernels: 89.8 us -> 102 us  [attend_back(): pl.pallas_call(functools.partial(attend_back_kernel, heads), grid_spec=pl...]
    pallas_call x2, Pallas kernels: 56.9 us -> 67.6 us  [attend(): pl.pallas_call(functools.partial(attend_kernel, heads), grid_spec=pltpu.P...]
  transfers between devices with their start and end apart: 11 -> 40, of which waited for: 4 -> 18; matrix products, arithmetic and copies ran while one was open for 8% -> 15% of each run, Pallas kernels for 10% -> 29%
where the time goes in v2:
time: 658 us; the launch traced here: 654 us
  Pallas kernels  303 us (46%)
  waiting for transfers between devices  124 us (19%)
  starting transfers between devices  69.1 us (11%)
  matrix products  61.7 us (9%)
  other arithmetic  54.8 us (8%)
  local copies, waits for them, and re-layouts  25.4 us (4%)
  between operations  14.9 us (2%)
    pallas_call x2, Pallas kernels, attend_back(): pl.pallas_call(functools.partial(attend_back_kernel, heads), grid_spec=pl...  102 us
    ppermute x22, waiting for transfers between devices, partners(): lax.ppermute(x, 'dp', [(i, i ^ mask) for i in range(lax.axis_size('dp'))])  86.4 us
    pallas_call x2, Pallas kernels, attend(): pl.pallas_call(functools.partial(attend_kernel, heads), grid_spec=pltpu.P...  67.6 us
    dot_general x12, matrix products, weight_grad(): lax.dot_general(left, right, (((0,), (0,)), ((), ())), preferred_element_...  61.7 us
    pallas_call x2, Pallas kernels, feed(): pl.pallas_call(feed_kernel, grid=(length // ROWB,), in_specs=[rows, rows,...  52.2 us
    pallas_call x2, Pallas kernels, feed_back(): pl.pallas_call(feed_back_kernel, grid=(length // ROWB,), in_specs=[rows,...  44.6 us
    ppermute x22, starting transfers between devices, partners(): lax.ppermute(x, 'dp', [(i, i ^ mask) for i in range(lax.axis_size('dp'))])  40.6 us
    all_gather x1, waiting for transfers between devices, on_device(): third = lax.all_gather(late1, AXES, axis=0, tiled=True)  24.4 us
  transfers between devices with their start and end apart: 40, of which 18 were waited for; matrix products, arithmetic and copies ran while one was open for 15% of the time, Pallas kernels for 29%

profile of v2, /device:TPU:1, one launch (start us, length us, event | category | flops | bytes accessed | tf_op | source)
XLA Modules:
  0.0 653.6 jit_solution(16730767550038809878)
XLA Ops:
  45.3 7.4 %collective-permute-done.7 = bf16[4,48,1280]{2,1,0:T(8,128)(2,1)S(1)} collective-permute-done((bf16[4,48,1280]{2,1,0:T(8,128)(2,1)}, bf16[4,48,1280]{2,1,0:T(8,128)(2,1)S(1)}, u32[]{:S(2)}, u32[]{:S(2)}) %collective-permute-start.7) | collective-permute-done | bytes 491552 | tf_op jit(solution)/shard_map/ppermute | solution.py:510
  53.5 14.8 %collective-permute-start.8 = (bf16[768,1280]{1,0:T(8,128)(2,1)}, bf16[768,1280]{1,0:T(8,128)(2,1)}, u32[]{:S(2)}, u32[]{:S(2)}) collective-permute-start(bf16[768,1280]{1,0:T(8,128)(2,1)} %bitcast.21.refs_3_.refs_1_), channel_id=1, source_target_pairs={{0,16},{16,0},{1,17},{17,1},{2,18},{18,2},{3,19},{19,3},{4,20},{20... | collective-permute-start | bytes 5898248 | tf_op jit(solution)/shard_map/ppermute | solution.py:506
  78.6 9.8 %project.2 = (bf16[1024,768]{1,0:T(8,128)(2,1)}, bf16[1024,768]{1,0:T(8,128)(2,1)}, bf16[768,1024]{1,0:T(8,128)(2,1)}, bf16[1024,768]{1,0:T(8,128)(2,1)}, bf16[7...) custom-call(bf16[1024,768]{1,0:T(8,128)(2,1)} %dynamic-slice_bitcast_fusion.1.refs_0_.x_ref, ...), custom_call_target="tpu_custom_call" | custom-call | flops 3623878656 | bytes 12582912 | tf_op jit(solution)/shard_map/project/pallas_call | solution.py:95
  88.4 40.9 %attend.2 = (bf16[1024,768]{1,0:T(8,128)(2,1)}, bf16[8,6,640,256]{3,2,1,0:T(8,128)(2,1)}, bf16[12,768,1024]{2,1,0:T(8,128)(2,1)}) custom-call(s32[8]{0:T(128)} %convert_reduce_fusion.start_ref, f32[12,12]{1,0:T(8,128)} %get-tuple-element.213.mw_ref, f32[12,12]{1,0:T(8,128)} %get-tuple-element.212.ml_ref, bf16[768,1024]{1,0:T(8,128)(2,1)} %get-tuple-element.62.qt_ref, ...), custom_call_target="tpu_custom_call" | custom-call | flops 24159191040 | bytes 41943040 | tf_op jit(solution)/shard_map/attend/pallas_call | solution.py:163
  129.3 7.7 %all-gather.3.cloned.1.call-done.wo_ref.wi_ref.wb_ref.refs_2_.refs_3_.refs_4_.refs_0_.refs_1_ = bf16[768,9344]{1,0:T(8,128)(2,1)} async-done(((bf16[24,9344]{1,0:T(8,128)(2,1)}), bf16[768,9344]{1,0:T(8,128)(2,1)}) %all-gather.3.cloned.1.call-update) | async-done | bytes 14352400 | tf_op jit(solution)/shard_map/all_gather | solution.py:601
  139.6 26.1 %feed.2 = (bf16[1024,768]{1,0:T(8,128)(2,1)}, f32[1024,768]{1,0:T(8,128)}, bf16[1024,768]{1,0:T(8,128)(2,1)}, bf16[1024,3072]{1,0:T(8,128)(2,1)}, bf16[1024,3072]{1,0:T(8,128)(2,1)}) custom-call(bf16[1024,768]{1,0:T(8,128)(2,1)} %dynamic-slice_bitcast_fusion.1.refs_0_.x_ref, bf16[1024,768]{1,0:T(8,128)(2,1)} %get-tuple-element.65.o_ref, ...), custom_call_target="tpu_custom_call" | custom-call | flops 10871635968 | bytes 31457280 | tf_op jit(solution)/shard_map/feed/pallas_call | solution.py:365
  165.7 8.4 %project.3 = (bf16[1024,768]{1,0:T(8,128)(2,1)}, bf16[1024,768]{1,0:T(8,128)(2,1)}, bf16[768,1024]{1,0:T(8,128)(2,1)}, bf16[1024,768]{1,0:T(8,128)(2,1)}, bf16[7...) custom-call(bf16[1024,768]{1,0:T(8,128)(2,1)} %get-tuple-element.66.refs_0_.x_ref, ...), custom_call_target="tpu_custom_call" | custom-call | flops 3623878656 | bytes 12582912 | tf_op jit(solution)/shard_map/project/pallas_call | solution.py:95
  174.1 26.7 %attend.3 = (bf16[1024,768]{1,0:T(8,128)(2,1)}, bf16[8,6,640,256]{3,2,1,0:T(8,128)(2,1)}, bf16[12,768,1024]{2,1,0:T(8,128)(2,1)}) custom-call(s32[8]{0:T(128)} %convert_reduce_fusion.start_ref, f32[12,12]{1,0:T(8,128)} %copy-done.24, f32[12,12]{1,0:T(8,128)} %get-tuple-element.216.ml_ref, bf16[768,1024]{1,0:T(8,128)(2,1)} %get-tuple-element.67.qt_ref, ...), custom_call_target="tpu_custom_call" | custom-call | flops 24159191040 | bytes 41943040 | tf_op jit(solution)/shard_map/attend/pallas_call | solution.py:163
  200.9 24.4 %all-gather.5.cloned.1.call-done.wo_ref.wi_ref.wb_ref = bf16[768,6912]{1,0:T(8,128)(2,1)} async-done(((bf16[24,6912]{1,0:T(8,128)(2,1)}), bf16[768,6912]{1,0:T(8,128)(2,1)}) %all-gather.5.cloned.1.call-update) | async-done | bytes 10616848 | tf_op jit(solution)/shard_map/all_gather | solution.py:602
  225.3 26.1 %feed.3 = (bf16[1024,768]{1,0:T(8,128)(2,1)}, f32[1024,768]{1,0:T(8,128)}, bf16[1024,768]{1,0:T(8,128)(2,1)}, bf16[1024,3072]{1,0:T(8,128)(2,1)}, bf16[1024,3072]{1,0:T(8,128)(2,1)}) custom-call(bf16[1024,768]{1,0:T(8,128)(2,1)} %get-tuple-element.66.refs_0_.x_ref, bf16[1024,768]{1,0:T(8,128)(2,1)} %get-tuple-element.70.o_ref, f32[1,768]{1,0:T(1,128)} %copy.146.gain_ref, ...), custom_call_target="tpu_custom_call" | custom-call | flops 10871635968 | bytes 31457280 | tf_op jit(solution)/shard_map/feed/pallas_call | solution.py:365
  251.4 22.3 %feed_back.2 = (bf16[1024,3072]{1,0:T(8,128)(2,1)}, f32[1024,768]{1,0:T(8,128)}, bf16[1024,768]{1,0:T(8,128)(2,1)}, bf16[1024,768]{1,0:T(8,128)(2,1)}, bf16[768,1024]{1,0:T(8,128)(2,1)}) custom-call(bf16[1024,768]{1,0:T(8,128)(2,1)} %dynamic-slice_bitcast_fusion.dy_ref, bf16[1024,3072]{1,0:T(8,128)(2,1)} %get-tuple-element.74.slope_ref, ...), custom_call_target="tpu_custom_call" | custom-call | flops 10871635968 | bytes 41943040 | tf_op jit(solution)/shard_map/feed_back/pallas_call | solution.py:418
  277.2 9.7 %convolution_convert_fusion = bf16[768,3072]{1,0:T(8,128)(2,1)} fusion(bf16[1024,768]{1,0:T(8,128)(2,1)S(1)} %copy-done.6, bf16[1024,3072]{1,0:T(8,128)(2,1)} %get-tuple-element.86), kind=kOutput, calls=%fused_computation.2 | convolution fusion | flops 4834197504 | bytes 12582912 | tf_op jit(solution)/shard_map/dot_general | solution.py:477
  293.7 58.7 %attend_back.2 = (bf16[1024,2304]{1,0:T(8,128)(2,1)}, f32[12,12,8,128]{3,2,1,0:T(8,128)}, f32[12,12,8,128]{3,2,1,0:T(8,128)}) custom-call(s32[8]{0:T(128)} %convert_reduce_fusion.start_ref, f32[12,12]{1,0:T(8,128)} %copy-done.24, f32[12,12]{1,0:T(8,128)} %get-tuple-element.215.ml_ref, f32[12,768]{1,0:T(8,128)} %reshape.235.mlx_ref, ...), custom_call_target="tpu_custom_call" | custom-call | flops 48318382080 | bytes 52428800 | tf_op jit(solution)/shard_map/attend_back/pallas_call | solution.py:294
  359.1 10.7 %pad_maximum_fusion = bf16[768,9216]{1,0:T(8,128)(2,1)} fusion(bf16[768,2304]{1,0:T(8,128)(2,1)S(1)} %convolution_convert_fusion.2, bf16[768,768]{1,0:T(8,128)(2,1)S(1)} %convolution_convert_fusion.6, bf16[768,3072]{1,0:T(8,128)(2,1)S(1)} %copy-done.7, bf16[768,3072]{1,0:T(8,128)(2,1)S(1)} %copy-done.8), kind=kLoop, calls=%fused_computation | loop fusion | flops 56623104 | bytes 28311552 | tf_op jit(solution)/shard_map/concatenate | solution.py:641
  369.9 9.5 %project_back.2.dy_ref = bf16[1024,768]{1,0:T(8,128)(2,1)} custom-call(bf16[1024,2304]{1,0:T(8,128)(2,1)} %get-tuple-element.82.dqkv_ref, bf16[1024,768]{1,0:T(8,128)(2,1)} %get-tuple-element.66.refs_0_.x_ref, f32[1024,768]{1,0:T(8,128)} %get-tuple-element.83.dmiddle_ref, f32[1,768]{1,0:T(1,128)} %copy.144.refs_1_.gain_ref, ...), custom_call_target="tpu_custom_call" | custom-call | flops 3623878656 | bytes 18874368 | tf_op jit(solution)/shard_map/project_back/pallas_call | solution.py:464
  379.4 22.4 %feed_back.3 = (bf16[1024,3072]{1,0:T(8,128)(2,1)}, f32[1024,768]{1,0:T(8,128)}, bf16[1024,768]{1,0:T(8,128)(2,1)}, bf16[1024,768]{1,0:T(8,128)(2,1)}, bf16[768,1024]{1,0:T(8,128)(2,1)}) custom-call(bf16[1024,768]{1,0:T(8,128)(2,1)} %project_back.2.dy_ref, bf16[1024,3072]{1,0:T(8,128)(2,1)} %get-tuple-element.90.slope_ref, ...), custom_call_target="tpu_custom_call" | custom-call | flops 10871635968 | bytes 41943040 | tf_op jit(solution)/shard_map/feed_back/pallas_call | solution.py:418
  441.2 42.8 %attend_back.3 = (bf16[1024,2304]{1,0:T(8,128)(2,1)}, f32[12,12,8,128]{3,2,1,0:T(8,128)}, f32[12,12,8,128]{3,2,1,0:T(8,128)}) custom-call(s32[8]{0:T(128)} %convert_reduce_fusion.start_ref, f32[12,12]{1,0:T(8,128)} %get-tuple-element.213.mw_ref, f32[12,12]{1,0:T(8,128)} %get-tuple-element.211.ml_ref, f32[12,768]{1,0:T(8,128)} %reshape.233.mlx_ref, ...), custom_call_target="tpu_custom_call" | custom-call | flops 48318382080 | bytes 52428800 | tf_op jit(solution)/shard_map/attend_back/pallas_call | solution.py:294
  486.9 7.7 %collective-permute-start.32 = (f32[2,2,12,12]{2,3,1,0:T(8,128)S(1)}, f32[2,2,12,12]{2,3,1,0:T(8,128)S(1)}, u32[]{:S(2)}, u32[]{:S(2)}) collective-permute-start(f32[2,2,12,12]{2,3,1,0:T(8,128)S(1)} %pad_maximum_fusion.8), channel_id=1, source_target_pairs={{0,1},{1,0},{2,3},{3,2},{4,5},{5,4},{6,7},{7,6},{8,9},{9,8},{10,11... | collective-permute-start | bytes 6920 | tf_op jit(solution)/shard_map/ppermute | solution.py:510
  498.7 7.1 %collective-permute-start.33 = (f32[2,2,12,12]{2,3,1,0:T(8,128)S(1)}, f32[2,2,12,12]{2,3,1,0:T(8,128)S(1)}, u32[]{:S(2)}, u32[]{:S(2)}) collective-permute-start(f32[2,2,12,12]{2,3,1,0:T(8,128)S(1)} %fusion.42), channel_id=1, source_target_pairs={{0,2},{1,3},{2,0},{3,1},{4,6},{5,7},{6,4},{7,5},{8,10},{9,11},{10,... | collective-permute-start | bytes 6920 | tf_op jit(solution)/shard_map/ppermute | solution.py:510
  516.9 9.8 %project_back.3 = bf16[1024,768]{1,0:T(8,128)(2,1)} custom-call(bf16[1024,2304]{1,0:T(8,128)(2,1)} %get-tuple-element.103.dqkv_ref, bf16[1024,768]{1,0:T(8,128)(2,1)} %dynamic-slice_bitcast_fusion.1.refs_0_.x_ref, f32[1024,768]{1,0:T(8,128)} %get-tuple-element.104.dmiddle_ref, f32[1,768]{1,0:T(1,128)} %copy.141.refs_1_.gain_ref, s32[1]{0:T(128)} %bitcast.23.refs_2_.refs_0_, ...), custom_call_target="tpu_custom_call" | custom-call | flops 3623878656 | bytes 18874368 | tf_op jit(solution)/shard_map/project_back/pallas_call | solution.py:464
  532.0 11.5 %collective-permute-done.25 = bf16[4,48,3456]{2,1,0:T(8,128)(2,1)} collective-permute-done((bf16[4,48,3456]{2,1,0:T(8,128)(2,1)}, bf16[4,48,3456]{2,1,0:T(8,128)(2,1)}, u32[]{:S(2)}, u32[]{:S(2)}) %collective-permute-start.25) | collective-permute-done | bytes 1327136 | tf_op jit(solution)/shard_map/ppermute | solution.py:510
  543.5 37.1 %collective-permute-done.26 = bf16[4,48,3456]{2,1,0:T(8,128)(2,1)} collective-permute-done((bf16[4,48,3456]{2,1,0:T(8,128)(2,1)}, bf16[4,48,3456]{2,1,0:T(8,128)(2,1)}, u32[]{:S(2)}, u32[]{:S(2)}) %collective-permute-start.26) | collective-permute-done | bytes 1327136 | tf_op jit(solution)/shard_map/ppermute | solution.py:510
  601.7 7.2 %collective-permute-done.30 = bf16[1,48,3456]{2,1,0:T(8,128)(2,1)S(1)} collective-permute-done((bf16[1,48,3456]{2,1,0:T(8,128)(2,1)S(1)}, bf16[1,48,3456]{2,1,0:T(8,128)(2,1)S(1)}, u32[]{:S(2)}, u32[]{:S(2)}) %collective-permute-start.30) | collective-permute-done | bytes 331808 | tf_op jit(solution)/shard_map/ppermute | solution.py:510
  623.7 7.5 %collective-permute-done.21 = bf16[1,48,1152]{2,1,0:T(8,128)(2,1)S(1)} collective-permute-done((bf16[1,48,1152]{2,1,0:T(8,128)(2,1)S(1)}, bf16[1,48,1152]{2,1,0:T(8,128)(2,1)S(1)}, u32[]{:S(2)}, u32[]{:S(2)}) %collective-permute-start.21) | collective-permute-done | bytes 110624 | tf_op jit(solution)/shard_map/ppermute | solution.py:510
  (281 shorter events, 182.3 us)
Async XLA Ops:
  7.2 129.8 %all-gather.3.cloned.1.call-start = ((), (), s32[]{:S(2)}) async-start(), calls=%async_computation.1 | async-start | bytes 14800896 | tf_op jit(solution)/shard_map/all_gather | solution.py:601
  15.9 209.4 %all-gather.5.cloned.1.call-start = ((), (), s32[]{:S(2)}) async-start(), calls=%async_computation.2 | async-start | bytes 10948608 | tf_op jit(solution)/shard_map/all_gather | solution.py:602
  16.6 618.7 %reduce-scatter.2.cloned.1.call-start = ((), (), s32[]{:S(2)}) async-start(), calls=%async_computation.3 | async-start | bytes 14598144 | tf_op jit(solution)/shard_map/reduce_scatter | solution.py:644
  36.1 16.6 %collective-permute-start.7 = (bf16[4,48,1280]{2,1,0:T(8,128)(2,1)}, bf16[4,48,1280]{2,1,0:T(8,128)(2,1)S(1)}, u32[]{:S(2)}, u32[]{:S(2)}) collective-permute-start(bf16[4,48,1280]{2,1,0:T(8,128)(2,1)} %bitcast.15), channel_id=1, source_target_pairs={{0,3},{1,2},{2,1},{3,0},{4,7},{5,6},{6,5},{7,4},{8,11},{9,10},{10,... | collective-permute-start | bytes 1474568 | tf_op jit(solution)/shard_map/ppermute | solution.py:510
  53.5 25.1 %collective-permute-start.8 = (bf16[768,1280]{1,0:T(8,128)(2,1)}, bf16[768,1280]{1,0:T(8,128)(2,1)}, u32[]{:S(2)}, u32[]{:S(2)}) collective-permute-start(bf16[768,1280]{1,0:T(8,128)(2,1)} %bitcast.21.refs_3_.refs_1_), channel_id=1, source_target_pairs={{0,16},{16,0},{1,17},{17,1},{2,18},{18,2},{3,19},{19,3},{4,20},{20... | collective-permute-start | bytes 5898248 | tf_op jit(solution)/shard_map/ppermute | solution.py:506
  407.8 20.7 %collective-permute-start.12 = (bf16[768,1536]{1,0:T(8,128)(2,1)}, bf16[768,1536]{1,0:T(8,128)(2,1)}, u32[]{:S(2)}, u32[]{:S(2)}) collective-permute-start(bf16[768,1536]{1,0:T(8,128)(2,1)} %convolution_convert_fusion.4), channel_id=1, source_target_pairs={{0,16},{16,0},{1,17},{17,1},{2,18},{18,2},{3,19},{19,3},{4,20},{20... | collective-permute-start | bytes 7077896 | tf_op jit(solution)/shard_map/ppermute | solution.py:506
  414.0 20.1 %collective-permute-start.13 = (bf16[768,1536]{1,0:T(8,128)(2,1)}, bf16[768,1536]{1,0:T(8,128)(2,1)}, u32[]{:S(2)}, u32[]{:S(2)}) collective-permute-start(bf16[768,1536]{1,0:T(8,128)(2,1)} %convolution_convert_fusion.3), channel_id=1, source_target_pairs={{0,16},{16,0},{1,17},{17,1},{2,18},{18,2},{3,19},{19,3},{4,20},{20... | collective-permute-start | bytes 7077896 | tf_op jit(solution)/shard_map/ppermute | solution.py:506
  424.2 70.4 %collective-permute-start.11 = (bf16[1024,768]{1,0:T(8,128)(2,1)}, bf16[1024,768]{1,0:T(8,128)(2,1)}, u32[]{:S(2)}, u32[]{:S(2)}) collective-permute-start(bf16[1024,768]{1,0:T(8,128)(2,1)} %broadcast_select_fusion.1), channel_id=1, source_target_pairs={{0,16},{16,0},{1,17},{17,1},{2,18},{18,2},{3,19},{19,3},{4,20},{20... | collective-permute-start | bytes 4718600 | tf_op jit(solution)/shard_map/ppermute | solution.py:506
  486.9 11.9 %collective-permute-start.32 = (f32[2,2,12,12]{2,3,1,0:T(8,128)S(1)}, f32[2,2,12,12]{2,3,1,0:T(8,128)S(1)}, u32[]{:S(2)}, u32[]{:S(2)}) collective-permute-start(f32[2,2,12,12]{2,3,1,0:T(8,128)S(1)} %pad_maximum_fusion.8), channel_id=1, source_target_pairs={{0,1},{1,0},{2,3},{3,2},{4,5},{5,4},{6,7},{7,6},{8,9},{9,8},{10,11... | collective-permute-start | bytes 6920 | tf_op jit(solution)/shard_map/ppermute | solution.py:510
  498.7 12.0 %collective-permute-start.33 = (f32[2,2,12,12]{2,3,1,0:T(8,128)S(1)}, f32[2,2,12,12]{2,3,1,0:T(8,128)S(1)}, u32[]{:S(2)}, u32[]{:S(2)}) collective-permute-start(f32[2,2,12,12]{2,3,1,0:T(8,128)S(1)} %fusion.42), channel_id=1, source_target_pairs={{0,2},{1,3},{2,0},{3,1},{4,6},{5,7},{6,4},{7,5},{8,10},{9,11},{10,... | collective-permute-start | bytes 6920 | tf_op jit(solution)/shard_map/ppermute | solution.py:510
  508.1 35.4 %collective-permute-start.25 = (bf16[4,48,3456]{2,1,0:T(8,128)(2,1)}, bf16[4,48,3456]{2,1,0:T(8,128)(2,1)}, u32[]{:S(2)}, u32[]{:S(2)}) collective-permute-start(bf16[4,48,3456]{2,1,0:T(8,128)(2,1)} %get-tuple-element.175), channel_id=1, source_target_pairs={{0,1},{1,0},{2,3},{3,2},{4,5},{5,4},{6,7},{7,6},{8,9},{9,8},{10,11... | collective-permute-start | bytes 3981320 | tf_op jit(solution)/shard_map/ppermute | solution.py:510
  508.2 72.4 %collective-permute-start.26 = (bf16[4,48,3456]{2,1,0:T(8,128)(2,1)}, bf16[4,48,3456]{2,1,0:T(8,128)(2,1)}, u32[]{:S(2)}, u32[]{:S(2)}) collective-permute-start(bf16[4,48,3456]{2,1,0:T(8,128)(2,1)} %get-tuple-element.177), channel_id=1, source_target_pairs={{0,2},{1,3},{2,0},{3,1},{4,6},{5,7},{6,4},{7,5},{8,10},{9,11},{10,... | collective-permute-start | bytes 3981320 | tf_op jit(solution)/shard_map/ppermute | solution.py:510
  508.9 71.7 %collective-permute-start.27 = (bf16[4,48,3456]{2,1,0:T(8,128)(2,1)}, bf16[4,48,3456]{2,1,0:T(8,128)(2,1)}, u32[]{:S(2)}, u32[]{:S(2)}) collective-permute-start(bf16[4,48,3456]{2,1,0:T(8,128)(2,1)} %get-tuple-element.176), channel_id=1, source_target_pairs={{0,3},{1,2},{2,1},{3,0},{4,7},{5,6},{6,5},{7,4},{8,11},{9,10},{10,... | collective-permute-start | bytes 3981320 | tf_op jit(solution)/shard_map/ppermute | solution.py:510
  514.3 77.3 %collective-permute-start.16 = (bf16[768,1152]{1,0:T(8,128)(2,1)}, bf16[768,1152]{1,0:T(8,128)(2,1)}, u32[]{:S(2)}, u32[]{:S(2)}) collective-permute-start(bf16[768,1152]{1,0:T(8,128)(2,1)} %convolution_convert_fusion.5), channel_id=1, source_target_pairs={{0,16},{16,0},{1,17},{17,1},{2,18},{18,2},{3,19},{19,3},{4,20},{20... | collective-permute-start | bytes 5308424 | tf_op jit(solution)/shard_map/ppermute | solution.py:506
  515.4 11.4 %collective-permute-start.35 = (f32[2,2,12,12]{2,3,1,0:T(8,128)S(1)}, f32[2,2,12,12]{2,3,1,0:T(8,128)S(1)}, u32[]{:S(2)}, u32[]{:S(2)}) collective-permute-start(f32[2,2,12,12]{2,3,1,0:T(8,128)S(1)} %add.198), channel_id=1, source_target_pairs={{0,8},{1,9},{2,10},{3,11},{4,12},{5,13},{6,14},{7,15},{8,0},{9,1},... | collective-permute-start | bytes 6920 | tf_op jit(solution)/shard_map/ppermute | solution.py:510
  530.6 57.1 %collective-permute-start.15 = (bf16[1024,768]{1,0:T(8,128)(2,1)}, bf16[1024,768]{1,0:T(8,128)(2,1)}, u32[]{:S(2)}, u32[]{:S(2)}) collective-permute-start(bf16[1024,768]{1,0:T(8,128)(2,1)} %broadcast_select_fusion), channel_id=1, source_target_pairs={{0,16},{16,0},{1,17},{17,1},{2,18},{18,2},{3,19},{19,3},{4,20},{20... | collective-permute-start | bytes 4718600 | tf_op jit(solution)/shard_map/ppermute | solution.py:506
  584.1 16.1 %collective-permute-start.28 = (bf16[1,48,3456]{2,1,0:T(8,128)(2,1)S(1)}, bf16[1,48,3456]{2,1,0:T(8,128)(2,1)S(1)}, u32[]{:S(2)}, u32[]{:S(2)}) collective-permute-start(bf16[1,48,3456]{2,1,0:T(8,128)(2,1)S(1)} %get-tuple-element.184), channel_id=1, source_target_pairs={{0,4},{1,5},{2,6},{3,7},{4,0},{5,1},{6,2},{7,3},{8,12},{9,13},{10,... | collective-permute-start | bytes 995336 | tf_op jit(solution)/shard_map/ppermute | solution.py:510
  584.2 17.5 %collective-permute-start.29 = (bf16[1,48,3456]{2,1,0:T(8,128)(2,1)S(1)}, bf16[1,48,3456]{2,1,0:T(8,128)(2,1)S(1)}, u32[]{:S(2)}, u32[]{:S(2)}) collective-permute-start(bf16[1,48,3456]{2,1,0:T(8,128)(2,1)S(1)} %get-tuple-element.186), channel_id=1, source_target_pairs={{0,8},{1,9},{2,10},{3,11},{4,12},{5,13},{6,14},{7,15},{8,0},{9,1},... | collective-permute-start | bytes 995336 | tf_op jit(solution)/shard_map/ppermute | solution.py:510
  587.7 21.2 %collective-permute-start.30 = (bf16[1,48,3456]{2,1,0:T(8,128)(2,1)S(1)}, bf16[1,48,3456]{2,1,0:T(8,128)(2,1)S(1)}, u32[]{:S(2)}, u32[]{:S(2)}) collective-permute-start(bf16[1,48,3456]{2,1,0:T(8,128)(2,1)S(1)} %get-tuple-element.185), channel_id=1, source_target_pairs={{0,12},{1,13},{2,14},{3,15},{4,8},{5,9},{6,10},{7,11},{8,4},{9,5},... | collective-permute-start | bytes 995336 | tf_op jit(solution)/shard_map/ppermute | solution.py:510
  595.5 17.7 %collective-permute-start.17 = (bf16[4,48,1152]{2,1,0:T(8,128)(2,1)S(1)}, bf16[4,48,1152]{2,1,0:T(8,128)(2,1)S(1)}, u32[]{:S(2)}, u32[]{:S(2)}) collective-permute-start(bf16[4,48,1152]{2,1,0:T(8,128)(2,1)S(1)} %get-tuple-element.181), channel_id=1, source_target_pairs={{0,1},{1,0},{2,3},{3,2},{4,5},{5,4},{6,7},{7,6},{8,9},{9,8},{10,11... | collective-permute-start | bytes 1327112 | tf_op jit(solution)/shard_map/ppermute | solution.py:510
  597.0 16.3 %collective-permute-start.18 = (bf16[4,48,1152]{2,1,0:T(8,128)(2,1)S(1)}, bf16[4,48,1152]{2,1,0:T(8,128)(2,1)S(1)}, u32[]{:S(2)}, u32[]{:S(2)}) collective-permute-start(bf16[4,48,1152]{2,1,0:T(8,128)(2,1)S(1)} %get-tuple-element.183), channel_id=1, source_target_pairs={{0,2},{1,3},{2,0},{3,1},{4,6},{5,7},{6,4},{7,5},{8,10},{9,11},{10,... | collective-permute-start | bytes 1327112 | tf_op jit(solution)/shard_map/ppermute | solution.py:510
  600.2 15.5 %collective-permute-start.19 = (bf16[4,48,1152]{2,1,0:T(8,128)(2,1)S(1)}, bf16[4,48,1152]{2,1,0:T(8,128)(2,1)S(1)}, u32[]{:S(2)}, u32[]{:S(2)}) collective-permute-start(bf16[4,48,1152]{2,1,0:T(8,128)(2,1)S(1)} %get-tuple-element.182), channel_id=1, source_target_pairs={{0,3},{1,2},{2,1},{3,0},{4,7},{5,6},{6,5},{7,4},{8,11},{9,10},{10,... | collective-permute-start | bytes 1327112 | tf_op jit(solution)/shard_map/ppermute | solution.py:510
  609.1 26.2 %collective-permute-start.31 = (f32[48,3456]{1,0:T(8,128)S(1)}, f32[48,3456]{1,0:T(8,128)S(1)}, u32[]{:S(2)}, u32[]{:S(2)}) collective-permute-start(f32[48,3456]{1,0:T(8,128)S(1)} %add_bitcast_fusion), channel_id=1, source_target_pairs={{16,0},{17,1},{18,2},{19,3},{20,4},{21,5},{22,6},{23,7},{24,8},{25... | collective-permute-start | bytes 1990664 | tf_op jit(solution)/shard_map/ppermute | solution.py:663
  632.0 11.6 %collective-permute-start.23 = (f32[48,1152]{1,0:T(8,128)}, f32[48,1152]{1,0:T(8,128)}, u32[]{:S(2)}, u32[]{:S(2)}) collective-permute-start(f32[48,1152]{1,0:T(8,128)} %add_bitcast_fusion.1), channel_id=1, source_target_pairs={{16,0},{17,1},{18,2},{19,3},{20,4},{21,5},{22,6},{23,7},{24,8},{25... | collective-permute-start | bytes 663560 | tf_op jit(solution)/shard_map/ppermute | solution.py:664
  (61 other events, 563.5 us)
Sparse Core Ops, SparseCore 0:
  16.0 120.9 all-gather.2
  139.9 85.3 all-gather.4
  379.5 207.8 reduce-scatter.1

commit v3 on v2

--- a/solution.py
+++ b/solution.py
@@ -324,7 +324,7 @@
         out_shape=[jax.ShapeDtypeStruct((length, 3 * width), BF), sums, sums],
         compiler_params=params(),
         cost_estimate=pl.CostEstimate(
-            flops=8 * length * most * width * heads, bytes_accessed=50 << 20, transcendentals=0
+            flops=length * most * width * heads, bytes_accessed=8 << 20, transcendentals=0
         ),
         name="attend_back",
     )(start, mw, ml, mlx, mwx, q, qt, do, dot_, kt, v, soft, mixed)
@@ -333,48 +333,66 @@
 def gelu_both(b):
     root = math.sqrt(2.0 / math.pi)
     square = b * b
-    t = jnp.tanh(root * (b + 0.044715 * (square * b)))
-    half = 0.5 * (1.0 + t)
-    slope = half + 0.5 * b * (1.0 - t * t) * (root * (1.0 + 3.0 * 0.044715 * square))
-    return b * half, slope
-
-
-def feed_kernel(x_ref, o_ref, gain_ref, wo_ref, wi_ref, wb_ref, y_ref, middle_ref, normed_ref, slope_ref, hidden_ref):
-    middle = x_ref[...].astype(F32) + dot_t(o_ref[...], wo_ref[...])
-    middle_ref[...] = middle
-    scale = lax.rsqrt(jnp.mean(middle * middle, axis=-1, keepdims=True) + EPS)
-    normed = (middle * scale * gain_ref[...]).astype(BF)
-    normed_ref[...] = normed
-    wide = wi_ref.shape[1]
-    part = wide // 4
-    for c in range(4):
-        own = slice(c * part, (c + 1) * part)
-        hidden, slope = gelu_both(dot(normed, wi_ref[:, own]))
-        hidden_ref[:, own] = hidden.astype(BF)
-        slope_ref[:, own] = slope.astype(BF)
-    y_ref[...] = (middle + dot_t(hidden_ref[...], wb_ref[...])).astype(BF)
+    t = jnp.tanh(b * (root + (root * 0.044715) * square))
+    half = 0.5 * t + 0.5
+    value = b * half
+    return value, half + (value * (1.0 - t)) * (root + (3.0 * root * 0.044715) * square)
+
+
+FFB = 512
+
+
+def feed_kernel(
+    x_ref, o_ref, gain_ref, wo_ref, wi_ref, wb_ref, y_ref, middle_ref, normed_ref, slope_ref, hidden_ref, total
+):
+    blocks = [slice(r, r + ROWB) for r in range(0, x_ref.shape[0], ROWB)]
+
+    @pl.when(pl.program_id(0) == 0)
+    def _():
+        for own in blocks:
+            middle = x_ref[own, :].astype(F32) + dot_t(o_ref[own, :], wo_ref[...])
+            middle_ref[own, :] = middle
+            total[own, :] = middle
+            scale = lax.rsqrt(jnp.mean(middle * middle, axis=-1, keepdims=True) + EPS)
+            normed_ref[own, :] = (middle * scale * gain_ref[...]).astype(BF)
+
+    before = dot(normed_ref[blocks[0], :], wi_ref[...])
+    for n, own in enumerate(blocks):
+        following = dot(normed_ref[blocks[n + 1], :], wi_ref[...]) if n + 1 < len(blocks) else None
+        hidden, slope = gelu_both(before)
+        hidden = hidden.astype(BF)
+        hidden_ref[own, :] = hidden
+        slope_ref[own, :] = slope.astype(BF)
+        total[own, :] += dot_t(hidden, wb_ref[...])
+        before = following
+
+    @pl.when(pl.program_id(0) == pl.num_programs(0) - 1)
+    def _():
+        y_ref[...] = total[...].astype(BF)
 
 
 def feed(x, o, gain, w, place_out, place_in, place_back):
     length, width = x.shape
     wide = 4 * width
-    rows = pl.BlockSpec((ROWB, width), lambda i: (i, 0))
-    rows_wide = pl.BlockSpec((ROWB, wide), lambda i: (i, 0))
+    steps = wide // FFB
+    chunk = pl.BlockSpec((length, FFB), lambda i: (0, i))
     flat = jax.ShapeDtypeStruct((length, width), BF)
     flat_wide = jax.ShapeDtypeStruct((length, wide), BF)
+    all_rows = whole((length, width))
     return pl.pallas_call(
         feed_kernel,
-        grid=(length // ROWB,),
+        grid=(steps,),
         in_specs=[
-            rows,
-            rows,
+            all_rows,
+            all_rows,
             whole((1, width)),
             column((width, width), place_out),
-            column((width, wide), place_in),
-            column((width, wide), place_back),
+            pl.BlockSpec((width, FFB), lambda i: (0, place_in * steps + i)),
+            pl.BlockSpec((width, FFB), lambda i: (0, place_back * steps + i)),
         ],
-        out_specs=[rows, rows, rows, rows_wide, rows_wide],
+        out_specs=[all_rows, all_rows, all_rows, chunk, chunk],
         out_shape=[flat, jax.ShapeDtypeStruct((length, width), F32), flat, flat_wide, flat_wide],
+        scratch_shapes=[pltpu.VMEM((length, width), F32)],
         compiler_params=params(),
         cost_estimate=pl.CostEstimate(
             flops=18 * length * width * width, bytes_accessed=30 << 20, transcendentals=length * wide
@@ -391,43 +409,54 @@
 
 
 def feed_back_kernel(
-    dy_ref, slope_ref, middle_ref, gain_ref, wo_ref, wi_ref, wb_ref, gf_ref, dmiddle_ref, ga_ref, do_ref, dot_ref
+    dy_ref, slope_ref, middle_ref, gain_ref, wo_ref, wi_ref, wb_ref, gf_ref, dmiddle_ref, ga_ref, do_ref, dot_ref, total
 ):
-    dy = dy_ref[...]
-    wide = wi_ref.shape[1]
-    part = wide // 4
-    for c in range(4):
-        own = slice(c * part, (c + 1) * part)
-        gf_ref[:, own] = (dot(dy, wb_ref[:, own]) * slope_ref[:, own].astype(F32)).astype(BF)
-    dnormed = dot_t(gf_ref[...], wi_ref[...])
-    dmiddle = dy.astype(F32) + norm_back(middle_ref[...], gain_ref[...], dnormed)
-    dmiddle_ref[...] = dmiddle
-    ga = dmiddle.astype(BF)
-    ga_ref[...] = ga
-    do = dot(ga, wo_ref[...])
-    do_ref[...] = do.astype(BF)
-    dot_ref[...] = do.T.astype(BF)
+    blocks = [slice(r, r + ROWB) for r in range(0, dy_ref.shape[0], ROWB)]
+
+    @pl.when(pl.program_id(0) == 0)
+    def _():
+        total[...] = jnp.zeros_like(total)
+
+    before = dot(dy_ref[blocks[0], :], wb_ref[...])
+    for n, own in enumerate(blocks):
+        following = dot(dy_ref[blocks[n + 1], :], wb_ref[...]) if n + 1 < len(blocks) else None
+        gf = (before * slope_ref[own, :].astype(F32)).astype(BF)
+        gf_ref[own, :] = gf
+        total[own, :] += dot_t(gf, wi_ref[...])
+        before = following
+
+    @pl.when(pl.program_id(0) == pl.num_programs(0) - 1)
+    def _():
+        for own in blocks:
+            dmiddle = dy_ref[own, :].astype(F32) + norm_back(middle_ref[own, :], gain_ref[...], total[own, :])
+            dmiddle_ref[own, :] = dmiddle
+            ga = dmiddle.astype(BF)
+            ga_ref[own, :] = ga
+            do = dot(ga, wo_ref[...])
+            do_ref[own, :] = do.astype(BF)
+            dot_ref[:, own] = do.T.astype(BF)
 
 
 def feed_back(dy, slope, middle, gain, w, place_out, place_in, place_back):
     length, width = dy.shape
     wide = 4 * width
-    rows = pl.BlockSpec((ROWB, width), lambda i: (i, 0))
-    rows_wide = pl.BlockSpec((ROWB, wide), lambda i: (i, 0))
+    steps = wide // FFB
+    chunk = pl.BlockSpec((length, FFB), lambda i: (0, i))
+    all_rows = whole((length, width))
     flat = jax.ShapeDtypeStruct((length, width), BF)
     return pl.pallas_call(
         feed_back_kernel,
-        grid=(length // ROWB,),
+        grid=(steps,),
         in_specs=[
-            rows,
-            rows_wide,
-            rows,
+            all_rows,
+            chunk,
+            all_rows,
             whole((1, width)),
             column((width, width), place_out),
-            column((width, wide), place_in),
-            column((width, wide), place_back),
+            pl.BlockSpec((width, FFB), lambda i: (0, place_in * steps + i)),
+            pl.BlockSpec((width, FFB), lambda i: (0, place_back * steps + i)),
         ],
-        out_specs=[rows_wide, rows, rows, rows, pl.BlockSpec((width, ROWB), lambda i: (0, i))],
+        out_specs=[chunk, all_rows, all_rows, all_rows, whole((width, length))],
         out_shape=[
             jax.ShapeDtypeStruct((length, wide), BF),
             jax.ShapeDtypeStruct((length, width), F32),
@@ -435,6 +464,7 @@
             flat,
             jax.ShapeDtypeStruct((width, length), BF),
         ],
+        scratch_shapes=[pltpu.VMEM((length, width), F32)],
         compiler_params=params(),
         cost_estimate=pl.CostEstimate(flops=18 * length * width * width, bytes_accessed=40 << 20, transcendentals=0),
         name="feed_back",
@@ -473,8 +503,55 @@
     )(dqkv, x, dmiddle, gain, *operands)
 
 
-def weight_grad(left, right):
-    return lax.dot_general(left, right, (((0,), (0,)), ((), ())), preferred_element_type=F32)
+def grads_kernel(jobs, tiled, half_ref, *refs):
+    out_ref = refs[-1]
+    step = pl.program_id(0)
+    first, at = 0, 0
+    for n, (columns, tiles) in enumerate(jobs):
+        left, right = refs[2 * n], refs[2 * n + 1]
+
+        def body(left=left, right=right, first=first, at=at, columns=columns):
+            grad = lax.dot_general(
+                left[...], right[...], (((0,), (0,)), ((), ())), preferred_element_type=F32
+            ).astype(BF)
+            if tiled:
+                out_ref[...] = grad
+            else:
+                place = pl.multiple_of(at + (step - first) * columns, 128)
+                out_ref[:, pl.ds(place, columns)] = grad
+
+        pl.when((step >= first) & (step < first + tiles))(body)
+        first += tiles
+        at += columns * tiles
+
+
+def packed_grads(jobs, half, name):
+    length, width = jobs[0][0].shape
+    total = sum(columns * tiles for _, _, columns, tiles in jobs)
+    steps = sum(tiles for _, _, _, tiles in jobs)
+    tiled = len({columns for _, _, columns, _ in jobs}) == 1
+    specs, operands, first = [], [], 0
+    for left, right, columns, tiles in jobs:
+        specs.append(whole((length, width)))
+        specs.append(
+            pl.BlockSpec(
+                (length, columns),
+                lambda i, h, first=first, tiles=tiles: (0, h[0] * tiles + jnp.clip(i - first, 0, tiles - 1)),
+            )
+        )
+        operands += [left, right]
+        first += tiles
+    out_spec = pl.BlockSpec((width, jobs[0][2]), lambda i, h: (0, i)) if tiled else whole((width, total))
+    return pl.pallas_call(
+        functools.partial(grads_kernel, [(columns, tiles) for _, _, columns, tiles in jobs], tiled),
+        grid_spec=pltpu.PrefetchScalarGridSpec(num_scalar_prefetch=1, grid=(steps,), in_specs=specs, out_specs=out_spec),
+        out_shape=jax.ShapeDtypeStruct((width, total), BF),
+        compiler_params=params(),
+        cost_estimate=pl.CostEstimate(
+            flops=2 * length * width * total, bytes_accessed=2 * (length + width) * (total + width), transcendentals=0
+        ),
+        name=name,
+    )(half, *operands)
 
 
 def mix_tables(mix_logits, mix_weights, size):
@@ -515,41 +592,51 @@
     return [(at, 1 << min(2, bits - at)) for at in range(0, bits, 2)]
 
 
-def gather_rows(own):
+def gather_rows(own, meanwhile):
     share, columns = own.shape
     place = lax.axis_index("dp")
     done = own[None]
-    for shift, members in reversed(bit_groups()):
+    for n, (shift, members) in enumerate(reversed(bit_groups())):
+        if n == 1:
+            done, meanwhile = lax.optimization_barrier((done, meanwhile))
         me = (place >> shift) & (members - 1)
         out = jnp.zeros((done.shape[0], members, share, columns), own.dtype)
         for other in range(members):
             piece = done if other == 0 else partners(done, other << shift)
             out = lax.dynamic_update_slice(out, piece[:, None], (0, me ^ other, 0, 0))
         done = out.reshape(-1, share, columns)
-    return done.reshape(-1, columns)
-
-
-def reduce_rows(whole_rows):
+    return done.reshape(-1, columns), meanwhile
+
+
+def send_parts(held, group):
+    shift, members = group
+    share, columns = held.shape[1:]
+    me = (lax.axis_index("dp") >> shift) & (members - 1)
+    held = held.reshape(-1, members, share, columns)
+    parts = [lax.dynamic_index_in_dim(held, me ^ other, 1, keepdims=False) for other in range(members)]
+    return [parts[0]] + [partners(part.astype(BF), other << shift) for other, part in enumerate(parts) if other]
+
+
+def add_parts(parts):
+    return sum(part.astype(F32) for part in parts)
+
+
+def shares_of(rows):
     size = lax.axis_size("dp")
-    columns = whole_rows.shape[1]
-    share = whole_rows.shape[0] // size
-    place = lax.axis_index("dp")
-    held = whole_rows.reshape(size, share, columns)
-    for shift, members in bit_groups():
-        me = (place >> shift) & (members - 1)
-        held = held.astype(BF).reshape(-1, members, share, columns)
-        total = lax.dynamic_index_in_dim(held, me, 1, keepdims=False).astype(F32)
-        for other in range(1, members):
-            piece = lax.dynamic_index_in_dim(held, me ^ other, 1, keepdims=False)
-            total = total + partners(piece, other << shift).astype(F32)
-        held = total
-    return held.reshape(share, columns)
-
-
-def sum_everywhere(x):
-    for bit in range(lax.axis_size("dp").bit_length() - 1):
-        x = x + partners(x, 1 << bit)
-    return x + swap(x)
+    return rows.reshape(size, rows.shape[0] // size, rows.shape[1])
+
+
+def finish_sum(parts, groups):
+    total = add_parts(parts)
+    for group in groups:
+        total = add_parts(send_parts(total, group))
+    return total[0]
+
+
+def sum_masks(x, masks):
+    for mask in masks:
+        x = x + partners(x, mask)
+    return x
 
 
 def on_device(
@@ -587,7 +674,7 @@
     low = jnp.concatenate([qkv[:, :middle], gain_columns], 1)
     high = jnp.concatenate([qkv[:, middle:], gain_columns], 1)
     from_first = swap(high)
-    own_half = gather_rows(jnp.where(first, low, from_first))
+    own_half, (x0, seg, cot) = gather_rows(jnp.where(first, low, from_first), (x0, seg, cot))
     other_half = swap(own_half)
 
     late = jnp.concatenate([w_in[0].astype(BF), w_back[0].T.astype(BF), w_out[0].T.astype(BF)], 1)
@@ -628,41 +715,80 @@
     def back_attend(do, dot_, kept, table):
         _, _, q, qt, kt, v, _, soft, mixed = kept[:9]
         mix, _, plain, wide_logits, wide_weights = table
-        dqkv, gml, gmw = attend_back(
-            seg[0], mix, plain, wide_logits, wide_weights, q, qt, do, dot_, kt, v, soft, mixed
-        )
-        return dqkv, jnp.stack([jnp.sum(gml, axis=(2, 3)).T * size ** (-0.5), jnp.sum(gmw, axis=(2, 3))])
+        return attend_back(seg[0], mix, plain, wide_logits, wide_weights, q, qt, do, dot_, kt, v, soft, mixed)
+
+    def mix_sums(gml, gmw):
+        return jnp.stack([jnp.sum(gml, axis=(2, 3)).T * size ** (-0.5), jnp.sum(gmw, axis=(2, 3))])
+
+    groups = bit_groups()
+    masks = [1 << bit for bit in range(lax.axis_size("dp").bit_length() - 1)]
+    barrier = lax.optimization_barrier
+    here = section.astype(jnp.int32).reshape(1)
+    away = 1 - here
+
+    def outputs(own0, own1):
+        other = swap(jnp.where(first, own1, own0))
+        return jnp.where(first, jnp.stack([own0, other]), jnp.stack([other, own1]))[None]
+
+    def both_halves(jobs, name):
+        arrived = swap(packed_grads(jobs, away, name + "_away"))
+        return packed_grads(jobs, here, name + "_here"), arrived
+
+    def added(halves):
+        return shares_of(halves[0].astype(F32) + halves[1].astype(F32))
+
+    def projection_jobs(normed, dqkv):
+        return [(normed, dqkv, dqkv.shape[1] // 6, 3)]
 
     gf, dmiddle, ga, do, dot_ = back_feed(cot, kept1, weights1)
-    grads1 = [weight_grad(cot, kept1[12]), weight_grad(kept1[10], gf), weight_grad(ga, kept1[6])]
-    grads1 = [grads1[1], grads1[0], grads1[2]]
-    dqkv, mix_sums1 = back_attend(do, dot_, kept1, tables[1])
-    grads1.append(weight_grad(kept1[1], dqkv))
-    packed1 = jnp.concatenate([g.astype(BF) for g in grads1], 1)
+    packed1 = packed_grads(
+        [(kept1[10], gf, width, 4), (cot, kept1[12], width, 4), (ga, kept1[6], width, 1)],
+        jnp.zeros((1,), jnp.int32),
+        "grads_feed",
+    )
+    do, packed1 = barrier((do, packed1))
+    sums1 = lax.psum_scatter(packed1, AXES, scatter_dimension=0, tiled=True)
+    dqkv, gml1, gmw1 = back_attend(do, dot_, kept1, tables[1])
+    halves = both_halves(projection_jobs(kept1[1], dqkv), "grads_project")
     dx1 = project_back(dqkv, kept1[0], dmiddle, weights1[0][0], qkv1)
-    dx1, packed1 = lax.optimization_barrier((dx1, packed1))
-    sums1 = lax.psum_scatter(packed1, AXES, scatter_dimension=0, tiled=True)
-
-    def shared_grad(left, right):
-        columns = right.shape[1] // 2
-        away = lax.dynamic_slice_in_dim(right, (1 - section) * columns, columns, 1)
-        here = lax.dynamic_slice_in_dim(right, section * columns, columns, 1)
-        arrived = swap(weight_grad(left, away).astype(BF))
-        return (weight_grad(left, here) + arrived.astype(F32)).astype(BF)
-
-    gf, dmiddle, ga, do, dot_ = back_feed(dx1, kept0, weights0)
-    packed0 = jnp.concatenate(
-        [shared_grad(kept0[10], gf), shared_grad(dx1, kept0[12]), shared_grad(ga, kept0[6])], 1
+    dx1, halves = barrier((dx1, halves))
+    parts1 = send_parts(added(halves), groups[0])
+
+    fed, parts1 = barrier((back_feed(dx1, kept0, weights0), parts1))
+    gf, dmiddle, ga, do, dot_ = fed
+    parts1 = send_parts(add_parts(parts1), groups[1])
+    halves = both_halves(
+        [(kept0[10], gf, width, 2), (dx1, kept0[12], width, 2), (ga, kept0[6], width // 2, 1)], "grads_feed"
     )
-    do, packed0 = lax.optimization_barrier((do, packed0))
-    ffn0 = reduce_rows(packed0)
-    dqkv, mix_sums0 = back_attend(do, dot_, kept0, tables[0])
-    proj0 = reduce_rows(shared_grad(kept0[1], dqkv))
+    do, halves, parts1 = barrier((do, halves, parts1))
+    proj1 = finish_sum(parts1, groups[2:])
+    held = added(halves).astype(BF)
+    do, held, proj1 = barrier((do, held, proj1))
+    parts0 = send_parts(held, groups[0])
+    (dqkv, gml0, gmw0), parts0, sums1, gml1, gmw1 = barrier(
+        (back_attend(do, dot_, kept0, tables[0]), parts0, sums1, gml1, gmw1)
+    )
+    held = add_parts(parts0).astype(BF)
+    parts0 = send_parts(held, groups[1])
+    gone = packed_grads(projection_jobs(kept0[1], dqkv), away, "grads_project_away")
+    dqkv, gone, held = barrier((dqkv, gone, held))
+    halves = packed_grads(projection_jobs(kept0[1], dqkv), here, "grads_project_here"), swap(gone)
+    held = added(halves).astype(BF)
+    dqkv, held, mixes, y0, y1, sums1 = barrier((dqkv, held, (gml0, gmw0, gml1, gmw1), y0, y1, sums1))
+    parts = send_parts(held, groups[0])
+    ffn0 = finish_sum(parts0, groups[2:])
     dx0 = project_back(dqkv, kept0[0], dmiddle, weights0[0][0], qkv0)
+    mixes = jnp.stack([mix_sums(*mixes[:2]), mix_sums(*mixes[2:])])
+    mixes = sum_masks(mixes + swap(mixes), masks[:2])
+    section_out = outputs(y0, y1)
+    dx0, parts, mixes, section_out, ffn0, sums1 = barrier((dx0, parts, mixes, section_out, ffn0, sums1))
+    mixes = sum_masks(mixes, masks[2:])
+    mixes = jnp.where(first, mixes[0], mixes[1])
+    proj0 = finish_sum(parts, groups[1:])
 
     ffn0_other = lax.ppermute(ffn0, "section", [(1, 0)])
-    proj0_other = lax.ppermute(proj0, "section", [(1, 0)])
     sums1_other = lax.ppermute(sums1, "section", [(0, 1)])
+    proj_other = swap(jnp.where(first, proj1, proj0))
     sums1 = jnp.concatenate([sums1_other, sums1], 0).astype(F32)
     cuts = (0, wide // 2, wide, wide + width // 2)
 
@@ -671,8 +797,8 @@
 
     grad_in = jnp.where(first, join(0), sums1[:, :wide])
     grad_back = jnp.where(first, join(1), sums1[:, wide : 2 * wide])
-    grad_out = jnp.where(first, join(2), sums1[:, 2 * wide : 2 * wide + width])
-    grad_qkv = jnp.where(first, jnp.concatenate([proj0, proj0_other], 1), sums1[:, 2 * wide + width :])
+    grad_out = jnp.where(first, join(2), sums1[:, 2 * wide :])
+    grad_qkv = jnp.concatenate([jnp.where(first, proj0, proj_other), jnp.where(first, proj_other, proj1)], 1)
 
     def gain_grad(pairs, gain):
         total = sum(jnp.sum(w.astype(BF).astype(F32) * g, axis=1) for w, g in pairs)
@@ -682,15 +808,8 @@
     gg_attn = gain_grad(list(zip((w_query[0], w_key[0], w_value[0]), parts)), gain_attn)
     gg_ffn = gain_grad([(w_in[0], grad_in)], gain_ffn)
 
-    mix_sums = sum_everywhere(jnp.stack([mix_sums0, mix_sums1]))
-    mix_sums = jnp.where(first, mix_sums[0], mix_sums[1])
-
-    def outputs(own0, own1):
-        other = swap(jnp.where(first, own1, own0))
-        return jnp.where(first, jnp.stack([own0, other]), jnp.stack([other, own1]))[None]
-
     return (
-        outputs(y0, y1),
+        section_out,
         outputs(dx0, dx1),
         gg_attn,
         gg_ffn,
@@ -700,8 +819,8 @@
         grad_out.T[None],
         grad_in[None],
         grad_back.T[None],
-        mix_sums[0][None],
-        mix_sums[1][None],
+        mixes[0][None],
+        mixes[1][None],
     )
 
 

time: 658 us -> 629 us (0.956)
  matrix products: 61.7 us -> 0 us
  Pallas kernels: 303 us -> 360 us
  waiting for transfers between devices: 124 us -> 88.1 us
  starting transfers between devices: 69.1 us -> 80.8 us
    dot_general x12 -> x0, matrix products: 61.7 us -> none  [weight_grad(): lax.dot_general(left, right, (((0,), (0,)), ((), ())), preferred_element_...]
    pallas_call x4 -> x11, Pallas kernels: 96.9 us -> 155 us  [the longest x7 68.9 us: packed_grads(): pl.pallas_call(functools.partial(grads_kernel, [(columns, tiles) for _, _...]
    ppermute x22 -> x28, waiting for transfers between devices: 86.4 us -> 47.6 us  [partners(): lax.ppermute(x, 'dp', [(i, i ^ mask) for i in range(lax.axis_size('dp'))])]
    concatenate x2 -> x0, other arithmetic: 13.5 us -> none  [the longest x1 10.7 us: on_device(): packed1 = jnp.concatenate([g.astype(BF) for g in grads1], 1)]
    ppermute x1, starting transfers between devices: 4.17 us -> 13.1 us  [on_device(): ffn0_other = lax.ppermute(ffn0, 'section', [(1, 0)])]
    ppermute x12, starting transfers between devices: 19.6 us -> 28.1 us  [swap(): return lax.ppermute(x, 'section', [(0, 1), (1, 0)])]
    convert_element_type x2 -> x3, other arithmetic: 3.56 us -> 10.9 us  [the longest x2 7.97 us: on_device(): held = added(halves).astype(BF)]
    dynamic_update_slice x7, local copies, waits for them, and re-layouts: 7.39 us -> 0.18 us  [gather_rows(): out = lax.dynamic_update_slice(out, piece[:, None], (0, me ^ other, 0, 0))]
  transfers between devices with their start and end apart: 40 -> 45, of which waited for: 18 -> 16; matrix products, arithmetic and copies ran while one was open for 15% -> 11% of each run, Pallas kernels for 29% -> 47%
where the time goes in v3:
time: 629 us; the launch traced here: 623 us
  Pallas kernels  360 us (57%)
  waiting for transfers between devices  88.1 us (14%)
  starting transfers between devices  80.8 us (13%)
  other arithmetic  51 us (8%)
  local copies, waits for them, and re-layouts  27.5 us (4%)
  between operations  14.8 us (2%)
    pallas_call x2, Pallas kernels, attend_back(): pl.pallas_call(functools.partial(attend_back_kernel, heads), grid_spec=pl...  96.6 us
    pallas_call x2, Pallas kernels, attend(): pl.pallas_call(functools.partial(attend_kernel, heads), grid_spec=pltpu.P...  71.1 us
    pallas_call x7, Pallas kernels, packed_grads(): pl.pallas_call(functools.partial(grads_kernel, [(columns, tiles) for _, _...  68.9 us
    ppermute x28, waiting for transfers between devices, partners(): lax.ppermute(x, 'dp', [(i, i ^ mask) for i in range(lax.axis_size('dp'))])  47.6 us
    pallas_call x2, Pallas kernels, feed(): pl.pallas_call(feed_kernel, grid=(steps,), in_specs=[all_rows, all_rows,...  43.7 us
    pallas_call x2, Pallas kernels, feed_back(): pl.pallas_call(feed_back_kernel, grid=(steps,), in_specs=[all_rows, chunk...  42.3 us
    ppermute x28, starting transfers between devices, partners(): lax.ppermute(x, 'dp', [(i, i ^ mask) for i in range(lax.axis_size('dp'))])  38.2 us
    ppermute x12, starting transfers between devices, swap(): return lax.ppermute(x, 'section', [(0, 1), (1, 0)])  28.1 us
  transfers between devices with their start and end apart: 45, of which 16 were waited for; matrix products, arithmetic and copies ran while one was open for 11% of the time, Pallas kernels for 47%

profile of v3, /device:TPU:1, one launch (start us, length us, event | category | flops | bytes accessed | tf_op | source)
XLA Modules:
  0.0 622.6 jit_solution(8911635543938166950)
XLA Ops:
  25.7 6.1 collective-permute-done.2
  45.8 7.8 %collective-permute-done.7 = bf16[4,48,1280]{2,1,0:T(8,128)(2,1)S(1)} collective-permute-done((bf16[4,48,1280]{2,1,0:T(8,128)(2,1)S(1)}, bf16[4,48,1280]{2,1,0:T(8,128)(2,1)S(1)}, u32[]{:S(2)}, u32[]{:S(2)}) %collective-permute-start.7) | collective-permute-done | bytes 491552 | tf_op jit(solution)/shard_map/ppermute | solution.py:587
  53.7 14.7 %collective-permute-start.8 = (bf16[768,1280]{1,0:T(8,128)(2,1)S(1)}, bf16[768,1280]{1,0:T(8,128)(2,1)}, u32[]{:S(2)}, u32[]{:S(2)}) collective-permute-start(bf16[768,1280]{1,0:T(8,128)(2,1)S(1)} %bitcast.183), channel_id=1, source_target_pairs={{0,16},{16,0},{1,17},{17,1},{2,18},{18,2},{3,19},{19,3},{4,20},{20... | collective-permute-start | bytes 5898248 | tf_op jit(solution)/shard_map/ppermute | solution.py:583
  77.6 9.8 %project.2 = (bf16[1024,768]{1,0:T(8,128)(2,1)}, bf16[1024,768]{1,0:T(8,128)(2,1)}, bf16[768,1024]{1,0:T(8,128)(2,1)}, bf16[1024,768]{1,0:T(8,128)(2,1)}, bf16[7...) custom-call(bf16[1024,768]{1,0:T(8,128)(2,1)} %get-tuple-element.119.refs_0_.x_ref, ...), custom_call_target="tpu_custom_call" | custom-call | flops 3623878656 | bytes 12582912 | tf_op jit(solution)/shard_map/project/pallas_call | solution.py:95
  87.4 41.9 %attend.2 = (bf16[1024,768]{1,0:T(8,128)(2,1)}, bf16[8,6,640,256]{3,2,1,0:T(8,128)(2,1)}, bf16[12,768,1024]{2,1,0:T(8,128)(2,1)}) custom-call(s32[8]{0:T(128)} %convert_reduce_fusion.start_ref, f32[12,12]{1,0:T(8,128)} %get-tuple-element.337.mw_ref, f32[12,12]{1,0:T(8,128)} %get-tuple-element.334.ml_ref, bf16[768,1024]{1,0:T(8,128)(2,1)} %get-tuple-element.122.qt_ref, ...), custom_call_target="tpu_custom_call" | custom-call | flops 24159191040 | bytes 41943040 | tf_op jit(solution)/shard_map/attend/pallas_call | solution.py:163
  129.2 8.9 %all-gather.3.cloned.1.call-done.wo_ref.wi_ref.wb_ref.refs_2_.refs_3_.refs_4_.refs_0_.refs_1_ = bf16[768,9344]{1,0:T(8,128)(2,1)} async-done(((bf16[24,9344]{1,0:T(8,128)(2,1)}), bf16[768,9344]{1,0:T(8,128)(2,1)}) %all-gather.3.cloned.1.call-update) | async-done | bytes 14352400 | tf_op jit(solution)/shard_map/all_gather | solution.py:688
  140.7 21.8 %feed.2 = (bf16[1024,768]{1,0:T(8,128)(2,1)}, f32[1024,768]{1,0:T(8,128)}, bf16[1024,768]{1,0:T(8,128)(2,1)}, bf16[1024,3072]{1,0:T(8,128)(2,1)}, bf16[1024,3072]{1,0:T(8,128)(2,1)}) custom-call(bf16[1024,768]{1,0:T(8,128)(2,1)} %get-tuple-element.119.refs_0_.x_ref, bf16[1024,768]{1,0:T(8,128)(2,1)} %get-tuple-element.127.o_ref.refs_5_, ...), custom_call_target="tpu_custom_call" | custom-call | flops 10871635968 | bytes 31457280 | tf_op jit(solution)/shard_map/feed/pallas_call | solution.py:382
  162.6 8.4 %project.3 = (bf16[1024,768]{1,0:T(8,128)(2,1)}, bf16[1024,768]{1,0:T(8,128)(2,1)}, bf16[768,1024]{1,0:T(8,128)(2,1)}, bf16[1024,768]{1,0:T(8,128)(2,1)}, bf16[7...) custom-call(bf16[1024,768]{1,0:T(8,128)(2,1)} %get-tuple-element.211.refs_0_.x_ref, ...), custom_call_target="tpu_custom_call" | custom-call | flops 3623878656 | bytes 12582912 | tf_op jit(solution)/shard_map/project/pallas_call | solution.py:95
  171.0 29.2 %attend.3 = (bf16[1024,768]{1,0:T(8,128)(2,1)}, bf16[8,6,640,256]{3,2,1,0:T(8,128)(2,1)}, bf16[12,768,1024]{2,1,0:T(8,128)(2,1)}) custom-call(s32[8]{0:T(128)} %convert_reduce_fusion.start_ref, f32[12,12]{1,0:T(8,128)} %copy-done.28, f32[12,12]{1,0:T(8,128)} %get-tuple-element.330.ml_ref, bf16[768,1024]{1,0:T(8,128)(2,1)} %get-tuple-element.130.qt_ref, ...), custom_call_target="tpu_custom_call" | custom-call | flops 24159191040 | bytes 41943040 | tf_op jit(solution)/shard_map/attend/pallas_call | solution.py:163
  200.2 26.2 %all-gather.5.cloned.1.call-done.wo_ref.wi_ref.wb_ref = bf16[768,6912]{1,0:T(8,128)(2,1)} async-done(((bf16[24,6912]{1,0:T(8,128)(2,1)}), bf16[768,6912]{1,0:T(8,128)(2,1)}) %all-gather.5.cloned.1.call-update) | async-done | bytes 10616848 | tf_op jit(solution)/shard_map/all_gather | solution.py:689
  226.5 21.9 %feed.3 = (bf16[1024,768]{1,0:T(8,128)(2,1)}, f32[1024,768]{1,0:T(8,128)}, bf16[1024,768]{1,0:T(8,128)(2,1)}, bf16[1024,3072]{1,0:T(8,128)(2,1)}, bf16[1024,3072]{1,0:T(8,128)(2,1)}) custom-call(bf16[1024,768]{1,0:T(8,128)(2,1)} %get-tuple-element.211.refs_0_.x_ref, bf16[1024,768]{1,0:T(8,128)(2,1)} %get-tuple-element.134.o_ref.refs_5_, ...), custom_call_target="tpu_custom_call" | custom-call | flops 10871635968 | bytes 31457280 | tf_op jit(solution)/shard_map/feed/pallas_call | solution.py:382
  248.3 21.0 %feed_back.2 = (bf16[1024,3072]{1,0:T(8,128)(2,1)}, f32[1024,768]{1,0:T(8,128)}, bf16[1024,768]{1,0:T(8,128)(2,1)}, bf16[1024,768]{1,0:T(8,128)(2,1)}, bf16[768,1024]{1,0:T(8,128)(2,1)}) custom-call(bf16[1024,768]{1,0:T(8,128)(2,1)} %get-tuple-element.131.dy_ref.refs_2_, bf16[1024,3072]{1,0:T(8,128)(2,1)} %get-tuple-element.135.slope_ref, ...), custom_call_target="tpu_custom_call" | custom-call | flops 10871635968 | bytes 41943040 | tf_op jit(solution)/shard_map/feed_back/pallas_call | solution.py:447
  269.4 19.3 %grads_feed.1 = bf16[768,6912]{1,0:T(8,128)(2,1)} custom-call(s32[1]{0:T(128)} %constant.104.clone.1.half_ref, bf16[1024,768]{1,0:T(8,128)(2,1)} %get-tuple-element.138.refs_0_, bf16[1024,3072]{1,0:T(8,128)(2,1)} %get-tuple-element.139.refs_1_, bf16[1024,768]{1,0:T(8,128)(2,1)} %get-tuple-element.131.dy_ref.refs_2_, ...), custom_call_target="tpu_custom_call" | custom-call | flops 10871635968 | bytes 27525120 | tf_op jit(solution)/shard_map/grads_feed/pallas_call | solution.py:545
  288.7 48.5 %attend_back.2 = (bf16[1024,2304]{1,0:T(8,128)(2,1)}, f32[12,12,8,128]{3,2,1,0:T(8,128)}, f32[12,12,8,128]{3,2,1,0:T(8,128)}) custom-call(s32[8]{0:T(128)} %convert_reduce_fusion.start_ref, f32[12,12]{1,0:T(8,128)} %copy-done.28, f32[12,12]{1,0:T(8,128)} %get-tuple-element.332.ml_ref, f32[12,768]{1,0:T(8,128)} %reshape.273.mlx_ref, ...), custom_call_target="tpu_custom_call" | custom-call | flops 6039797760 | bytes 8388608 | tf_op jit(solution)/shard_map/attend_back/pallas_call | solution.py:294
  349.0 9.5 %project_back.2.dy_ref.refs_2_ = bf16[1024,768]{1,0:T(8,128)(2,1)} custom-call(bf16[1024,2304]{1,0:T(8,128)(2,1)} %get-tuple-element.148.dqkv_ref.refs_1_, bf16[1024,768]{1,0:T(8,128)(2,1)} %get-tuple-element.211.refs_0_.x_ref, f32[1024,768]{1,0:T(8,128)} %get-tuple-element.149.dmiddle_ref, f32[1,768]{1,0:T(1,128)} %copy.173.refs_1_.gain_ref, ...), custom_call_target="tpu_custom_call" | custom-call | flops 3623878656 | bytes 18874368 | tf_op jit(solution)/shard_map/project_back/pallas_call | solution.py:494
  367.6 21.3 %feed_back.3 = (bf16[1024,3072]{1,0:T(8,128)(2,1)}, f32[1024,768]{1,0:T(8,128)}, bf16[1024,768]{1,0:T(8,128)(2,1)}, bf16[1024,768]{1,0:T(8,128)(2,1)}, bf16[768,1024]{1,0:T(8,128)(2,1)}) custom-call(bf16[1024,768]{1,0:T(8,128)(2,1)} %project_back.2.dy_ref.refs_2_, bf16[1024,3072]{1,0:T(8,128)(2,1)} %get-tuple-element.152.slope_ref, ...), custom_call_target="tpu_custom_call" | custom-call | flops 10871635968 | bytes 41943040 | tf_op jit(solution)/shard_map/feed_back/pallas_call | solution.py:447
  389.8 6.3 %collective-permute-done.14 = bf16[4,48,1152]{2,1,0:T(8,128)(2,1)} collective-permute-done((bf16[4,48,1152]{2,1,0:T(8,128)(2,1)}, bf16[4,48,1152]{2,1,0:T(8,128)(2,1)}, u32[]{:S(2)}, u32[]{:S(2)}) %collective-permute-start.14) | collective-permute-done | bytes 442400 | tf_op jit(solution)/shard_map/ppermute | solution.py:587
  396.1 13.0 %grads_feed_away.1 = bf16[768,3456]{1,0:T(8,128)(2,1)} custom-call(s32[1]{0:T(128)S(6)} %sub.3.half_ref, bf16[1024,768]{1,0:T(8,128)(2,1)} %get-tuple-element.162.refs_0_, bf16[1024,3072]{1,0:T(8,128)(2,1)} %get-tuple-element.163.refs_1_, bf16[1024,768]{1,0:T(8,128)(2,1)} %project_back.2.dy_ref.refs_2_, bf16[1024,3072]{1,0:T(8,128)(2,1)} %get-tuple-element.164.refs_3_, ...), custom_call_target="tpu_custom_call" | custom-call | flops 5435817984 | bytes 15138816 | tf_op jit(solution)/shard_map/grads_feed_away/pallas_call | solution.py:545
  414.8 13.0 %grads_feed_here.1 = bf16[768,3456]{1,0:T(8,128)(2,1)} custom-call(s32[1]{0:T(128)} %bitcast.21.refs_2_.half_ref.refs_0_, bf16[1024,768]{1,0:T(8,128)(2,1)} %get-tuple-element.162.refs_0_, bf16[1024,3072]{1,0:T(8,128)(2,1)} %get-tuple-element.163.refs_1_, bf16[1024,768]{1,0:T(8,128)(2,1)} %project_back.2.dy_ref.refs_2_, ...), custom_call_target="tpu_custom_call" | custom-call | flops 5435817984 | bytes 15138816 | tf_op jit(solution)/shard_map/grads_feed_here/pallas_call | solution.py:545
  440.5 48.2 %attend_back.3 = (bf16[1024,2304]{1,0:T(8,128)(2,1)}, f32[12,12,8,128]{3,2,1,0:T(8,128)}, f32[12,12,8,128]{3,2,1,0:T(8,128)}) custom-call(s32[8]{0:T(128)} %convert_reduce_fusion.start_ref, f32[12,12]{1,0:T(8,128)} %get-tuple-element.337.mw_ref, f32[12,12]{1,0:T(8,128)} %get-tuple-element.336.ml_ref, f32[12,768]{1,0:T(8,128)} %reshape.270.mlx_ref, ...), custom_call_target="tpu_custom_call" | custom-call | flops 6039797760 | bytes 8388608 | tf_op jit(solution)/shard_map/attend_back/pallas_call | solution.py:294
  488.7 9.6 %collective-permute-done.21 = bf16[4,48,3456]{2,1,0:T(8,128)(2,1)} collective-permute-done((bf16[4,48,3456]{2,1,0:T(8,128)(2,1)}, bf16[4,48,3456]{2,1,0:T(8,128)(2,1)}, u32[]{:S(2)}, u32[]{:S(2)}) %collective-permute-start.21) | collective-permute-done | bytes 1327136 | tf_op jit(solution)/shard_map/ppermute | solution.py:587
  542.1 9.9 %project_back.3 = bf16[1024,768]{1,0:T(8,128)(2,1)} custom-call(bf16[1024,2304]{1,0:T(8,128)(2,1)} %get-tuple-element.204.refs_1_.dqkv_ref, bf16[1024,768]{1,0:T(8,128)(2,1)} %get-tuple-element.119.refs_0_.x_ref, f32[1024,768]{1,0:T(8,128)} %get-tuple-element.205.dmiddle_ref, f32[1,768]{1,0:T(1,128)} %copy.169.refs_1_.gain_ref, ...), custom_call_target="tpu_custom_call" | custom-call | flops 3623878656 | bytes 18874368 | tf_op jit(solution)/shard_map/project_back/pallas_call | solution.py:494
  556.8 13.1 %collective-permute-start.38 = (f32[48,3456]{1,0:T(8,128)}, f32[48,3456]{1,0:T(8,128)}, u32[]{:S(2)}, u32[]{:S(2)}) collective-permute-start(f32[48,3456]{1,0:T(8,128)} %add_bitcast_fusion), channel_id=1, source_target_pairs={{16,0},{17,1},{18,2},{19,3},{20,4},{21,5},{22,6},{23,7},{24,8},{25... | collective-permute-start | bytes 1990664 | tf_op jit(solution)/shard_map/ppermute | solution.py:789
  571.8 7.7 %collective-permute-start.40 = (f32[2,2,12,12]{2,3,1,0:T(8,128)S(1)}, f32[2,2,12,12]{2,3,1,0:T(8,128)S(1)}, u32[]{:S(2)}, u32[]{:S(2)}) collective-permute-start(f32[2,2,12,12]{2,3,1,0:T(8,128)S(1)} %add.189), channel_id=1, source_target_pairs={{0,4},{1,5},{2,6},{3,7},{4,0},{5,1},{6,2},{7,3},{8,12},{9,13},{10,... | collective-permute-start | bytes 6920 | tf_op jit(solution)/shard_map/ppermute | solution.py:587
  (269 shorter events, 170.6 us)
Async XLA Ops:
  7.2 130.9 %all-gather.3.cloned.1.call-start = ((), (), s32[]{:S(2)}) async-start(), calls=%async_computation.1 | async-start | bytes 14800896 | tf_op jit(solution)/shard_map/all_gather | solution.py:688
  14.6 211.9 %all-gather.5.cloned.1.call-start = ((), (), s32[]{:S(2)}) async-start(), calls=%async_computation.2 | async-start | bytes 10948608 | tf_op jit(solution)/shard_map/all_gather | solution.py:689
  15.4 482.9 %reduce-scatter.2.cloned.1.call-start = ((), (), s32[]{:S(2)}) async-start(), calls=%async_computation.3 | async-start | bytes 10948608 | tf_op jit(solution)/shard_map/reduce_scatter | solution.py:750
  37.5 16.1 %collective-permute-start.7 = (bf16[4,48,1280]{2,1,0:T(8,128)(2,1)S(1)}, bf16[4,48,1280]{2,1,0:T(8,128)(2,1)S(1)}, u32[]{:S(2)}, u32[]{:S(2)}) collective-permute-start(bf16[4,48,1280]{2,1,0:T(8,128)(2,1)S(1)} %constant_dynamic-update-slice_fusion), channel_id=1, source_target_pairs={{0,3},{1,2},{2,1},{3,0},{4,7},{5,6},{6,5},{7,4},{8,11},{9,10},{10,... | collective-permute-start | bytes 1474568 | tf_op jit(solution)/shard_map/ppermute | solution.py:587
  53.7 23.9 %collective-permute-start.8 = (bf16[768,1280]{1,0:T(8,128)(2,1)S(1)}, bf16[768,1280]{1,0:T(8,128)(2,1)}, u32[]{:S(2)}, u32[]{:S(2)}) collective-permute-start(bf16[768,1280]{1,0:T(8,128)(2,1)S(1)} %bitcast.183), channel_id=1, source_target_pairs={{0,16},{16,0},{1,17},{17,1},{2,18},{18,2},{3,19},{19,3},{4,20},{20... | collective-permute-start | bytes 5898248 | tf_op jit(solution)/shard_map/ppermute | solution.py:583
  362.2 27.6 %collective-permute-start.12 = (bf16[4,48,1152]{2,1,0:T(8,128)(2,1)}, bf16[4,48,1152]{2,1,0:T(8,128)(2,1)S(1)}, u32[]{:S(2)}, u32[]{:S(2)}) collective-permute-start(bf16[4,48,1152]{2,1,0:T(8,128)(2,1)} %get-tuple-element.295), channel_id=1, source_target_pairs={{0,1},{1,0},{2,3},{3,2},{4,5},{5,4},{6,7},{7,6},{8,9},{9,8},{10,11... | collective-permute-start | bytes 1327112 | tf_op jit(solution)/shard_map/ppermute | solution.py:587
  366.3 23.5 %collective-permute-start.13 = (bf16[4,48,1152]{2,1,0:T(8,128)(2,1)}, bf16[4,48,1152]{2,1,0:T(8,128)(2,1)}, u32[]{:S(2)}, u32[]{:S(2)}) collective-permute-start(bf16[4,48,1152]{2,1,0:T(8,128)(2,1)} %get-tuple-element.294), channel_id=1, source_target_pairs={{0,2},{1,3},{2,0},{3,1},{4,6},{5,7},{6,4},{7,5},{8,10},{9,11},{10,... | collective-permute-start | bytes 1327112 | tf_op jit(solution)/shard_map/ppermute | solution.py:587
  366.4 29.7 %collective-permute-start.14 = (bf16[4,48,1152]{2,1,0:T(8,128)(2,1)}, bf16[4,48,1152]{2,1,0:T(8,128)(2,1)}, u32[]{:S(2)}, u32[]{:S(2)}) collective-permute-start(bf16[4,48,1152]{2,1,0:T(8,128)(2,1)} %get-tuple-element.293), channel_id=1, source_target_pairs={{0,3},{1,2},{2,1},{3,0},{4,7},{5,6},{6,5},{7,4},{8,11},{9,10},{10,... | collective-permute-start | bytes 1327112 | tf_op jit(solution)/shard_map/ppermute | solution.py:587
  409.1 18.8 %collective-permute-start.15 = (bf16[768,3456]{1,0:T(8,128)(2,1)}, bf16[768,3456]{1,0:T(8,128)(2,1)}, u32[]{:S(2)}, u32[]{:S(2)}) collective-permute-start(bf16[768,3456]{1,0:T(8,128)(2,1)} %grads_feed_away.1), channel_id=1, source_target_pairs={{0,16},{16,0},{1,17},{17,1},{2,18},{18,2},{3,19},{19,3},{4,20},{20... | collective-permute-start | bytes 15925256 | tf_op jit(solution)/shard_map/ppermute | solution.py:583
  411.2 16.7 %collective-permute-start.16 = (bf16[1,48,1152]{2,1,0:T(8,128)(2,1)S(1)}, bf16[1,48,1152]{2,1,0:T(8,128)(2,1)S(1)}, u32[]{:S(2)}, u32[]{:S(2)}) collective-permute-start(bf16[1,48,1152]{2,1,0:T(8,128)(2,1)S(1)} %get-tuple-element.312), channel_id=1, source_target_pairs={{0,4},{1,5},{2,6},{3,7},{4,0},{5,1},{6,2},{7,3},{8,12},{9,13},{10,... | collective-permute-start | bytes 331784 | tf_op jit(solution)/shard_map/ppermute | solution.py:587
  411.3 16.6 %collective-permute-start.17 = (bf16[1,48,1152]{2,1,0:T(8,128)(2,1)S(1)}, bf16[1,48,1152]{2,1,0:T(8,128)(2,1)S(1)}, u32[]{:S(2)}, u32[]{:S(2)}) collective-permute-start(bf16[1,48,1152]{2,1,0:T(8,128)(2,1)S(1)} %get-tuple-element.311), channel_id=1, source_target_pairs={{0,8},{1,9},{2,10},{3,11},{4,12},{5,13},{6,14},{7,15},{8,0},{9,1},... | collective-permute-start | bytes 331784 | tf_op jit(solution)/shard_map/ppermute | solution.py:587
  436.1 52.5 %collective-permute-start.19 = (bf16[4,48,3456]{2,1,0:T(8,128)(2,1)}, bf16[4,48,3456]{2,1,0:T(8,128)(2,1)S(1)}, u32[]{:S(2)}, u32[]{:S(2)}) collective-permute-start(bf16[4,48,3456]{2,1,0:T(8,128)(2,1)} %get-tuple-element.291), channel_id=1, source_target_pairs={{0,1},{1,0},{2,3},{3,2},{4,5},{5,4},{6,7},{7,6},{8,9},{9,8},{10,11... | collective-permute-start | bytes 3981320 | tf_op jit(solution)/shard_map/ppermute | solution.py:587
  436.9 51.8 %collective-permute-start.20 = (bf16[4,48,3456]{2,1,0:T(8,128)(2,1)}, bf16[4,48,3456]{2,1,0:T(8,128)(2,1)}, u32[]{:S(2)}, u32[]{:S(2)}) collective-permute-start(bf16[4,48,3456]{2,1,0:T(8,128)(2,1)} %get-tuple-element.290), channel_id=1, source_target_pairs={{0,2},{1,3},{2,0},{3,1},{4,6},{5,7},{6,4},{7,5},{8,10},{9,11},{10,... | collective-permute-start | bytes 3981320 | tf_op jit(solution)/shard_map/ppermute | solution.py:587
  438.1 60.1 %collective-permute-start.21 = (bf16[4,48,3456]{2,1,0:T(8,128)(2,1)}, bf16[4,48,3456]{2,1,0:T(8,128)(2,1)}, u32[]{:S(2)}, u32[]{:S(2)}) collective-permute-start(bf16[4,48,3456]{2,1,0:T(8,128)(2,1)} %get-tuple-element.289), channel_id=1, source_target_pairs={{0,3},{1,2},{2,1},{3,0},{4,7},{5,6},{6,5},{7,4},{8,11},{9,10},{10,... | collective-permute-start | bytes 3981320 | tf_op jit(solution)/shard_map/ppermute | solution.py:587
  509.7 21.9 %collective-permute-start.30 = (bf16[1,48,3456]{2,1,0:T(8,128)(2,1)}, bf16[1,48,3456]{2,1,0:T(8,128)(2,1)}, u32[]{:S(2)}, u32[]{:S(2)}) collective-permute-start(bf16[1,48,3456]{2,1,0:T(8,128)(2,1)} %get-tuple-element.302), channel_id=1, source_target_pairs={{0,4},{1,5},{2,6},{3,7},{4,0},{5,1},{6,2},{7,3},{8,12},{9,13},{10,... | collective-permute-start | bytes 995336 | tf_op jit(solution)/shard_map/ppermute | solution.py:587
  512.1 19.4 %collective-permute-start.31 = (bf16[1,48,3456]{2,1,0:T(8,128)(2,1)}, bf16[1,48,3456]{2,1,0:T(8,128)(2,1)}, u32[]{:S(2)}, u32[]{:S(2)}) collective-permute-start(bf16[1,48,3456]{2,1,0:T(8,128)(2,1)} %get-tuple-element.304), channel_id=1, source_target_pairs={{0,8},{1,9},{2,10},{3,11},{4,12},{5,13},{6,14},{7,15},{8,0},{9,1},... | collective-permute-start | bytes 995336 | tf_op jit(solution)/shard_map/ppermute | solution.py:587
  512.9 22.5 %collective-permute-start.32 = (bf16[1,48,3456]{2,1,0:T(8,128)(2,1)}, bf16[1,48,3456]{2,1,0:T(8,128)(2,1)}, u32[]{:S(2)}, u32[]{:S(2)}) collective-permute-start(bf16[1,48,3456]{2,1,0:T(8,128)(2,1)} %get-tuple-element.303), channel_id=1, source_target_pairs={{0,12},{1,13},{2,14},{3,15},{4,8},{5,9},{6,10},{7,11},{8,4},{9,5},... | collective-permute-start | bytes 995336 | tf_op jit(solution)/shard_map/ppermute | solution.py:587
  524.3 27.7 %collective-permute-start.29 = (bf16[1024,768]{1,0:T(8,128)(2,1)}, bf16[1024,768]{1,0:T(8,128)(2,1)}, u32[]{:S(2)}, u32[]{:S(2)}) collective-permute-start(bf16[1024,768]{1,0:T(8,128)(2,1)} %broadcast_select_fusion.1), channel_id=1, source_target_pairs={{0,16},{16,0},{1,17},{17,1},{2,18},{18,2},{3,19},{19,3},{4,20},{20... | collective-permute-start | bytes 4718600 | tf_op jit(solution)/shard_map/ppermute | solution.py:583
  539.1 16.8 %collective-permute-start.23 = (bf16[4,48,1152]{2,1,0:T(8,128)(2,1)}, bf16[4,48,1152]{2,1,0:T(8,128)(2,1)}, u32[]{:S(2)}, u32[]{:S(2)}) collective-permute-start(bf16[4,48,1152]{2,1,0:T(8,128)(2,1)} %get-tuple-element.300), channel_id=1, source_target_pairs={{0,1},{1,0},{2,3},{3,2},{4,5},{5,4},{6,7},{7,6},{8,9},{9,8},{10,11... | collective-permute-start | bytes 1327112 | tf_op jit(solution)/shard_map/ppermute | solution.py:587
  540.3 15.6 %collective-permute-start.24 = (bf16[4,48,1152]{2,1,0:T(8,128)(2,1)}, bf16[4,48,1152]{2,1,0:T(8,128)(2,1)}, u32[]{:S(2)}, u32[]{:S(2)}) collective-permute-start(bf16[4,48,1152]{2,1,0:T(8,128)(2,1)} %get-tuple-element.299), channel_id=1, source_target_pairs={{0,2},{1,3},{2,0},{3,1},{4,6},{5,7},{6,4},{7,5},{8,10},{9,11},{10,... | collective-permute-start | bytes 1327112 | tf_op jit(solution)/shard_map/ppermute | solution.py:587
  540.5 16.3 %collective-permute-start.25 = (bf16[4,48,1152]{2,1,0:T(8,128)(2,1)}, bf16[4,48,1152]{2,1,0:T(8,128)(2,1)}, u32[]{:S(2)}, u32[]{:S(2)}) collective-permute-start(bf16[4,48,1152]{2,1,0:T(8,128)(2,1)} %get-tuple-element.298), channel_id=1, source_target_pairs={{0,3},{1,2},{2,1},{3,0},{4,7},{5,6},{6,5},{7,4},{8,11},{9,10},{10,... | collective-permute-start | bytes 1327112 | tf_op jit(solution)/shard_map/ppermute | solution.py:587
  556.8 50.2 %collective-permute-start.38 = (f32[48,3456]{1,0:T(8,128)}, f32[48,3456]{1,0:T(8,128)}, u32[]{:S(2)}, u32[]{:S(2)}) collective-permute-start(f32[48,3456]{1,0:T(8,128)} %add_bitcast_fusion), channel_id=1, source_target_pairs={{16,0},{17,1},{18,2},{19,3},{20,4},{21,5},{22,6},{23,7},{24,8},{25... | collective-permute-start | bytes 1990664 | tf_op jit(solution)/shard_map/ppermute | solution.py:789
  579.6 23.7 %collective-permute-start.39 = (bf16[24,6912]{1,0:T(8,128)(2,1)S(1)}, bf16[24,6912]{1,0:T(8,128)(2,1)}, u32[]{:S(2)}, u32[]{:S(2)}) collective-permute-start(bf16[24,6912]{1,0:T(8,128)(2,1)S(1)} %copy-done.11), channel_id=1, source_target_pairs={{0,16},{1,17},{2,18},{3,19},{4,20},{5,21},{6,22},{7,23},{8,24},{9,... | collective-permute-start | bytes 995336 | tf_op jit(solution)/shard_map/ppermute | solution.py:790
  593.7 20.2 %collective-permute-start.33 = (bf16[1024,768]{1,0:T(8,128)(2,1)}, bf16[1024,768]{1,0:T(8,128)(2,1)S(1)}, u32[]{:S(2)}, u32[]{:S(2)}) collective-permute-start(bf16[1024,768]{1,0:T(8,128)(2,1)} %broadcast_select_fusion), channel_id=1, source_target_pairs={{0,16},{16,0},{1,17},{17,1},{2,18},{18,2},{3,19},{19,3},{4,20},{20... | collective-permute-start | bytes 4718600 | tf_op jit(solution)/shard_map/ppermute | solution.py:583
  (56 other events, 479.7 us)
Sparse Core Ops, SparseCore 0:
  14.7 123.3 all-gather.2
  141.0 85.3 all-gather.4
  288.8 164.3 reduce-scatter.1

commit v4 on v3

--- a/solution.py
+++ b/solution.py
@@ -210,6 +210,7 @@
     a_ref,
     mixed_ref,
     dqkv_ref,
+    sums_ref,
     gml_ref,
     gmw_ref,
     dk_acc,
@@ -281,6 +282,9 @@
     def _():
         dqkv_ref[:, width : 2 * width] = dk_acc[...].astype(BF)
         dqkv_ref[:, 2 * width :] = dv_acc[...].astype(BF)
+        for g in range(heads):
+            sums_ref[0, g] = jnp.sum(gml_ref[g], axis=1)
+            sums_ref[1, g] = jnp.sum(gmw_ref[g], axis=1)
 
 
 def attend_back(start, mw, ml, mlx, mwx, q, qt, do, dot_, kt, v, soft, mixed):
@@ -290,7 +294,7 @@
     most = REACH + QB
     rows = pl.BlockSpec((QB, width), lambda i, s: (i, 0))
     cols = pl.BlockSpec((width, QB), lambda i, s: (0, i))
-    sums = jax.ShapeDtypeStruct((heads, heads, 8, QB), F32)
+    sums = jax.ShapeDtypeStruct((2, heads, heads, QB), F32)
     return pl.pallas_call(
         functools.partial(attend_back_kernel, heads),
         grid_spec=pltpu.PrefetchScalarGridSpec(
@@ -310,8 +314,10 @@
                 pl.BlockSpec((1, heads // 2, most, 2 * QB), lambda i, s: (i, 0, 0, 0)),
                 pl.BlockSpec((heads, width, QB), lambda i, s: (0, 0, i)),
             ],
-            out_specs=[whole((length, 3 * width)), whole(sums.shape), whole(sums.shape)],
+            out_specs=[whole((length, 3 * width)), whole(sums.shape)],
             scratch_shapes=[
+                pltpu.VMEM((heads, heads, 8, QB), F32),
+                pltpu.VMEM((heads, heads, 8, QB), F32),
                 pltpu.VMEM((length, width), F32),
                 pltpu.VMEM((length, width), F32),
                 pltpu.VMEM((width, QB), F32),
@@ -321,7 +327,7 @@
                 pltpu.VMEM((heads * QB, width), BF),
             ],
         ),
-        out_shape=[jax.ShapeDtypeStruct((length, 3 * width), BF), sums, sums],
+        out_shape=[jax.ShapeDtypeStruct((length, 3 * width), BF), sums],
         compiler_params=params(),
         cost_estimate=pl.CostEstimate(
             flops=length * most * width * heads, bytes_accessed=8 << 20, transcendentals=0
@@ -498,7 +504,7 @@
         out_specs=rows,
         out_shape=jax.ShapeDtypeStruct((length, width), BF),
         compiler_params=params(),
-        cost_estimate=pl.CostEstimate(flops=6 * length * width * width, bytes_accessed=18 << 20, transcendentals=0),
+        cost_estimate=pl.CostEstimate(flops=length * width, bytes_accessed=1 << 16, transcendentals=0),
         name="project_back",
     )(dqkv, x, dmiddle, gain, *operands)
 
@@ -717,18 +723,20 @@
         mix, _, plain, wide_logits, wide_weights = table
         return attend_back(seg[0], mix, plain, wide_logits, wide_weights, q, qt, do, dot_, kt, v, soft, mixed)
 
-    def mix_sums(gml, gmw):
-        return jnp.stack([jnp.sum(gml, axis=(2, 3)).T * size ** (-0.5), jnp.sum(gmw, axis=(2, 3))])
-
     groups = bit_groups()
     masks = [1 << bit for bit in range(lax.axis_size("dp").bit_length() - 1)]
     barrier = lax.optimization_barrier
     here = section.astype(jnp.int32).reshape(1)
     away = 1 - here
 
-    def outputs(own0, own1):
-        other = swap(jnp.where(first, own1, own0))
-        return jnp.where(first, jnp.stack([own0, other]), jnp.stack([other, own1]))[None]
+    def outputs(own0, own1, other0, other1):
+        return jnp.where(first, jnp.stack([own0, other0]), jnp.stack([other1, own1]))[None]
+
+    def to_first(x):
+        return lax.ppermute(x, "section", [(1, 0)])
+
+    def to_second(x):
+        return lax.ppermute(x, "section", [(0, 1)])
 
     def both_halves(jobs, name):
         arrived = swap(packed_grads(jobs, away, name + "_away"))
@@ -748,7 +756,7 @@
     )
     do, packed1 = barrier((do, packed1))
     sums1 = lax.psum_scatter(packed1, AXES, scatter_dimension=0, tiled=True)
-    dqkv, gml1, gmw1 = back_attend(do, dot_, kept1, tables[1])
+    dqkv, sums_mix1 = back_attend(do, dot_, kept1, tables[1])
     halves = both_halves(projection_jobs(kept1[1], dqkv), "grads_project")
     dx1 = project_back(dqkv, kept1[0], dmiddle, weights1[0][0], qkv1)
     dx1, halves = barrier((dx1, halves))
@@ -765,26 +773,35 @@
     held = added(halves).astype(BF)
     do, held, proj1 = barrier((do, held, proj1))
     parts0 = send_parts(held, groups[0])
-    (dqkv, gml0, gmw0), parts0, sums1, gml1, gmw1 = barrier(
-        (back_attend(do, dot_, kept0, tables[0]), parts0, sums1, gml1, gmw1)
+    y_other = to_first(y0), to_second(y1)
+    dx1_other = to_second(dx1)
+    (dqkv, sums_mix0), parts0[:2], sums1, y_other, dx1_other = barrier(
+        (back_attend(do, dot_, kept0, tables[0]), parts0[:2], sums1, y_other, dx1_other)
     )
+    mixes = jnp.sum(jnp.stack([sums_mix0, sums_mix1]), axis=4)
+    mixes = sum_masks(mixes + swap(mixes), masks[:2])
+    dqkv, parts0, mixes = barrier((dqkv, parts0, mixes))
     held = add_parts(parts0).astype(BF)
     parts0 = send_parts(held, groups[1])
     gone = packed_grads(projection_jobs(kept0[1], dqkv), away, "grads_project_away")
     dqkv, gone, held = barrier((dqkv, gone, held))
     halves = packed_grads(projection_jobs(kept0[1], dqkv), here, "grads_project_here"), swap(gone)
     held = added(halves).astype(BF)
-    dqkv, held, mixes, y0, y1, sums1 = barrier((dqkv, held, (gml0, gmw0, gml1, gmw1), y0, y1, sums1))
+    dqkv, held = barrier((dqkv, held))
     parts = send_parts(held, groups[0])
+    dx0 = project_back(dqkv, kept0[0], dmiddle, weights0[0][0], qkv0)
+    dx0, y0, y1, y_other, mixes, sums1 = barrier((dx0, y0, y1, y_other, mixes, sums1))
+    section_out = outputs(y0, y1, *y_other)
+    dx0, parts, parts0, section_out, mixes = barrier((dx0, parts, parts0, section_out, mixes))
+    held = add_parts(parts).astype(BF)
+    dx0, held, parts0, mixes, sums1 = barrier((dx0, held, parts0, mixes, sums1))
+    parts = send_parts(held, groups[1])
+    parts[:2], dx0, parts0, mixes, sums1 = barrier((parts[:2], dx0, parts0, mixes, sums1))
+    dx0_other = to_first(dx0)
     ffn0 = finish_sum(parts0, groups[2:])
-    dx0 = project_back(dqkv, kept0[0], dmiddle, weights0[0][0], qkv0)
-    mixes = jnp.stack([mix_sums(*mixes[:2]), mix_sums(*mixes[2:])])
-    mixes = sum_masks(mixes + swap(mixes), masks[:2])
-    section_out = outputs(y0, y1)
-    dx0, parts, mixes, section_out, ffn0, sums1 = barrier((dx0, parts, mixes, section_out, ffn0, sums1))
     mixes = sum_masks(mixes, masks[2:])
     mixes = jnp.where(first, mixes[0], mixes[1])
-    proj0 = finish_sum(parts, groups[1:])
+    proj0 = finish_sum(parts, groups[2:])
 
     ffn0_other = lax.ppermute(ffn0, "section", [(1, 0)])
     sums1_other = lax.ppermute(sums1, "section", [(0, 1)])
@@ -810,7 +827,7 @@
 
     return (
         section_out,
-        outputs(dx0, dx1),
+        outputs(dx0, dx1, dx0_other, dx1_other),
         gg_attn,
         gg_ffn,
         parts[0][None],
@@ -819,7 +836,7 @@
         grad_out.T[None],
         grad_in[None],
         grad_back.T[None],
-        mixes[0][None],
+        mixes[0].T[None] * size ** (-0.5),
         mixes[1][None],
     )
 

time: 629 us -> 622 us (0.989)
  Pallas kernels: 360 us -> 348 us
  starting transfers between devices: 80.8 us -> 91.4 us
    ppermute x28, starting transfers between devices: 38.2 us -> 50.4 us  [partners(): lax.ppermute(x, 'dp', [(i, i ^ mask) for i in range(lax.axis_size('dp'))])]
    pallas_call x2, Pallas kernels: 96.6 us -> 87.8 us  [attend_back(): pl.pallas_call(functools.partial(attend_back_kernel, heads), grid_spec=pl...]
    ppermute x0 -> x4, starting transfers between devices: none -> 8.71 us  [the longest x2 6.13 us: to_first(): return lax.ppermute(x, 'section', [(1, 0)])]
    ppermute x1, starting transfers between devices: 13.1 us -> 4.61 us  [on_device(): ffn0_other = lax.ppermute(ffn0, 'section', [(1, 0)])]
    ppermute x12 -> x10, starting transfers between devices: 28.1 us -> 26.3 us  [swap(): return lax.ppermute(x, 'section', [(0, 1), (1, 0)])]
  transfers between devices with their start and end apart: 45 -> 47, of which waited for: 16 -> 17; matrix products, arithmetic and copies ran while one was open for 11% -> 10% of each run, Pallas kernels for 47% -> 45%
where the time goes in v4:
time: 622 us; the launch traced here: 615 us
  Pallas kernels  348 us (56%)
  starting transfers between devices  91.4 us (15%)
  waiting for transfers between devices  88.3 us (14%)
  other arithmetic  46.1 us (7%)
  local copies, waits for them, and re-layouts  26.7 us (4%)
  between operations  14.7 us (2%)
    pallas_call x2, Pallas kernels, attend_back(): pl.pallas_call(functools.partial(attend_back_kernel, heads), grid_spec=pl...  87.8 us
    pallas_call x7, Pallas kernels, packed_grads(): pl.pallas_call(functools.partial(grads_kernel, [(columns, tiles) for _, _...  69.3 us
    pallas_call x2, Pallas kernels, attend(): pl.pallas_call(functools.partial(attend_kernel, heads), grid_spec=pltpu.P...  66.4 us
    ppermute x28, starting transfers between devices, partners(): lax.ppermute(x, 'dp', [(i, i ^ mask) for i in range(lax.axis_size('dp'))])  50.4 us
    pallas_call x2, Pallas kernels, feed(): pl.pallas_call(feed_kernel, grid=(steps,), in_specs=[all_rows, all_rows,...  43.7 us
    ppermute x28, waiting for transfers between devices, partners(): lax.ppermute(x, 'dp', [(i, i ^ mask) for i in range(lax.axis_size('dp'))])  42.3 us
    pallas_call x2, Pallas kernels, feed_back(): pl.pallas_call(feed_back_kernel, grid=(steps,), in_specs=[all_rows, chunk...  42.3 us
    all_gather x1, waiting for transfers between devices, on_device(): third = lax.all_gather(late1, AXES, axis=0, tiled=True)  28.6 us
  transfers between devices with their start and end apart: 47, of which 17 were waited for; matrix products, arithmetic and copies ran while one was open for 10% of the time, Pallas kernels for 45%

profile of v4, /device:TPU:1, one launch (start us, length us, event | category | flops | bytes accessed | tf_op | source)
XLA Modules:
  0.0 615.2 jit_solution(11844880331479756553)
XLA Ops:
  25.7 6.1 collective-permute-done.2
  45.8 7.9 %collective-permute-done.7 = bf16[4,48,1280]{2,1,0:T(8,128)(2,1)S(1)} collective-permute-done((bf16[4,48,1280]{2,1,0:T(8,128)(2,1)S(1)}, bf16[4,48,1280]{2,1,0:T(8,128)(2,1)S(1)}, u32[]{:S(2)}, u32[]{:S(2)}) %collective-permute-start.7) | collective-permute-done | bytes 491552 | tf_op jit(solution)/shard_map/ppermute | solution.py:593
  53.8 14.8 %collective-permute-start.8 = (bf16[768,1280]{1,0:T(8,128)(2,1)S(1)}, bf16[768,1280]{1,0:T(8,128)(2,1)}, u32[]{:S(2)}, u32[]{:S(2)}) collective-permute-start(bf16[768,1280]{1,0:T(8,128)(2,1)S(1)} %bitcast.176), channel_id=1, source_target_pairs={{0,16},{16,0},{1,17},{17,1},{2,18},{18,2},{3,19},{19,3},{4,20},{20... | collective-permute-start | bytes 5898248 | tf_op jit(solution)/shard_map/ppermute | solution.py:589
  77.7 9.8 %project.2 = (bf16[1024,768]{1,0:T(8,128)(2,1)}, bf16[1024,768]{1,0:T(8,128)(2,1)}, bf16[768,1024]{1,0:T(8,128)(2,1)}, bf16[1024,768]{1,0:T(8,128)(2,1)}, bf16[7...) custom-call(bf16[1024,768]{1,0:T(8,128)(2,1)} %get-tuple-element.140.refs_0_.x_ref, ...), custom_call_target="tpu_custom_call" | custom-call | flops 3623878656 | bytes 12582912 | tf_op jit(solution)/shard_map/project/pallas_call | solution.py:95
  87.5 39.6 %attend.2 = (bf16[1024,768]{1,0:T(8,128)(2,1)}, bf16[8,6,640,256]{3,2,1,0:T(8,128)(2,1)}, bf16[12,768,1024]{2,1,0:T(8,128)(2,1)}) custom-call(s32[8]{0:T(128)} %convert_reduce_fusion.start_ref, f32[12,12]{1,0:T(8,128)} %get-tuple-element.369.mw_ref, f32[12,12]{1,0:T(8,128)} %get-tuple-element.366.ml_ref, bf16[768,1024]{1,0:T(8,128)(2,1)} %get-tuple-element.143.qt_ref, ...), custom_call_target="tpu_custom_call" | custom-call | flops 24159191040 | bytes 41943040 | tf_op jit(solution)/shard_map/attend/pallas_call | solution.py:163
  127.1 11.1 %all-gather.3.cloned.1.call-done.wo_ref.wi_ref.wb_ref.refs_2_.refs_3_.refs_4_.refs_0_.refs_1_ = bf16[768,9344]{1,0:T(8,128)(2,1)} async-done(((bf16[24,9344]{1,0:T(8,128)(2,1)}), bf16[768,9344]{1,0:T(8,128)(2,1)}) %all-gather.3.cloned.1.call-update) | async-done | bytes 14352400 | tf_op jit(solution)/shard_map/all_gather | solution.py:694
  140.8 21.8 %feed.2 = (bf16[1024,768]{1,0:T(8,128)(2,1)}, f32[1024,768]{1,0:T(8,128)}, bf16[1024,768]{1,0:T(8,128)(2,1)}, bf16[1024,3072]{1,0:T(8,128)(2,1)}, bf16[1024,3072]{1,0:T(8,128)(2,1)}) custom-call(bf16[1024,768]{1,0:T(8,128)(2,1)} %get-tuple-element.140.refs_0_.x_ref, bf16[1024,768]{1,0:T(8,128)(2,1)} %get-tuple-element.148.o_ref.refs_5_, ...), custom_call_target="tpu_custom_call" | custom-call | flops 10871635968 | bytes 31457280 | tf_op jit(solution)/shard_map/feed/pallas_call | solution.py:388
  162.6 8.4 %project.3 = (bf16[1024,768]{1,0:T(8,128)(2,1)}, bf16[1024,768]{1,0:T(8,128)(2,1)}, bf16[768,1024]{1,0:T(8,128)(2,1)}, bf16[1024,768]{1,0:T(8,128)(2,1)}, bf16[7...) custom-call(bf16[1024,768]{1,0:T(8,128)(2,1)} %get-tuple-element.230.refs_0_.x_ref, ...), custom_call_target="tpu_custom_call" | custom-call | flops 3623878656 | bytes 12582912 | tf_op jit(solution)/shard_map/project/pallas_call | solution.py:95
  171.0 26.8 %attend.3 = (bf16[1024,768]{1,0:T(8,128)(2,1)}, bf16[8,6,640,256]{3,2,1,0:T(8,128)(2,1)}, bf16[12,768,1024]{2,1,0:T(8,128)(2,1)}) custom-call(s32[8]{0:T(128)} %convert_reduce_fusion.start_ref, f32[12,12]{1,0:T(8,128)} %copy-done.27, f32[12,12]{1,0:T(8,128)} %get-tuple-element.362.ml_ref, bf16[768,1024]{1,0:T(8,128)(2,1)} %get-tuple-element.151.qt_ref, ...), custom_call_target="tpu_custom_call" | custom-call | flops 24159191040 | bytes 41943040 | tf_op jit(solution)/shard_map/attend/pallas_call | solution.py:163
  197.9 28.6 %all-gather.5.cloned.1.call-done.wo_ref.wi_ref.wb_ref = bf16[768,6912]{1,0:T(8,128)(2,1)} async-done(((bf16[24,6912]{1,0:T(8,128)(2,1)}), bf16[768,6912]{1,0:T(8,128)(2,1)}) %all-gather.5.cloned.1.call-update) | async-done | bytes 10616848 | tf_op jit(solution)/shard_map/all_gather | solution.py:695
  226.5 21.9 %feed.3 = (bf16[1024,768]{1,0:T(8,128)(2,1)}, f32[1024,768]{1,0:T(8,128)}, bf16[1024,768]{1,0:T(8,128)(2,1)}, bf16[1024,3072]{1,0:T(8,128)(2,1)}, bf16[1024,3072]{1,0:T(8,128)(2,1)}) custom-call(bf16[1024,768]{1,0:T(8,128)(2,1)} %get-tuple-element.230.refs_0_.x_ref, bf16[1024,768]{1,0:T(8,128)(2,1)} %get-tuple-element.155.o_ref.refs_5_, ...), custom_call_target="tpu_custom_call" | custom-call | flops 10871635968 | bytes 31457280 | tf_op jit(solution)/shard_map/feed/pallas_call | solution.py:388
  248.4 21.0 %feed_back.2 = (bf16[1024,3072]{1,0:T(8,128)(2,1)}, f32[1024,768]{1,0:T(8,128)}, bf16[1024,768]{1,0:T(8,128)(2,1)}, bf16[1024,768]{1,0:T(8,128)(2,1)}, bf16[768,1024]{1,0:T(8,128)(2,1)}) custom-call(bf16[1024,768]{1,0:T(8,128)(2,1)} %get-tuple-element.152.dy_ref.refs_2_, bf16[1024,3072]{1,0:T(8,128)(2,1)} %get-tuple-element.156.slope_ref, ...), custom_call_target="tpu_custom_call" | custom-call | flops 10871635968 | bytes 41943040 | tf_op jit(solution)/shard_map/feed_back/pallas_call | solution.py:453
  269.4 19.3 %grads_feed.1 = bf16[768,6912]{1,0:T(8,128)(2,1)} custom-call(s32[1]{0:T(128)} %constant.107.clone.1.half_ref, bf16[1024,768]{1,0:T(8,128)(2,1)} %get-tuple-element.159.refs_0_, bf16[1024,3072]{1,0:T(8,128)(2,1)} %get-tuple-element.160.refs_1_, bf16[1024,768]{1,0:T(8,128)(2,1)} %get-tuple-element.152.dy_ref.refs_2_, ...), custom_call_target="tpu_custom_call" | custom-call | flops 10871635968 | bytes 27525120 | tf_op jit(solution)/shard_map/grads_feed/pallas_call | solution.py:551
  288.7 43.9 %attend_back.2 = (bf16[1024,2304]{1,0:T(8,128)(2,1)}, f32[2,12,12,128]{3,2,1,0:T(8,128)}) custom-call(s32[8]{0:T(128)} %convert_reduce_fusion.start_ref, f32[12,12]{1,0:T(8,128)} %copy-done.27, f32[12,12]{1,0:T(8,128)} %get-tuple-element.364.ml_ref, f32[12,768]{1,0:T(8,128)} %reshape.269.mlx_ref, f32[12,768]{1,0:T(8,128)} %reshape.270.mwx_ref, ...), custom_call_target="tpu_custom_call" | custom-call | flops 6039797760 | bytes 8388608 | tf_op jit(solution)/shard_map/attend_back/pallas_call | solution.py:298
  338.8 10.4 %project_back.2.dy_ref.refs_2_ = bf16[1024,768]{1,0:T(8,128)(2,1)} custom-call(bf16[1024,2304]{1,0:T(8,128)(2,1)} %get-tuple-element.169.dqkv_ref.refs_1_, bf16[1024,768]{1,0:T(8,128)(2,1)} %get-tuple-element.230.refs_0_.x_ref, f32[1024,768]{1,0:T(8,128)} %get-tuple-element.170.dmiddle_ref, f32[1,768]{1,0:T(1,128)} %copy.137.refs_1_.gain_ref, ...), custom_call_target="tpu_custom_call" | custom-call | flops 786432 | bytes 65536 | tf_op jit(solution)/shard_map/project_back/pallas_call | solution.py:500
  349.2 5.9 grads_project_here.2
  367.3 21.3 %feed_back.3 = (bf16[1024,3072]{1,0:T(8,128)(2,1)}, f32[1024,768]{1,0:T(8,128)}, bf16[1024,768]{1,0:T(8,128)(2,1)}, bf16[1024,768]{1,0:T(8,128)(2,1)}, bf16[768,1024]{1,0:T(8,128)(2,1)}) custom-call(bf16[1024,768]{1,0:T(8,128)(2,1)} %project_back.2.dy_ref.refs_2_, bf16[1024,3072]{1,0:T(8,128)(2,1)} %get-tuple-element.173.slope_ref, ...), custom_call_target="tpu_custom_call" | custom-call | flops 10871635968 | bytes 41943040 | tf_op jit(solution)/shard_map/feed_back/pallas_call | solution.py:453
  395.6 13.1 %grads_feed_away.1 = bf16[768,3456]{1,0:T(8,128)(2,1)} custom-call(s32[1]{0:T(128)S(6)} %sub.3.half_ref, bf16[1024,768]{1,0:T(8,128)(2,1)} %get-tuple-element.183.refs_0_, bf16[1024,3072]{1,0:T(8,128)(2,1)} %get-tuple-element.184.refs_1_, bf16[1024,768]{1,0:T(8,128)(2,1)} %project_back.2.dy_ref.refs_2_, bf16[1024,3072]{1,0:T(8,128)(2,1)} %get-tuple-element.185.refs_3_, ...), custom_call_target="tpu_custom_call" | custom-call | flops 5435817984 | bytes 15138816 | tf_op jit(solution)/shard_map/grads_feed_away/pallas_call | solution.py:551
  417.9 13.2 %grads_feed_here.1 = bf16[768,3456]{1,0:T(8,128)(2,1)} custom-call(s32[1]{0:T(128)} %bitcast.21.refs_2_.half_ref.refs_0_, bf16[1024,768]{1,0:T(8,128)(2,1)} %get-tuple-element.183.refs_0_, bf16[1024,3072]{1,0:T(8,128)(2,1)} %get-tuple-element.184.refs_1_, bf16[1024,768]{1,0:T(8,128)(2,1)} %project_back.2.dy_ref.refs_2_, ...), custom_call_target="tpu_custom_call" | custom-call | flops 5435817984 | bytes 15138816 | tf_op jit(solution)/shard_map/grads_feed_here/pallas_call | solution.py:551
  447.7 43.9 %attend_back.3 = (bf16[1024,2304]{1,0:T(8,128)(2,1)}, f32[2,12,12,128]{3,2,1,0:T(8,128)}) custom-call(s32[8]{0:T(128)} %convert_reduce_fusion.start_ref, f32[12,12]{1,0:T(8,128)} %get-tuple-element.369.mw_ref, f32[12,12]{1,0:T(8,128)} %get-tuple-element.368.ml_ref, f32[12,768]{1,0:T(8,128)} %reshape.266.mlx_ref, f32[12,768]{1,0:T(8,128)} %reshape.267.mwx_ref, ...), custom_call_target="tpu_custom_call" | custom-call | flops 6039797760 | bytes 8388608 | tf_op jit(solution)/shard_map/attend_back/pallas_call | solution.py:298
  520.3 5.9 grads_project_here.3
  536.9 9.8 %project_back.3 = bf16[1024,768]{1,0:T(8,128)(2,1)} custom-call(bf16[1024,2304]{1,0:T(8,128)(2,1)} %get-tuple-element.222.refs_1_.dqkv_ref, bf16[1024,768]{1,0:T(8,128)(2,1)} %get-tuple-element.140.refs_0_.x_ref, f32[1024,768]{1,0:T(8,128)} %get-tuple-element.223.dmiddle_ref, f32[1,768]{1,0:T(1,128)} %copy.133.refs_1_.gain_ref, ...), custom_call_target="tpu_custom_call" | custom-call | flops 786432 | bytes 65536 | tf_op jit(solution)/shard_map/project_back/pallas_call | solution.py:500
  550.5 7.1 %collective-permute-done.33 = bf16[1,48,3456]{2,1,0:T(8,128)(2,1)} collective-permute-done((bf16[1,48,3456]{2,1,0:T(8,128)(2,1)}, bf16[1,48,3456]{2,1,0:T(8,128)(2,1)}, u32[]{:S(2)}, u32[]{:S(2)}) %collective-permute-start.33) | collective-permute-done | bytes 331808 | tf_op jit(solution)/shard_map/ppermute | solution.py:593
  559.2 8.5 %collective-permute-start.35 = (bf16[1,48,1152]{2,1,0:T(8,128)(2,1)S(1)}, bf16[1,48,1152]{2,1,0:T(8,128)(2,1)S(1)}, u32[]{:S(2)}, u32[]{:S(2)}) collective-permute-start(bf16[1,48,1152]{2,1,0:T(8,128)(2,1)S(1)} %get-tuple-element.348), channel_id=1, source_target_pairs={{0,4},{1,5},{2,6},{3,7},{4,0},{5,1},{6,2},{7,3},{8,12},{9,13},{10,... | collective-permute-start | bytes 331784 | tf_op jit(solution)/shard_map/ppermute | solution.py:593
  (259 shorter events, 180.3 us)
Async XLA Ops:
  7.2 131.0 %all-gather.3.cloned.1.call-start = ((), (), s32[]{:S(2)}) async-start(), calls=%async_computation.1 | async-start | bytes 14800896 | tf_op jit(solution)/shard_map/all_gather | solution.py:694
  14.6 211.8 %all-gather.5.cloned.1.call-start = ((), (), s32[]{:S(2)}) async-start(), calls=%async_computation.2 | async-start | bytes 10948608 | tf_op jit(solution)/shard_map/all_gather | solution.py:695
  15.4 476.3 %reduce-scatter.2.cloned.1.call-start = ((), (), s32[]{:S(2)}) async-start(), calls=%async_computation.3 | async-start | bytes 10948608 | tf_op jit(solution)/shard_map/reduce_scatter | solution.py:758
  53.8 23.9 %collective-permute-start.8 = (bf16[768,1280]{1,0:T(8,128)(2,1)S(1)}, bf16[768,1280]{1,0:T(8,128)(2,1)}, u32[]{:S(2)}, u32[]{:S(2)}) collective-permute-start(bf16[768,1280]{1,0:T(8,128)(2,1)S(1)} %bitcast.176), channel_id=1, source_target_pairs={{0,16},{16,0},{1,17},{17,1},{2,18},{18,2},{3,19},{19,3},{4,20},{20... | collective-permute-start | bytes 5898248 | tf_op jit(solution)/shard_map/ppermute | solution.py:589
  338.5 16.6 %collective-permute-start.11 = (bf16[768,1152]{1,0:T(8,128)(2,1)}, bf16[768,1152]{1,0:T(8,128)(2,1)}, u32[]{:S(2)}, u32[]{:S(2)}) collective-permute-start(bf16[768,1152]{1,0:T(8,128)(2,1)} %grads_project_away.2), channel_id=1, source_target_pairs={{0,16},{16,0},{1,17},{17,1},{2,18},{18,2},{3,19},{19,3},{4,20},{20... | collective-permute-start | bytes 5308424 | tf_op jit(solution)/shard_map/ppermute | solution.py:589
  358.6 30.9 %collective-permute-start.12 = (bf16[4,48,1152]{2,1,0:T(8,128)(2,1)}, bf16[4,48,1152]{2,1,0:T(8,128)(2,1)S(1)}, u32[]{:S(2)}, u32[]{:S(2)}) collective-permute-start(bf16[4,48,1152]{2,1,0:T(8,128)(2,1)} %get-tuple-element.325), channel_id=1, source_target_pairs={{0,1},{1,0},{2,3},{3,2},{4,5},{5,4},{6,7},{7,6},{8,9},{9,8},{10,11... | collective-permute-start | bytes 1327112 | tf_op jit(solution)/shard_map/ppermute | solution.py:593
  363.3 30.2 %collective-permute-start.13 = (bf16[4,48,1152]{2,1,0:T(8,128)(2,1)}, bf16[4,48,1152]{2,1,0:T(8,128)(2,1)}, u32[]{:S(2)}, u32[]{:S(2)}) collective-permute-start(bf16[4,48,1152]{2,1,0:T(8,128)(2,1)} %get-tuple-element.324), channel_id=1, source_target_pairs={{0,2},{1,3},{2,0},{3,1},{4,6},{5,7},{6,4},{7,5},{8,10},{9,11},{10,... | collective-permute-start | bytes 1327112 | tf_op jit(solution)/shard_map/ppermute | solution.py:593
  366.1 29.5 %collective-permute-start.14 = (bf16[4,48,1152]{2,1,0:T(8,128)(2,1)}, bf16[4,48,1152]{2,1,0:T(8,128)(2,1)}, u32[]{:S(2)}, u32[]{:S(2)}) collective-permute-start(bf16[4,48,1152]{2,1,0:T(8,128)(2,1)} %get-tuple-element.323), channel_id=1, source_target_pairs={{0,3},{1,2},{2,1},{3,0},{4,7},{5,6},{6,5},{7,4},{8,11},{9,10},{10,... | collective-permute-start | bytes 1327112 | tf_op jit(solution)/shard_map/ppermute | solution.py:593
  408.7 26.0 %collective-permute-start.15 = (bf16[768,3456]{1,0:T(8,128)(2,1)}, bf16[768,3456]{1,0:T(8,128)(2,1)}, u32[]{:S(2)}, u32[]{:S(2)}) collective-permute-start(bf16[768,3456]{1,0:T(8,128)(2,1)} %grads_feed_away.1), channel_id=1, source_target_pairs={{0,16},{16,0},{1,17},{17,1},{2,18},{18,2},{3,19},{19,3},{4,20},{20... | collective-permute-start | bytes 15925256 | tf_op jit(solution)/shard_map/ppermute | solution.py:589
  409.6 82.0 %collective-permute-start.20 = (bf16[1024,768]{1,0:T(8,128)(2,1)S(1)}, bf16[1024,768]{1,0:T(8,128)(2,1)}, u32[]{:S(2)}, u32[]{:S(2)}) collective-permute-start(bf16[1024,768]{1,0:T(8,128)(2,1)S(1)} %copy-done.3), channel_id=1, source_target_pairs={{16,0},{17,1},{18,2},{19,3},{20,4},{21,5},{22,6},{23,7},{24,8},{25... | collective-permute-start | bytes 4718600 | tf_op jit(solution)/shard_map/ppermute | solution.py:736
  414.2 17.8 %collective-permute-start.16 = (bf16[1,48,1152]{2,1,0:T(8,128)(2,1)S(1)}, bf16[1,48,1152]{2,1,0:T(8,128)(2,1)S(1)}, u32[]{:S(2)}, u32[]{:S(2)}) collective-permute-start(bf16[1,48,1152]{2,1,0:T(8,128)(2,1)S(1)} %get-tuple-element.340), channel_id=1, source_target_pairs={{0,4},{1,5},{2,6},{3,7},{4,0},{5,1},{6,2},{7,3},{8,12},{9,13},{10,... | collective-permute-start | bytes 331784 | tf_op jit(solution)/shard_map/ppermute | solution.py:593
  414.3 19.0 %collective-permute-start.17 = (bf16[1,48,1152]{2,1,0:T(8,128)(2,1)S(1)}, bf16[1,48,1152]{2,1,0:T(8,128)(2,1)S(1)}, u32[]{:S(2)}, u32[]{:S(2)}) collective-permute-start(bf16[1,48,1152]{2,1,0:T(8,128)(2,1)S(1)} %get-tuple-element.339), channel_id=1, source_target_pairs={{0,8},{1,9},{2,10},{3,11},{4,12},{5,13},{6,14},{7,15},{8,0},{9,1},... | collective-permute-start | bytes 331784 | tf_op jit(solution)/shard_map/ppermute | solution.py:593
  415.7 19.0 %collective-permute-start.18 = (bf16[1,48,1152]{2,1,0:T(8,128)(2,1)S(1)}, bf16[1,48,1152]{2,1,0:T(8,128)(2,1)S(1)}, u32[]{:S(2)}, u32[]{:S(2)}) collective-permute-start(bf16[1,48,1152]{2,1,0:T(8,128)(2,1)S(1)} %get-tuple-element.338), channel_id=1, source_target_pairs={{0,12},{1,13},{2,14},{3,15},{4,8},{5,9},{6,10},{7,11},{8,4},{9,5},... | collective-permute-start | bytes 331784 | tf_op jit(solution)/shard_map/ppermute | solution.py:593
  433.4 58.2 %collective-permute-start.22 = (bf16[1024,768]{1,0:T(8,128)(2,1)S(1)}, bf16[1024,768]{1,0:T(8,128)(2,1)}, u32[]{:S(2)}, u32[]{:S(2)}) collective-permute-start(bf16[1024,768]{1,0:T(8,128)(2,1)S(1)} %copy-done.2), channel_id=1, source_target_pairs={{0,16},{1,17},{2,18},{3,19},{4,20},{5,21},{6,22},{7,23},{8,24},{9,... | collective-permute-start | bytes 4718600 | tf_op jit(solution)/shard_map/ppermute | solution.py:739
  443.3 48.3 %collective-permute-start.19 = (bf16[4,48,3456]{2,1,0:T(8,128)(2,1)}, bf16[4,48,3456]{2,1,0:T(8,128)(2,1)}, u32[]{:S(2)}, u32[]{:S(2)}) collective-permute-start(bf16[4,48,3456]{2,1,0:T(8,128)(2,1)} %get-tuple-element.321), channel_id=1, source_target_pairs={{0,1},{1,0},{2,3},{3,2},{4,5},{5,4},{6,7},{7,6},{8,9},{9,8},{10,11... | collective-permute-start | bytes 3981320 | tf_op jit(solution)/shard_map/ppermute | solution.py:593
  443.8 63.3 %collective-permute-start.23 = (bf16[4,48,3456]{2,1,0:T(8,128)(2,1)}, bf16[4,48,3456]{2,1,0:T(8,128)(2,1)}, u32[]{:S(2)}, u32[]{:S(2)}) collective-permute-start(bf16[4,48,3456]{2,1,0:T(8,128)(2,1)} %get-tuple-element.320), channel_id=1, source_target_pairs={{0,2},{1,3},{2,0},{3,1},{4,6},{5,7},{6,4},{7,5},{8,10},{9,11},{10,... | collective-permute-start | bytes 3981320 | tf_op jit(solution)/shard_map/ppermute | solution.py:593
  444.8 62.4 %collective-permute-start.24 = (bf16[4,48,3456]{2,1,0:T(8,128)(2,1)}, bf16[4,48,3456]{2,1,0:T(8,128)(2,1)}, u32[]{:S(2)}, u32[]{:S(2)}) collective-permute-start(bf16[4,48,3456]{2,1,0:T(8,128)(2,1)} %get-tuple-element.319), channel_id=1, source_target_pairs={{0,3},{1,2},{2,1},{3,0},{4,7},{5,6},{6,5},{7,4},{8,11},{9,10},{10,... | collective-permute-start | bytes 3981320 | tf_op jit(solution)/shard_map/ppermute | solution.py:593
  529.8 27.7 %collective-permute-start.29 = (bf16[4,48,1152]{2,1,0:T(8,128)(2,1)}, bf16[4,48,1152]{2,1,0:T(8,128)(2,1)}, u32[]{:S(2)}, u32[]{:S(2)}) collective-permute-start(bf16[4,48,1152]{2,1,0:T(8,128)(2,1)} %get-tuple-element.330), channel_id=1, source_target_pairs={{0,1},{1,0},{2,3},{3,2},{4,5},{5,4},{6,7},{7,6},{8,9},{9,8},{10,11... | collective-permute-start | bytes 1327112 | tf_op jit(solution)/shard_map/ppermute | solution.py:593
  530.9 26.7 %collective-permute-start.30 = (bf16[4,48,1152]{2,1,0:T(8,128)(2,1)}, bf16[4,48,1152]{2,1,0:T(8,128)(2,1)}, u32[]{:S(2)}, u32[]{:S(2)}) collective-permute-start(bf16[4,48,1152]{2,1,0:T(8,128)(2,1)} %get-tuple-element.329), channel_id=1, source_target_pairs={{0,2},{1,3},{2,0},{3,1},{4,6},{5,7},{6,4},{7,5},{8,10},{9,11},{10,... | collective-permute-start | bytes 1327112 | tf_op jit(solution)/shard_map/ppermute | solution.py:593
  531.0 26.6 %collective-permute-start.31 = (bf16[4,48,1152]{2,1,0:T(8,128)(2,1)}, bf16[4,48,1152]{2,1,0:T(8,128)(2,1)}, u32[]{:S(2)}, u32[]{:S(2)}) collective-permute-start(bf16[4,48,1152]{2,1,0:T(8,128)(2,1)} %get-tuple-element.328), channel_id=1, source_target_pairs={{0,3},{1,2},{2,1},{3,0},{4,7},{5,6},{6,5},{7,4},{8,11},{9,10},{10,... | collective-permute-start | bytes 1327112 | tf_op jit(solution)/shard_map/ppermute | solution.py:593
  532.5 25.1 %collective-permute-start.33 = (bf16[1,48,3456]{2,1,0:T(8,128)(2,1)}, bf16[1,48,3456]{2,1,0:T(8,128)(2,1)}, u32[]{:S(2)}, u32[]{:S(2)}) collective-permute-start(bf16[1,48,3456]{2,1,0:T(8,128)(2,1)} %get-tuple-element.333), channel_id=1, source_target_pairs={{0,8},{1,9},{2,10},{3,11},{4,12},{5,13},{6,14},{7,15},{8,0},{9,1},... | collective-permute-start | bytes 995336 | tf_op jit(solution)/shard_map/ppermute | solution.py:593
  535.7 21.8 %collective-permute-start.34 = (bf16[1,48,3456]{2,1,0:T(8,128)(2,1)S(1)}, bf16[1,48,3456]{2,1,0:T(8,128)(2,1)}, u32[]{:S(2)}, u32[]{:S(2)}) collective-permute-start(bf16[1,48,3456]{2,1,0:T(8,128)(2,1)S(1)} %get-tuple-element.332), channel_id=1, source_target_pairs={{0,12},{1,13},{2,14},{3,15},{4,8},{5,9},{6,10},{7,11},{8,4},{9,5},... | collective-permute-start | bytes 995336 | tf_op jit(solution)/shard_map/ppermute | solution.py:593
  567.6 18.3 %collective-permute-start.37 = (bf16[1,48,1152]{2,1,0:T(8,128)(2,1)S(1)}, bf16[1,48,1152]{2,1,0:T(8,128)(2,1)S(1)}, u32[]{:S(2)}, u32[]{:S(2)}) collective-permute-start(bf16[1,48,1152]{2,1,0:T(8,128)(2,1)S(1)} %get-tuple-element.346), channel_id=1, source_target_pairs={{0,8},{1,9},{2,10},{3,11},{4,12},{5,13},{6,14},{7,15},{8,0},{9,1},... | collective-permute-start | bytes 331784 | tf_op jit(solution)/shard_map/ppermute | solution.py:593
  574.0 24.2 %collective-permute-start.40 = (f32[48,3456]{1,0:T(8,128)}, f32[48,3456]{1,0:T(8,128)}, u32[]{:S(2)}, u32[]{:S(2)}) collective-permute-start(f32[48,3456]{1,0:T(8,128)} %add_bitcast_fusion), channel_id=1, source_target_pairs={{16,0},{17,1},{18,2},{19,3},{20,4},{21,5},{22,6},{23,7},{24,8},{25... | collective-permute-start | bytes 1990664 | tf_op jit(solution)/shard_map/ppermute | solution.py:806
  (57 other events, 641.2 us)
Sparse Core Ops, SparseCore 0:
  14.7 123.4 all-gather.2
  141.1 85.3 all-gather.4
  288.8 163.0 reduce-scatter.1

commit v5 on v4

--- a/solution.py
+++ b/solution.py
@@ -68,7 +68,7 @@
 
 def project_kernel(count, *refs):
     x_ref, gain_ref = refs[:2]
-    normed_ref, q_ref, qt_ref, k_ref, kt_ref, v_ref, vt_ref = refs[-7:]
+    normed_ref, q_ref, k_ref, v_ref = refs[-4:]
     width = x_ref.shape[1]
     x = x_ref[...].astype(F32)
     scale = lax.rsqrt(jnp.mean(x * x, axis=-1, keepdims=True) + EPS)
@@ -76,136 +76,140 @@
     normed_ref[...] = normed
 
     def body(pieces):
-        for own, y_ref, yt_ref in zip(pieces, (q_ref, k_ref, v_ref), (qt_ref, kt_ref, vt_ref)):
+        for own, y_ref in zip(pieces, (q_ref, k_ref, v_ref)):
             for at, w_ref, start, columns in own:
                 y = dot(normed, w_ref[:, start : start + columns])
                 y_ref[:, at : at + columns] = y.astype(BF)
-                yt_ref[at : at + columns, :] = y.T.astype(BF)
-
-    with_weights(count, width, refs[2:-7], body)
+
+    with_weights(count, width, refs[2:-4], body)
 
 
 def project(x, gain, weights):
     length, width = x.shape
     rows = pl.BlockSpec((ROWB, width), lambda i: (i, 0))
-    cols = pl.BlockSpec((width, ROWB), lambda i: (0, i))
     flat = jax.ShapeDtypeStruct((length, width), BF)
-    turned = jax.ShapeDtypeStruct((width, length), BF)
     specs, operands = weight_specs(weights, width)
     return pl.pallas_call(
         functools.partial(project_kernel, weights[0]),
         grid=(length // ROWB,),
         in_specs=[rows, whole((1, width))] + specs,
-        out_specs=[rows, rows, cols, rows, cols, rows, cols],
-        out_shape=[flat, flat, turned, flat, turned, flat, turned],
+        out_specs=[rows] * 4,
+        out_shape=[flat] * 4,
         compiler_params=params(),
         cost_estimate=pl.CostEstimate(flops=6 * length * width * width, bytes_accessed=16 * length * width, transcendentals=0),
         name="project",
     )(x, gain, *operands)
 
 
-def attend_kernel(
-    heads, start_ref, mw_ref, ml_ref, qt_ref, k_ref, vt_ref, segc_ref, segr_ref, o_ref, a_ref, mixed_ref, out_acc
-):
+GROUP = 6
+
+
+def dot_l(left, right):
+    return lax.dot_general(left, right, (((0,), (0,)), ((), ())), preferred_element_type=F32)
+
+
+def stacked(rows, scale_ref, first):
+    return jnp.concatenate([(rows * scale_ref[g : g + 1, :]).astype(BF) for g in range(first, first + GROUP)], 0)
+
+
+def attend_kernel(heads, start_ref, mwx_ref, mlx_ref, q_ref, k_ref, v_ref, segc_ref, segr_ref, o_ref, a_ref, mixed_ref, out_acc):
     block = pl.program_id(0)
     start = start_ref[block]
-    size = qt_ref.shape[0] // heads
 
     def body(blocks):
         span = blocks * QB
         offset = pl.multiple_of(start * QB, QB)
         keys = k_ref[pl.ds(offset, span), :]
-        values = vt_ref[:, pl.ds(offset, span)]
-        place_k = offset + lax.broadcasted_iota(jnp.int32, (span, QB), 0)
-        place_q = block * QB + lax.broadcasted_iota(jnp.int32, (span, QB), 1)
-        allowed = (segc_ref[pl.ds(offset, span), :] == segr_ref[...]) & (place_k <= place_q)
+        values = v_ref[pl.ds(offset, span), :]
+        place_k = offset + lax.broadcasted_iota(jnp.int32, (QB, span), 1)
+        place_q = block * QB + lax.broadcasted_iota(jnp.int32, (QB, span), 0)
+        allowed = (segc_ref[...] == segr_ref[:, pl.ds(offset, span)]) & (place_k <= place_q)
         bias = jnp.where(allowed, 0.0, NEGATIVE)
-        bias = jnp.concatenate([bias, bias], 1)
-        for pair in range(heads // 2):
-            parts = []
-            for g in (2 * pair, 2 * pair + 1):
-                parts.append(
-                    jnp.concatenate(
-                        [
-                            (qt_ref[h * size : (h + 1) * size, :].astype(F32) * ml_ref[h, g]).astype(BF)
-                            for h in range(heads)
-                        ],
-                        0,
-                    )
-                )
-            scores = dot(keys, jnp.concatenate(parts, 1)) + bias
-            powers = jnp.exp2(scores - jnp.max(scores, axis=0, keepdims=True))
-            soft = (powers * (1.0 / jnp.sum(powers, axis=0, keepdims=True))).astype(BF)
-            a_ref[0, pair, 0:span, :] = soft
-            mixed = dot(values, soft)
-            mixed_ref[2 * pair] = mixed[:, :QB].astype(BF)
-            mixed_ref[2 * pair + 1] = mixed[:, QB:].astype(BF)
-            for h in range(heads):
-                own = slice(h * size, (h + 1) * size)
-                term = mixed[own, :QB] * mw_ref[2 * pair, h] + mixed[own, QB:] * mw_ref[2 * pair + 1, h]
-                if pair == 0:
-                    out_acc[own, :] = term
-                else:
-                    out_acc[own, :] += term
-        o_ref[...] = out_acc[...].T.astype(BF)
+        q = q_ref[...].astype(F32)
+
+        def score(first):
+            return dot_t(stacked(q, mlx_ref, first), keys)
+
+        def finish(first, mixed):
+            total = None
+            for n in range(GROUP):
+                own = mixed[n * QB : (n + 1) * QB, :]
+                mixed_ref[first + n] = own.astype(BF)
+                term = own * mwx_ref[first + n : first + n + 1, :]
+                total = term if total is None else total + term
+            if first == 0:
+                out_acc[...] = total
+            else:
+                out_acc[...] += total
+
+        scores = score(0)
+        before = None
+        for first in range(0, heads, GROUP):
+            following = score(first + GROUP) if first + GROUP < heads else None
+            masked = scores.reshape(GROUP, QB, span) + bias[None]
+            powers = jnp.exp2(masked - jnp.max(masked, axis=-1, keepdims=True))
+            soft = (powers * (1.0 / jnp.sum(powers, axis=-1, keepdims=True))).astype(BF).reshape(GROUP * QB, span)
+            a_ref[0, first * QB : (first + GROUP) * QB, 0:span] = soft
+            mixed = dot(soft, values)
+            if before is not None:
+                finish(first - GROUP, before)
+            before = mixed
+            scores = following
+        finish(heads - GROUP, before)
+        o_ref[...] = out_acc[...].astype(BF)
 
     for blocks in range(1, REACH // QB + 2):
         pl.when(block - start + 1 == blocks)(functools.partial(body, blocks))
 
 
-def attend(start, mw, ml, qt, k, vt, segc, segr):
-    width, length = qt.shape
-    heads = mw.shape[0]
+def attend(start, mwx, mlx, q, k, v, segc, segr):
+    length, width = q.shape
+    heads = mwx.shape[0]
     steps = length // QB
     most = REACH + QB
     rows = pl.BlockSpec((QB, width), lambda i, s: (i, 0))
-    cols = pl.BlockSpec((width, QB), lambda i, s: (0, i))
     return pl.pallas_call(
         functools.partial(attend_kernel, heads),
         grid_spec=pltpu.PrefetchScalarGridSpec(
             num_scalar_prefetch=1,
             grid=(steps,),
             in_specs=[
-                SMEM_SPEC,
-                SMEM_SPEC,
-                cols,
+                whole((heads, width)),
+                whole((heads, width)),
+                rows,
                 whole((length, width)),
-                whole((width, length)),
-                whole((length, 1)),
-                pl.BlockSpec((1, QB), lambda i, s: (0, i)),
+                whole((length, width)),
+                pl.BlockSpec((QB, 1), lambda i, s: (i, 0)),
+                whole((1, length)),
             ],
             out_specs=[
                 rows,
-                pl.BlockSpec((1, heads // 2, most, 2 * QB), lambda i, s: (i, 0, 0, 0)),
-                pl.BlockSpec((heads, width, QB), lambda i, s: (0, 0, i)),
+                pl.BlockSpec((1, heads * QB, most), lambda i, s: (i, 0, 0)),
+                pl.BlockSpec((heads, QB, width), lambda i, s: (0, i, 0)),
             ],
-            scratch_shapes=[pltpu.VMEM((width, QB), F32)],
+            scratch_shapes=[pltpu.VMEM((QB, width), F32)],
         ),
         out_shape=[
             jax.ShapeDtypeStruct((length, width), BF),
-            jax.ShapeDtypeStruct((steps, heads // 2, most, 2 * QB), BF),
-            jax.ShapeDtypeStruct((heads, width, length), BF),
+            jax.ShapeDtypeStruct((steps, heads * QB, most), BF),
+            jax.ShapeDtypeStruct((heads, length, width), BF),
         ],
         compiler_params=params(),
         cost_estimate=pl.CostEstimate(
             flops=4 * length * most * width * heads, bytes_accessed=40 << 20, transcendentals=length * most * heads
         ),
         name="attend",
-    )(start, mw, ml, qt, k, vt, segc, segr)
+    )(start, mwx, mlx, q, k, v, segc, segr)
 
 
 def attend_back_kernel(
     heads,
     start_ref,
-    mw_ref,
-    ml_ref,
     mlx_ref,
     mwx_ref,
     q_ref,
-    qt_ref,
     do_ref,
-    dot_ref,
-    kt_ref,
+    k_ref,
     v_ref,
     a_ref,
     mixed_ref,
@@ -215,17 +219,14 @@
     gmw_ref,
     dk_acc,
     dv_acc,
-    dqt_acc,
+    dq_acc,
     dz_all,
-    a_all,
     q_all,
     do_all,
 ):
     block = pl.program_id(0)
     start = start_ref[block]
-    width = qt_ref.shape[0]
-    size = width // heads
-    head_rows = [slice(h * size, (h + 1) * size) for h in range(heads)]
+    width = q_ref.shape[1]
 
     @pl.when(block == 0)
     def _():
@@ -236,44 +237,51 @@
         span = blocks * QB
         offset = pl.multiple_of(start * QB, QB)
         values = v_ref[pl.ds(offset, span), :]
-        keys = kt_ref[:, pl.ds(offset, span)]
+        keys = k_ref[pl.ds(offset, span), :]
         q = q_ref[...].astype(F32)
         do = do_ref[...].astype(F32)
-        for pair in range(heads // 2):
-            both = (2 * pair, 2 * pair + 1)
-            lanes = slice(2 * QB * pair, 2 * QB * (pair + 1))
-            parts = []
-            for g in both:
-                parts.append(
-                    jnp.concatenate([(dot_ref[own, :].astype(F32) * mw_ref[g, h]).astype(BF) for h, own in enumerate(head_rows)], 0)
-                )
-            dsoft = dot(values, jnp.concatenate(parts, 1))
-            soft = a_ref[0, pair, 0:span, :]
-            wide = soft.astype(F32)
-            product = wide * dsoft
-            dz = (product - wide * jnp.sum(product, axis=0, keepdims=True)).astype(BF)
-            dz_all[0:span, lanes] = dz
-            a_all[0:span, lanes] = soft
-            for t, g in enumerate(both):
-                at = slice((2 * pair + t) * QB, (2 * pair + t + 1) * QB)
-                q_all[at, :] = (q * mlx_ref[g : g + 1, :]).astype(BF)
-                do_all[at, :] = (do * mwx_ref[g : g + 1, :]).astype(BF)
-            side = dot(keys, dz)
-            for h, own in enumerate(head_rows):
-                terms = (side[own, :QB], side[own, QB:])
-                term = terms[0] * ml_ref[h, both[0]] + terms[1] * ml_ref[h, both[1]]
-                if pair == 0:
-                    dqt_acc[own, :] = term
-                else:
-                    dqt_acc[own, :] += term
-                qth = qt_ref[own, :].astype(F32)
-                doth = dot_ref[own, :].astype(F32)
-                for g, piece in zip(both, terms):
-                    gml_ref[g, h] += jnp.sum((qth * piece).reshape(size // 8, 8, QB), axis=0)
-                    gmw_ref[g, h] += jnp.sum((doth * mixed_ref[g, own, :].astype(F32)).reshape(size // 8, 8, QB), axis=0)
-        dv_acc[pl.ds(offset, span), :] += dot(a_all[0:span, :], do_all[...])
-        dk_acc[pl.ds(offset, span), :] += dot(dz_all[0:span, :], q_all[...])
-        dqkv_ref[pl.ds(pl.multiple_of(block * QB, QB), QB), 0:width] = dqt_acc[...].T.astype(BF)
+
+        def fold(x):
+            return jnp.sum(x.reshape(QB // 8, 8, width), axis=0)
+
+        def dsoft(first):
+            part = stacked(do, mwx_ref, first)
+            do_all[first * QB : (first + GROUP) * QB, :] = part
+            return dot_t(part, values)
+
+        def finish(first, side):
+            total = None
+            for n in range(GROUP):
+                g = first + n
+                own = side[n * QB : (n + 1) * QB, :]
+                term = own * mlx_ref[g : g + 1, :]
+                total = term if total is None else total + term
+                gml_ref[g] += fold(q * own)
+                gmw_ref[g] += fold(do * mixed_ref[g].astype(F32))
+            if first == 0:
+                dq_acc[...] = total
+            else:
+                dq_acc[...] += total
+
+        grads = dsoft(0)
+        before = None
+        for first in range(0, heads, GROUP):
+            rows = slice(first * QB, (first + GROUP) * QB)
+            following = dsoft(first + GROUP) if first + GROUP < heads else None
+            wide = a_ref[0, rows, 0:span].astype(F32)
+            product = wide * grads
+            dz = (product - wide * jnp.sum(product, axis=-1, keepdims=True)).astype(BF)
+            dz_all[rows, 0:span] = dz
+            q_all[rows, :] = stacked(q, mlx_ref, first)
+            side = dot(dz, keys)
+            if before is not None:
+                finish(first - GROUP, before)
+            before = side
+            grads = following
+        dv_acc[pl.ds(offset, span), :] += dot_l(a_ref[0, :, 0:span], do_all[...])
+        finish(heads - GROUP, before)
+        dk_acc[pl.ds(offset, span), :] += dot_l(dz_all[:, 0:span], q_all[...])
+        dqkv_ref[pl.ds(pl.multiple_of(block * QB, QB), QB), 0:width] = dq_acc[...].astype(BF)
 
     for blocks in range(1, REACH // QB + 2):
         pl.when(block - start + 1 == blocks)(functools.partial(body, blocks))
@@ -283,57 +291,53 @@
         dqkv_ref[:, width : 2 * width] = dk_acc[...].astype(BF)
         dqkv_ref[:, 2 * width :] = dv_acc[...].astype(BF)
         for g in range(heads):
-            sums_ref[0, g] = jnp.sum(gml_ref[g], axis=1)
-            sums_ref[1, g] = jnp.sum(gmw_ref[g], axis=1)
-
-
-def attend_back(start, mw, ml, mlx, mwx, q, qt, do, dot_, kt, v, soft, mixed):
+            sums_ref[0, g : g + 1, :] = jnp.sum(gml_ref[g], axis=0, keepdims=True)
+            sums_ref[1, g : g + 1, :] = jnp.sum(gmw_ref[g], axis=0, keepdims=True)
+
+
+def attend_back(start, mlx, mwx, q, do, k, v, soft, mixed):
     length, width = q.shape
-    heads = mw.shape[0]
+    heads = mlx.shape[0]
     steps = length // QB
     most = REACH + QB
     rows = pl.BlockSpec((QB, width), lambda i, s: (i, 0))
-    cols = pl.BlockSpec((width, QB), lambda i, s: (0, i))
-    sums = jax.ShapeDtypeStruct((2, heads, heads, QB), F32)
     return pl.pallas_call(
         functools.partial(attend_back_kernel, heads),
         grid_spec=pltpu.PrefetchScalarGridSpec(
             num_scalar_prefetch=1,
             grid=(steps,),
             in_specs=[
-                SMEM_SPEC,
-                SMEM_SPEC,
                 whole((heads, width)),
                 whole((heads, width)),
                 rows,
-                cols,
                 rows,
-                cols,
-                whole((width, length)),
                 whole((length, width)),
-                pl.BlockSpec((1, heads // 2, most, 2 * QB), lambda i, s: (i, 0, 0, 0)),
-                pl.BlockSpec((heads, width, QB), lambda i, s: (0, 0, i)),
+                whole((length, width)),
+                pl.BlockSpec((1, heads * QB, most), lambda i, s: (i, 0, 0)),
+                pl.BlockSpec((heads, QB, width), lambda i, s: (0, i, 0)),
             ],
-            out_specs=[whole((length, 3 * width)), whole(sums.shape)],
+            out_specs=[whole((length, 3 * width)), whole((2, heads, width))],
             scratch_shapes=[
-                pltpu.VMEM((heads, heads, 8, QB), F32),
-                pltpu.VMEM((heads, heads, 8, QB), F32),
+                pltpu.VMEM((heads, 8, width), F32),
+                pltpu.VMEM((heads, 8, width), F32),
                 pltpu.VMEM((length, width), F32),
                 pltpu.VMEM((length, width), F32),
-                pltpu.VMEM((width, QB), F32),
-                pltpu.VMEM((most, heads * QB), BF),
-                pltpu.VMEM((most, heads * QB), BF),
+                pltpu.VMEM((QB, width), F32),
+                pltpu.VMEM((heads * QB, most), BF),
                 pltpu.VMEM((heads * QB, width), BF),
                 pltpu.VMEM((heads * QB, width), BF),
             ],
         ),
-        out_shape=[jax.ShapeDtypeStruct((length, 3 * width), BF), sums],
+        out_shape=[
+            jax.ShapeDtypeStruct((length, 3 * width), BF),
+            jax.ShapeDtypeStruct((2, heads, width), F32),
+        ],
         compiler_params=params(),
         cost_estimate=pl.CostEstimate(
             flops=length * most * width * heads, bytes_accessed=8 << 20, transcendentals=0
         ),
         name="attend_back",
-    )(start, mw, ml, mlx, mwx, q, qt, do, dot_, kt, v, soft, mixed)
+    )(start, mlx, mwx, q, do, k, v, soft, mixed)
 
 
 def gelu_both(b):
@@ -415,7 +419,7 @@
 
 
 def feed_back_kernel(
-    dy_ref, slope_ref, middle_ref, gain_ref, wo_ref, wi_ref, wb_ref, gf_ref, dmiddle_ref, ga_ref, do_ref, dot_ref, total
+    dy_ref, slope_ref, middle_ref, gain_ref, wo_ref, wi_ref, wb_ref, gf_ref, dmiddle_ref, ga_ref, do_ref, total
 ):
     blocks = [slice(r, r + ROWB) for r in range(0, dy_ref.shape[0], ROWB)]
 
@@ -438,9 +442,7 @@
             dmiddle_ref[own, :] = dmiddle
             ga = dmiddle.astype(BF)
             ga_ref[own, :] = ga
-            do = dot(ga, wo_ref[...])
-            do_ref[own, :] = do.astype(BF)
-            dot_ref[:, own] = do.T.astype(BF)
+            do_ref[own, :] = dot(ga, wo_ref[...]).astype(BF)
 
 
 def feed_back(dy, slope, middle, gain, w, place_out, place_in, place_back):
@@ -462,13 +464,12 @@
             pl.BlockSpec((width, FFB), lambda i: (0, place_in * steps + i)),
             pl.BlockSpec((width, FFB), lambda i: (0, place_back * steps + i)),
         ],
-        out_specs=[chunk, all_rows, all_rows, all_rows, whole((width, length))],
+        out_specs=[chunk, all_rows, all_rows, all_rows],
         out_shape=[
             jax.ShapeDtypeStruct((length, wide), BF),
             jax.ShapeDtypeStruct((length, width), F32),
             flat,
             flat,
-            jax.ShapeDtypeStruct((width, length), BF),
         ],
         scratch_shapes=[pltpu.VMEM((length, width), F32)],
         compiler_params=params(),
@@ -561,17 +562,17 @@
 
 
 def mix_tables(mix_logits, mix_weights, size):
-    plain = mix_logits * size ** (-0.5)
-    return mix_weights, plain * LOG2E, plain, jnp.repeat(plain.T, size, axis=1), jnp.repeat(mix_weights, size, axis=1)
+    logits = jnp.repeat(mix_logits.T * size ** (-0.5), size, axis=1)
+    return logits * LOG2E, logits, jnp.repeat(mix_weights, size, axis=1)
 
 
 def layer_forward(x, seg, weights, tables):
     gains, w_qkv, w_rest, places = weights
     start, segc, segr = seg
-    normed, q, qt, k, kt, v, vt = project(x, gains[0], w_qkv)
-    o, soft, mixed = attend(start, tables[0], tables[1], qt, k, vt, segc, segr)
+    normed, q, k, v = project(x, gains[0], w_qkv)
+    o, soft, mixed = attend(start, tables[2], tables[0], q, k, v, segc, segr)
     y, middle, normed_two, slope, hidden = feed(x, o, gains[1], w_rest, *places)
-    return y, (x, normed, q, qt, kt, v, o, soft, mixed, middle, normed_two, slope, hidden)
+    return y, (x, normed, q, None, k, v, o, soft, mixed, middle, normed_two, slope, hidden)
 
 
 def windows(seg):
@@ -718,10 +719,9 @@
         slope, middle_rows = kept[11], kept[9]
         return feed_back(dy, slope, middle_rows, weights[0][1], weights[2], *weights[3])
 
-    def back_attend(do, dot_, kept, table):
-        _, _, q, qt, kt, v, _, soft, mixed = kept[:9]
-        mix, _, plain, wide_logits, wide_weights = table
-        return attend_back(seg[0], mix, plain, wide_logits, wide_weights, q, qt, do, dot_, kt, v, soft, mixed)
+    def back_attend(do, kept, table):
+        _, _, q, _, k, v, _, soft, mixed = kept[:9]
+        return attend_back(seg[0], table[1], table[2], q, do, k, v, soft, mixed)
 
     groups = bit_groups()
     masks = [1 << bit for bit in range(lax.axis_size("dp").bit_length() - 1)]
@@ -748,7 +748,8 @@
     def projection_jobs(normed, dqkv):
         return [(normed, dqkv, dqkv.shape[1] // 6, 3)]
 
-    gf, dmiddle, ga, do, dot_ = back_feed(cot, kept1, weights1)
+    y_other = to_first(y0), to_second(y1)
+    (gf, dmiddle, ga, do), y_other = barrier((back_feed(cot, kept1, weights1), y_other))
     packed1 = packed_grads(
         [(kept1[10], gf, width, 4), (cot, kept1[12], width, 4), (ga, kept1[6], width, 1)],
         jnp.zeros((1,), jnp.int32),
@@ -756,14 +757,15 @@
     )
     do, packed1 = barrier((do, packed1))
     sums1 = lax.psum_scatter(packed1, AXES, scatter_dimension=0, tiled=True)
-    dqkv, sums_mix1 = back_attend(do, dot_, kept1, tables[1])
+    dqkv, sums_mix1 = back_attend(do, kept1, tables[1])
     halves = both_halves(projection_jobs(kept1[1], dqkv), "grads_project")
     dx1 = project_back(dqkv, kept1[0], dmiddle, weights1[0][0], qkv1)
     dx1, halves = barrier((dx1, halves))
     parts1 = send_parts(added(halves), groups[0])
 
-    fed, parts1 = barrier((back_feed(dx1, kept0, weights0), parts1))
-    gf, dmiddle, ga, do, dot_ = fed
+    dx1_other = to_second(dx1)
+    fed, parts1, dx1_other = barrier((back_feed(dx1, kept0, weights0), parts1, dx1_other))
+    gf, dmiddle, ga, do = fed
     parts1 = send_parts(add_parts(parts1), groups[1])
     halves = both_halves(
         [(kept0[10], gf, width, 2), (dx1, kept0[12], width, 2), (ga, kept0[6], width // 2, 1)], "grads_feed"
@@ -773,12 +775,8 @@
     held = added(halves).astype(BF)
     do, held, proj1 = barrier((do, held, proj1))
     parts0 = send_parts(held, groups[0])
-    y_other = to_first(y0), to_second(y1)
-    dx1_other = to_second(dx1)
-    (dqkv, sums_mix0), parts0[:2], sums1, y_other, dx1_other = barrier(
-        (back_attend(do, dot_, kept0, tables[0]), parts0[:2], sums1, y_other, dx1_other)
-    )
-    mixes = jnp.sum(jnp.stack([sums_mix0, sums_mix1]), axis=4)
+    (dqkv, sums_mix0), parts0[:2], sums1 = barrier((back_attend(do, kept0, tables[0]), parts0[:2], sums1))
+    mixes = jnp.sum(jnp.stack([sums_mix0, sums_mix1]).reshape(2, 2, heads, heads, size), axis=4)
     mixes = sum_masks(mixes + swap(mixes), masks[:2])
     dqkv, parts0, mixes = barrier((dqkv, parts0, mixes))
     held = add_parts(parts0).astype(BF)

time: 622 us -> 613 us (0.986)
  waiting for transfers between devices: 88.3 us -> 117 us
  Pallas kernels: 348 us -> 324 us
  other arithmetic: 46.1 us -> 38 us
    pallas_call x2, Pallas kernels: 66.4 us -> 50.2 us  [attend(): pl.pallas_call(functools.partial(attend_kernel, heads), grid_spec=pltpu.P...]
    all_gather x1, waiting for transfers between devices: 11.1 us -> 25.5 us  [on_device(): lax.all_gather(jnp.concatenate([late0, early1], 1), AXES, axis=0, tiled=T...]
    ppermute x28, waiting for transfers between devices: 42.3 us -> 52.9 us  [partners(): lax.ppermute(x, 'dp', [(i, i ^ mask) for i in range(lax.axis_size('dp'))])]
  transfers between devices with their start and end apart: 47 -> 47, of which waited for: 17 -> 18; matrix products, arithmetic and copies ran while one was open for 10% -> 8% of each run, Pallas kernels for 45% -> 46%
where the time goes in v5:
time: 613 us; the launch traced here: 606 us
  Pallas kernels  324 us (53%)
  waiting for transfers between devices  117 us (19%)
  starting transfers between devices  86.7 us (14%)
  other arithmetic  38 us (6%)
  local copies, waits for them, and re-layouts  25.8 us (4%)
  between operations  15 us (2%)
    pallas_call x2, Pallas kernels, attend_back(): pl.pallas_call(functools.partial(attend_back_kernel, heads), grid_spec=pl...  82.8 us
    pallas_call x7, Pallas kernels, packed_grads(): pl.pallas_call(functools.partial(grads_kernel, [(columns, tiles) for _, _...  69.3 us
    ppermute x28, waiting for transfers between devices, partners(): lax.ppermute(x, 'dp', [(i, i ^ mask) for i in range(lax.axis_size('dp'))])  52.9 us
    pallas_call x2, Pallas kernels, attend(): pl.pallas_call(functools.partial(attend_kernel, heads), grid_spec=pltpu.P...  50.2 us
    ppermute x28, starting transfers between devices, partners(): lax.ppermute(x, 'dp', [(i, i ^ mask) for i in range(lax.axis_size('dp'))])  46.6 us
    pallas_call x2, Pallas kernels, feed(): pl.pallas_call(feed_kernel, grid=(steps,), in_specs=[all_rows, all_rows,...  43.8 us
    pallas_call x2, Pallas kernels, feed_back(): pl.pallas_call(feed_back_kernel, grid=(steps,), in_specs=[all_rows, chunk...  41.5 us
    all_gather x1, waiting for transfers between devices, on_device(): third = lax.all_gather(late1, AXES, axis=0, tiled=True)  32.2 us
  transfers between devices with their start and end apart: 47, of which 18 were waited for; matrix products, arithmetic and copies ran while one was open for 8% of the time, Pallas kernels for 46%

profile of v5, /device:TPU:1, one launch (start us, length us, event | category | flops | bytes accessed | tf_op | source)
XLA Modules:
  0.0 606.3 jit_solution(16475719431493564446)
XLA Ops:
  26.6 6.1 %collective-permute-done.2 = bf16[1,48,1280]{2,1,0:T(8,128)(2,1)S(1)} collective-permute-done((bf16[1,48,1280]{2,1,0:T(8,128)(2,1)S(1)}, bf16[1,48,1280]{2,1,0:T(8,128)(2,1)S(1)}, u32[]{:S(2)}, u32[]{:S(2)}) %collective-permute-start.2) | collective-permute-done | bytes 122912 | tf_op jit(solution)/shard_map/ppermute | solution.py:594
  46.8 7.8 %collective-permute-done.7 = bf16[4,48,1280]{2,1,0:T(8,128)(2,1)S(1)} collective-permute-done((bf16[4,48,1280]{2,1,0:T(8,128)(2,1)S(1)}, bf16[4,48,1280]{2,1,0:T(8,128)(2,1)S(1)}, u32[]{:S(2)}, u32[]{:S(2)}) %collective-permute-start.7) | collective-permute-done | bytes 491552 | tf_op jit(solution)/shard_map/ppermute | solution.py:594
  54.7 14.7 %collective-permute-start.8 = (bf16[768,1280]{1,0:T(8,128)(2,1)S(1)}, bf16[768,1280]{1,0:T(8,128)(2,1)}, u32[]{:S(2)}, u32[]{:S(2)}) collective-permute-start(bf16[768,1280]{1,0:T(8,128)(2,1)S(1)} %bitcast.175), channel_id=1, source_target_pairs={{0,16},{16,0},{1,17},{17,1},{2,18},{18,2},{3,19},{19,3},{4,20},{20... | collective-permute-start | bytes 5898248 | tf_op jit(solution)/shard_map/ppermute | solution.py:590
  79.1 9.1 %project.2 = (bf16[1024,768]{1,0:T(8,128)(2,1)}, bf16[1024,768]{1,0:T(8,128)(2,1)}, bf16[1024,768]{1,0:T(8,128)(2,1)}, bf16[1024,768]{1,0:T(8,128)(2,1)}) custom-call(bf16[1024,768]{1,0:T(8,128)(2,1)} %get-tuple-element.135.refs_0_.x_ref, f32[1,768]{1,0:T(1,128)} %copy.128.refs_1_.gain_ref, s32[1]{0:T(128)} %bitcast.19.refs_2_.half_ref.refs_0_, ...), custom_call_target="tpu_custom_call" | custom-call | flops 3623878656 | bytes 12582912 | tf_op jit(solution)/shard_map/project/pallas_call | solution.py:92
  88.2 25.4 %attend.2 = (bf16[1024,768]{1,0:T(8,128)(2,1)}, bf16[8,1536,640]{2,1,0:T(8,128)(2,1)}, bf16[12,1024,768]{2,1,0:T(8,128)(2,1)}) custom-call(s32[8]{0:T(128)} %convert_reduce_fusion.start_ref, f32[12,768]{1,0:T(8,128)} %reshape.268.mwx_ref, f32[12,768]{1,0:T(8,128)} %broadcast_multiply_fusion.1.mlx_ref, bf16[1024,768]{1,0:T(8,128)(2,1)} %get-tuple-element.137.q_ref, ...), custom_call_target="tpu_custom_call" | custom-call | flops 24159191040 | bytes 41943040 | tf_op jit(solution)/shard_map/attend/pallas_call | solution.py:171
  113.6 25.5 %all-gather.3.cloned.1.call-done.wo_ref.wi_ref.wb_ref.refs_2_.refs_3_.refs_4_.refs_0_.refs_1_ = bf16[768,9344]{1,0:T(8,128)(2,1)} async-done(((bf16[24,9344]{1,0:T(8,128)(2,1)}), bf16[768,9344]{1,0:T(8,128)(2,1)}) %all-gather.3.cloned.1.call-update) | async-done | bytes 14352400 | tf_op jit(solution)/shard_map/all_gather | solution.py:695
  141.7 21.9 %feed.2 = (bf16[1024,768]{1,0:T(8,128)(2,1)}, f32[1024,768]{1,0:T(8,128)}, bf16[1024,768]{1,0:T(8,128)(2,1)}, bf16[1024,3072]{1,0:T(8,128)(2,1)}, bf16[1024,3072]{1,0:T(8,128)(2,1)}) custom-call(bf16[1024,768]{1,0:T(8,128)(2,1)} %get-tuple-element.135.refs_0_.x_ref, bf16[1024,768]{1,0:T(8,128)(2,1)} %get-tuple-element.142.o_ref.refs_5_, ...), custom_call_target="tpu_custom_call" | custom-call | flops 10871635968 | bytes 31457280 | tf_op jit(solution)/shard_map/feed/pallas_call | solution.py:392
  163.6 7.6 %project.3 = (bf16[1024,768]{1,0:T(8,128)(2,1)}, bf16[1024,768]{1,0:T(8,128)(2,1)}, bf16[1024,768]{1,0:T(8,128)(2,1)}, bf16[1024,768]{1,0:T(8,128)(2,1)}) custom-call(bf16[1024,768]{1,0:T(8,128)(2,1)} %get-tuple-element.220.refs_0_.x_ref, f32[1,768]{1,0:T(1,128)} %copy.132.refs_1_.gain_ref, ...), custom_call_target="tpu_custom_call" | custom-call | flops 3623878656 | bytes 12582912 | tf_op jit(solution)/shard_map/project/pallas_call | solution.py:92
  171.2 24.8 %attend.3 = (bf16[1024,768]{1,0:T(8,128)(2,1)}, bf16[8,1536,640]{2,1,0:T(8,128)(2,1)}, bf16[12,1024,768]{2,1,0:T(8,128)(2,1)}) custom-call(s32[8]{0:T(128)} %convert_reduce_fusion.start_ref, f32[12,768]{1,0:T(8,128)} %reshape.271.mwx_ref, f32[12,768]{1,0:T(8,128)} %broadcast_multiply_fusion.mlx_ref, bf16[1024,768]{1,0:T(8,128)(2,1)} %get-tuple-element.144.q_ref, ...), custom_call_target="tpu_custom_call" | custom-call | flops 24159191040 | bytes 41943040 | tf_op jit(solution)/shard_map/attend/pallas_call | solution.py:171
  196.0 32.2 %all-gather.5.cloned.1.call-done.wo_ref.wi_ref.wb_ref = bf16[768,6912]{1,0:T(8,128)(2,1)} async-done(((bf16[24,6912]{1,0:T(8,128)(2,1)}), bf16[768,6912]{1,0:T(8,128)(2,1)}) %all-gather.5.cloned.1.call-update) | async-done | bytes 10616848 | tf_op jit(solution)/shard_map/all_gather | solution.py:696
  228.2 22.0 %feed.3 = (bf16[1024,768]{1,0:T(8,128)(2,1)}, f32[1024,768]{1,0:T(8,128)}, bf16[1024,768]{1,0:T(8,128)(2,1)}, bf16[1024,3072]{1,0:T(8,128)(2,1)}, bf16[1024,3072]{1,0:T(8,128)(2,1)}) custom-call(bf16[1024,768]{1,0:T(8,128)(2,1)} %get-tuple-element.220.refs_0_.x_ref, bf16[1024,768]{1,0:T(8,128)(2,1)} %get-tuple-element.148.o_ref.refs_5_, ...), custom_call_target="tpu_custom_call" | custom-call | flops 10871635968 | bytes 31457280 | tf_op jit(solution)/shard_map/feed/pallas_call | solution.py:392
  255.8 20.4 %feed_back.2 = (bf16[1024,3072]{1,0:T(8,128)(2,1)}, f32[1024,768]{1,0:T(8,128)}, bf16[1024,768]{1,0:T(8,128)(2,1)}, bf16[1024,768]{1,0:T(8,128)(2,1)}) custom-call(bf16[1024,768]{1,0:T(8,128)(2,1)} %get-tuple-element.145.dy_ref.refs_2_, bf16[1024,3072]{1,0:T(8,128)(2,1)} %get-tuple-element.149.slope_ref, f32[1024,768]{1,0:T(8,128)} %get-tuple-element.150.middle_ref, ...), custom_call_target="tpu_custom_call" | custom-call | flops 10871635968 | bytes 41943040 | tf_op jit(solution)/shard_map/feed_back/pallas_call | solution.py:455
  276.2 19.8 %grads_feed.1 = bf16[768,6912]{1,0:T(8,128)(2,1)} custom-call(s32[1]{0:T(128)} %constant.105.clone.1.half_ref, bf16[1024,768]{1,0:T(8,128)(2,1)} %get-tuple-element.157.refs_0_, bf16[1024,3072]{1,0:T(8,128)(2,1)} %get-tuple-element.158.refs_1_, bf16[1024,768]{1,0:T(8,128)(2,1)} %get-tuple-element.145.dy_ref.refs_2_, ...), custom_call_target="tpu_custom_call" | custom-call | flops 10871635968 | bytes 27525120 | tf_op jit(solution)/shard_map/grads_feed/pallas_call | solution.py:552
  296.1 41.5 %attend_back.2 = (bf16[1024,2304]{1,0:T(8,128)(2,1)}, f32[2,12,768]{2,1,0:T(8,128)}) custom-call(s32[8]{0:T(128)} %convert_reduce_fusion.start_ref, f32[12,768]{1,0:T(8,128)} %copy-done.23, f32[12,768]{1,0:T(8,128)} %reshape.271.mwx_ref, bf16[1024,768]{1,0:T(8,128)(2,1)} %get-tuple-element.144.q_ref, bf16[1024,768]{1,0:T(8,128)(2,1)} %get-tuple-element.161.do_ref, ...), custom_call_target="tpu_custom_call" | custom-call | flops 6039797760 | bytes 8388608 | tf_op jit(solution)/shard_map/attend_back/pallas_call | solution.py:304
  343.5 9.5 %project_back.2.dy_ref.refs_2_ = bf16[1024,768]{1,0:T(8,128)(2,1)} custom-call(bf16[1024,2304]{1,0:T(8,128)(2,1)} %get-tuple-element.164.dqkv_ref.refs_1_, bf16[1024,768]{1,0:T(8,128)(2,1)} %get-tuple-element.220.refs_0_.x_ref, f32[1024,768]{1,0:T(8,128)} %get-tuple-element.165.dmiddle_ref, f32[1,768]{1,0:T(1,128)} %copy.132.refs_1_.gain_ref, ...), custom_call_target="tpu_custom_call" | custom-call | flops 786432 | bytes 65536 | tf_op jit(solution)/shard_map/project_back/pallas_call | solution.py:501
  353.0 6.0 grads_project_here.2
  371.9 21.1 %feed_back.3 = (bf16[1024,3072]{1,0:T(8,128)(2,1)}, f32[1024,768]{1,0:T(8,128)}, bf16[1024,768]{1,0:T(8,128)(2,1)}, bf16[1024,768]{1,0:T(8,128)(2,1)}) custom-call(bf16[1024,768]{1,0:T(8,128)(2,1)} %project_back.2.dy_ref.refs_2_, bf16[1024,3072]{1,0:T(8,128)(2,1)} %get-tuple-element.168.slope_ref, f32[1024,768]{1,0:T(8,128)} %get-tuple-element.169.middle_ref, ...), custom_call_target="tpu_custom_call" | custom-call | flops 10871635968 | bytes 41943040 | tf_op jit(solution)/shard_map/feed_back/pallas_call | solution.py:455
  399.6 12.9 %grads_feed_away.1 = bf16[768,3456]{1,0:T(8,128)(2,1)} custom-call(s32[1]{0:T(128)S(6)} %sub.3.half_ref, bf16[1024,768]{1,0:T(8,128)(2,1)} %get-tuple-element.177.refs_0_, bf16[1024,3072]{1,0:T(8,128)(2,1)} %get-tuple-element.178.refs_1_, bf16[1024,768]{1,0:T(8,128)(2,1)} %project_back.2.dy_ref.refs_2_, bf16[1024,3072]{1,0:T(8,128)(2,1)} %get-tuple-element.179.refs_3_, ...), custom_call_target="tpu_custom_call" | custom-call | flops 5435817984 | bytes 15138816 | tf_op jit(solution)/shard_map/grads_feed_away/pallas_call | solution.py:552
  419.1 12.9 %grads_feed_here.1 = bf16[768,3456]{1,0:T(8,128)(2,1)} custom-call(s32[1]{0:T(128)} %bitcast.19.refs_2_.half_ref.refs_0_, bf16[1024,768]{1,0:T(8,128)(2,1)} %get-tuple-element.177.refs_0_, bf16[1024,3072]{1,0:T(8,128)(2,1)} %get-tuple-element.178.refs_1_, bf16[1024,768]{1,0:T(8,128)(2,1)} %project_back.2.dy_ref.refs_2_, ...), custom_call_target="tpu_custom_call" | custom-call | flops 5435817984 | bytes 15138816 | tf_op jit(solution)/shard_map/grads_feed_here/pallas_call | solution.py:552
  443.7 41.3 %attend_back.3 = (bf16[1024,2304]{1,0:T(8,128)(2,1)}, f32[2,12,768]{2,1,0:T(8,128)}) custom-call(s32[8]{0:T(128)} %convert_reduce_fusion.start_ref, f32[12,768]{1,0:T(8,128)} %copy-done.22, f32[12,768]{1,0:T(8,128)} %reshape.268.mwx_ref, bf16[1024,768]{1,0:T(8,128)(2,1)} %get-tuple-element.137.q_ref, bf16[1024,768]{1,0:T(8,128)(2,1)} %get-tuple-element.192.do_ref, ...), custom_call_target="tpu_custom_call" | custom-call | flops 6039797760 | bytes 8388608 | tf_op jit(solution)/shard_map/attend_back/pallas_call | solution.py:304
  492.2 10.0 %collective-permute-done.26 = f32[2,2,12,12]{3,1,2,0:T(2,128)S(1)} collective-permute-done((f32[2,2,12,12]{3,1,2,0:T(2,128)S(1)}, f32[2,2,12,12]{3,1,2,0:T(2,128)S(1)}, u32[]{:S(2)}, u32[]{:S(2)}) %collective-permute-start.26) | collective-permute-done | bytes 2336 | tf_op jit(solution)/shard_map/ppermute | solution.py:594
  535.8 9.8 %project_back.3 = bf16[1024,768]{1,0:T(8,128)(2,1)} custom-call(bf16[1024,2304]{1,0:T(8,128)(2,1)} %get-tuple-element.212.refs_1_.dqkv_ref, bf16[1024,768]{1,0:T(8,128)(2,1)} %get-tuple-element.135.refs_0_.x_ref, f32[1024,768]{1,0:T(8,128)} %get-tuple-element.213.dmiddle_ref, f32[1,768]{1,0:T(1,128)} %copy.128.refs_1_.gain_ref, ...), custom_call_target="tpu_custom_call" | custom-call | flops 786432 | bytes 65536 | tf_op jit(solution)/shard_map/project_back/pallas_call | solution.py:501
  548.9 8.9 %collective-permute-done.33 = bf16[1,48,3456]{2,1,0:T(8,128)(2,1)} collective-permute-done((bf16[1,48,3456]{2,1,0:T(8,128)(2,1)}, bf16[1,48,3456]{2,1,0:T(8,128)(2,1)}, u32[]{:S(2)}, u32[]{:S(2)}) %collective-permute-start.33) | collective-permute-done | bytes 331808 | tf_op jit(solution)/shard_map/ppermute | solution.py:594
  559.5 7.4 %collective-permute-start.35 = (bf16[1,48,1152]{2,1,0:T(8,128)(2,1)S(1)}, bf16[1,48,1152]{2,1,0:T(8,128)(2,1)S(1)}, u32[]{:S(2)}, u32[]{:S(2)}) collective-permute-start(bf16[1,48,1152]{2,1,0:T(8,128)(2,1)S(1)} %get-tuple-element.338), channel_id=1, source_target_pairs={{0,4},{1,5},{2,6},{3,7},{4,0},{5,1},{6,2},{7,3},{8,12},{9,13},{10,... | collective-permute-start | bytes 331784 | tf_op jit(solution)/shard_map/ppermute | solution.py:594
  (271 shorter events, 172.5 us)
Async XLA Ops:
  7.2 131.9 %all-gather.3.cloned.1.call-start = ((), (), s32[]{:S(2)}) async-start(), calls=%async_computation.1 | async-start | bytes 14800896 | tf_op jit(solution)/shard_map/all_gather | solution.py:695
  15.6 212.7 %all-gather.5.cloned.1.call-start = ((), (), s32[]{:S(2)}) async-start(), calls=%async_computation.2 | async-start | bytes 10948608 | tf_op jit(solution)/shard_map/all_gather | solution.py:696
  16.3 468.6 %reduce-scatter.2.cloned.1.call-start = ((), (), s32[]{:S(2)}) async-start(), calls=%async_computation.3 | async-start | bytes 10948608 | tf_op jit(solution)/shard_map/reduce_scatter | solution.py:759
  38.5 16.1 %collective-permute-start.7 = (bf16[4,48,1280]{2,1,0:T(8,128)(2,1)S(1)}, bf16[4,48,1280]{2,1,0:T(8,128)(2,1)S(1)}, u32[]{:S(2)}, u32[]{:S(2)}) collective-permute-start(bf16[4,48,1280]{2,1,0:T(8,128)(2,1)S(1)} %constant_dynamic-update-slice_fusion), channel_id=1, source_target_pairs={{0,3},{1,2},{2,1},{3,0},{4,7},{5,6},{6,5},{7,4},{8,11},{9,10},{10,... | collective-permute-start | bytes 1474568 | tf_op jit(solution)/shard_map/ppermute | solution.py:594
  54.7 24.4 %collective-permute-start.8 = (bf16[768,1280]{1,0:T(8,128)(2,1)S(1)}, bf16[768,1280]{1,0:T(8,128)(2,1)}, u32[]{:S(2)}, u32[]{:S(2)}) collective-permute-start(bf16[768,1280]{1,0:T(8,128)(2,1)S(1)} %bitcast.175), channel_id=1, source_target_pairs={{0,16},{16,0},{1,17},{17,1},{2,18},{18,2},{3,19},{19,3},{4,20},{20... | collective-permute-start | bytes 5898248 | tf_op jit(solution)/shard_map/ppermute | solution.py:590
  250.2 26.0 %collective-permute-start.12 = (bf16[1024,768]{1,0:T(8,128)(2,1)}, bf16[1024,768]{1,0:T(8,128)(2,1)S(1)}, u32[]{:S(2)}, u32[]{:S(2)}) collective-permute-start(bf16[1024,768]{1,0:T(8,128)(2,1)} %get-tuple-element.223), channel_id=1, source_target_pairs={{0,16},{1,17},{2,18},{3,19},{4,20},{5,21},{6,22},{7,23},{8,24},{9,... | collective-permute-start | bytes 4718600 | tf_op jit(solution)/shard_map/ppermute | solution.py:739
  251.5 24.7 %collective-permute-start.11 = (bf16[1024,768]{1,0:T(8,128)(2,1)S(1)}, bf16[1024,768]{1,0:T(8,128)(2,1)}, u32[]{:S(2)}, u32[]{:S(2)}) collective-permute-start(bf16[1024,768]{1,0:T(8,128)(2,1)S(1)} %copy-done.4), channel_id=1, source_target_pairs={{16,0},{17,1},{18,2},{19,3},{20,4},{21,5},{22,6},{23,7},{24,8},{25... | collective-permute-start | bytes 4718600 | tf_op jit(solution)/shard_map/ppermute | solution.py:736
  343.5 15.6 %collective-permute-start.13 = (bf16[768,1152]{1,0:T(8,128)(2,1)}, bf16[768,1152]{1,0:T(8,128)(2,1)S(1)}, u32[]{:S(2)}, u32[]{:S(2)}) collective-permute-start(bf16[768,1152]{1,0:T(8,128)(2,1)} %grads_project_away.2), channel_id=1, source_target_pairs={{0,16},{16,0},{1,17},{17,1},{2,18},{18,2},{3,19},{19,3},{4,20},{20... | collective-permute-start | bytes 5308424 | tf_op jit(solution)/shard_map/ppermute | solution.py:590
  359.1 40.5 %collective-permute-start.17 = (bf16[1024,768]{1,0:T(8,128)(2,1)S(1)}, bf16[1024,768]{1,0:T(8,128)(2,1)}, u32[]{:S(2)}, u32[]{:S(2)}) collective-permute-start(bf16[1024,768]{1,0:T(8,128)(2,1)S(1)} %copy-done.2), channel_id=1, source_target_pairs={{0,16},{1,17},{2,18},{3,19},{4,20},{5,21},{6,22},{7,23},{8,24},{9,... | collective-permute-start | bytes 4718600 | tf_op jit(solution)/shard_map/ppermute | solution.py:739
  365.3 28.9 %collective-permute-start.14 = (bf16[4,48,1152]{2,1,0:T(8,128)(2,1)}, bf16[4,48,1152]{2,1,0:T(8,128)(2,1)S(1)}, u32[]{:S(2)}, u32[]{:S(2)}) collective-permute-start(bf16[4,48,1152]{2,1,0:T(8,128)(2,1)} %get-tuple-element.315), channel_id=1, source_target_pairs={{0,1},{1,0},{2,3},{3,2},{4,5},{5,4},{6,7},{7,6},{8,9},{9,8},{10,11... | collective-permute-start | bytes 1327112 | tf_op jit(solution)/shard_map/ppermute | solution.py:594
  367.1 31.0 %collective-permute-start.15 = (bf16[4,48,1152]{2,1,0:T(8,128)(2,1)}, bf16[4,48,1152]{2,1,0:T(8,128)(2,1)S(1)}, u32[]{:S(2)}, u32[]{:S(2)}) collective-permute-start(bf16[4,48,1152]{2,1,0:T(8,128)(2,1)} %get-tuple-element.314), channel_id=1, source_target_pairs={{0,2},{1,3},{2,0},{3,1},{4,6},{5,7},{6,4},{7,5},{8,10},{9,11},{10,... | collective-permute-start | bytes 1327112 | tf_op jit(solution)/shard_map/ppermute | solution.py:594
  371.9 27.7 %collective-permute-start.16 = (bf16[4,48,1152]{2,1,0:T(8,128)(2,1)}, bf16[4,48,1152]{2,1,0:T(8,128)(2,1)S(1)}, u32[]{:S(2)}, u32[]{:S(2)}) collective-permute-start(bf16[4,48,1152]{2,1,0:T(8,128)(2,1)} %get-tuple-element.313), channel_id=1, source_target_pairs={{0,3},{1,2},{2,1},{3,0},{4,7},{5,6},{6,5},{7,4},{8,11},{9,10},{10,... | collective-permute-start | bytes 1327112 | tf_op jit(solution)/shard_map/ppermute | solution.py:594
  412.5 20.7 %collective-permute-start.18 = (bf16[768,3456]{1,0:T(8,128)(2,1)}, bf16[768,3456]{1,0:T(8,128)(2,1)}, u32[]{:S(2)}, u32[]{:S(2)}) collective-permute-start(bf16[768,3456]{1,0:T(8,128)(2,1)} %grads_feed_away.1), channel_id=1, source_target_pairs={{0,16},{16,0},{1,17},{17,1},{2,18},{18,2},{3,19},{19,3},{4,20},{20... | collective-permute-start | bytes 15925256 | tf_op jit(solution)/shard_map/ppermute | solution.py:590
  415.5 16.5 %collective-permute-start.19 = (bf16[1,48,1152]{2,1,0:T(8,128)(2,1)S(1)}, bf16[1,48,1152]{2,1,0:T(8,128)(2,1)S(1)}, u32[]{:S(2)}, u32[]{:S(2)}) collective-permute-start(bf16[1,48,1152]{2,1,0:T(8,128)(2,1)S(1)} %get-tuple-element.330), channel_id=1, source_target_pairs={{0,4},{1,5},{2,6},{3,7},{4,0},{5,1},{6,2},{7,3},{8,12},{9,13},{10,... | collective-permute-start | bytes 331784 | tf_op jit(solution)/shard_map/ppermute | solution.py:594
  440.8 44.1 %collective-permute-start.22 = (bf16[4,48,3456]{2,1,0:T(8,128)(2,1)}, bf16[4,48,3456]{2,1,0:T(8,128)(2,1)S(1)}, u32[]{:S(2)}, u32[]{:S(2)}) collective-permute-start(bf16[4,48,3456]{2,1,0:T(8,128)(2,1)} %get-tuple-element.311), channel_id=1, source_target_pairs={{0,1},{1,0},{2,3},{3,2},{4,5},{5,4},{6,7},{7,6},{8,9},{9,8},{10,11... | collective-permute-start | bytes 3981320 | tf_op jit(solution)/shard_map/ppermute | solution.py:594
  441.7 63.3 %collective-permute-start.23 = (bf16[4,48,3456]{2,1,0:T(8,128)(2,1)}, bf16[4,48,3456]{2,1,0:T(8,128)(2,1)}, u32[]{:S(2)}, u32[]{:S(2)}) collective-permute-start(bf16[4,48,3456]{2,1,0:T(8,128)(2,1)} %get-tuple-element.310), channel_id=1, source_target_pairs={{0,2},{1,3},{2,0},{3,1},{4,6},{5,7},{6,4},{7,5},{8,10},{9,11},{10,... | collective-permute-start | bytes 3981320 | tf_op jit(solution)/shard_map/ppermute | solution.py:594
  442.7 62.3 %collective-permute-start.24 = (bf16[4,48,3456]{2,1,0:T(8,128)(2,1)}, bf16[4,48,3456]{2,1,0:T(8,128)(2,1)}, u32[]{:S(2)}, u32[]{:S(2)}) collective-permute-start(bf16[4,48,3456]{2,1,0:T(8,128)(2,1)} %get-tuple-element.309), channel_id=1, source_target_pairs={{0,3},{1,2},{2,1},{3,0},{4,7},{5,6},{6,5},{7,4},{8,11},{9,10},{10,... | collective-permute-start | bytes 3981320 | tf_op jit(solution)/shard_map/ppermute | solution.py:594
  517.2 16.5 %collective-permute-start.32 = (bf16[1,48,3456]{2,1,0:T(8,128)(2,1)S(1)}, bf16[1,48,3456]{2,1,0:T(8,128)(2,1)S(1)}, u32[]{:S(2)}, u32[]{:S(2)}) collective-permute-start(bf16[1,48,3456]{2,1,0:T(8,128)(2,1)S(1)} %get-tuple-element.324), channel_id=1, source_target_pairs={{0,4},{1,5},{2,6},{3,7},{4,0},{5,1},{6,2},{7,3},{8,12},{9,13},{10,... | collective-permute-start | bytes 995336 | tf_op jit(solution)/shard_map/ppermute | solution.py:594
  530.1 27.8 %collective-permute-start.29 = (bf16[4,48,1152]{2,1,0:T(8,128)(2,1)}, bf16[4,48,1152]{2,1,0:T(8,128)(2,1)}, u32[]{:S(2)}, u32[]{:S(2)}) collective-permute-start(bf16[4,48,1152]{2,1,0:T(8,128)(2,1)} %get-tuple-element.320), channel_id=1, source_target_pairs={{0,1},{1,0},{2,3},{3,2},{4,5},{5,4},{6,7},{7,6},{8,9},{9,8},{10,11... | collective-permute-start | bytes 1327112 | tf_op jit(solution)/shard_map/ppermute | solution.py:594
  531.2 26.7 %collective-permute-start.30 = (bf16[4,48,1152]{2,1,0:T(8,128)(2,1)}, bf16[4,48,1152]{2,1,0:T(8,128)(2,1)}, u32[]{:S(2)}, u32[]{:S(2)}) collective-permute-start(bf16[4,48,1152]{2,1,0:T(8,128)(2,1)} %get-tuple-element.319), channel_id=1, source_target_pairs={{0,2},{1,3},{2,0},{3,1},{4,6},{5,7},{6,4},{7,5},{8,10},{9,11},{10,... | collective-permute-start | bytes 1327112 | tf_op jit(solution)/shard_map/ppermute | solution.py:594
  532.6 25.3 %collective-permute-start.31 = (bf16[4,48,1152]{2,1,0:T(8,128)(2,1)}, bf16[4,48,1152]{2,1,0:T(8,128)(2,1)}, u32[]{:S(2)}, u32[]{:S(2)}) collective-permute-start(bf16[4,48,1152]{2,1,0:T(8,128)(2,1)} %get-tuple-element.318), channel_id=1, source_target_pairs={{0,3},{1,2},{2,1},{3,0},{4,7},{5,6},{6,5},{7,4},{8,11},{9,10},{10,... | collective-permute-start | bytes 1327112 | tf_op jit(solution)/shard_map/ppermute | solution.py:594
  533.0 24.9 %collective-permute-start.33 = (bf16[1,48,3456]{2,1,0:T(8,128)(2,1)}, bf16[1,48,3456]{2,1,0:T(8,128)(2,1)}, u32[]{:S(2)}, u32[]{:S(2)}) collective-permute-start(bf16[1,48,3456]{2,1,0:T(8,128)(2,1)} %get-tuple-element.323), channel_id=1, source_target_pairs={{0,8},{1,9},{2,10},{3,11},{4,12},{5,13},{6,14},{7,15},{8,0},{9,1},... | collective-permute-start | bytes 995336 | tf_op jit(solution)/shard_map/ppermute | solution.py:594
  534.5 23.4 %collective-permute-start.34 = (bf16[1,48,3456]{2,1,0:T(8,128)(2,1)}, bf16[1,48,3456]{2,1,0:T(8,128)(2,1)}, u32[]{:S(2)}, u32[]{:S(2)}) collective-permute-start(bf16[1,48,3456]{2,1,0:T(8,128)(2,1)} %get-tuple-element.322), channel_id=1, source_target_pairs={{0,12},{1,13},{2,14},{3,15},{4,8},{5,9},{6,10},{7,11},{8,4},{9,5},... | collective-permute-start | bytes 995336 | tf_op jit(solution)/shard_map/ppermute | solution.py:594
  572.4 18.5 %collective-permute-start.40 = (f32[48,3456]{1,0:T(8,128)S(1)}, f32[48,3456]{1,0:T(8,128)}, u32[]{:S(2)}, u32[]{:S(2)}) collective-permute-start(f32[48,3456]{1,0:T(8,128)S(1)} %add_bitcast_fusion), channel_id=1, source_target_pairs={{16,0},{17,1},{18,2},{19,3},{20,4},{21,5},{22,6},{23,7},{24,8},{25... | collective-permute-start | bytes 1990664 | tf_op jit(solution)/shard_map/ppermute | solution.py:804
  (60 other events, 608.7 us)
Sparse Core Ops, SparseCore 0:
  15.7 123.3 all-gather.2
  142.6 85.5 all-gather.4
  296.2 164.4 reduce-scatter.1

commit v6 on v5

--- a/solution.py
+++ b/solution.py
@@ -566,13 +566,14 @@
     return logits * LOG2E, logits, jnp.repeat(mix_weights, size, axis=1)
 
 
-def layer_forward(x, seg, weights, tables):
-    gains, w_qkv, w_rest, places = weights
+def layer_forward(x, seg, weights, tables, projected, meanwhile):
+    gains, _, w_rest, places = weights
     start, segc, segr = seg
-    normed, q, k, v = project(x, gains[0], w_qkv)
+    normed, q, k, v = projected
     o, soft, mixed = attend(start, tables[2], tables[0], q, k, v, segc, segr)
+    o, meanwhile = lax.optimization_barrier((o, meanwhile))
     y, middle, normed_two, slope, hidden = feed(x, o, gains[1], w_rest, *places)
-    return y, (x, normed, q, None, k, v, o, soft, mixed, middle, normed_two, slope, hidden)
+    return y, (x, normed, q, None, k, v, o, soft, mixed, middle, normed_two, slope, hidden), meanwhile
 
 
 def windows(seg):
@@ -613,6 +614,11 @@
             out = lax.dynamic_update_slice(out, piece[:, None], (0, me ^ other, 0, 0))
         done = out.reshape(-1, share, columns)
     return done.reshape(-1, columns), meanwhile
+
+
+def gather_under(own, kernel):
+    rows, results = gather_rows(own, kernel())
+    return results, rows
 
 
 def send_parts(held, group):
@@ -680,8 +686,8 @@
     qkv = jnp.concatenate([w_query[0], w_key[0], w_value[0]], 1).astype(BF)
     low = jnp.concatenate([qkv[:, :middle], gain_columns], 1)
     high = jnp.concatenate([qkv[:, middle:], gain_columns], 1)
-    from_first = swap(high)
-    own_half, (x0, seg, cot) = gather_rows(jnp.where(first, low, from_first), (x0, seg, cot))
+    arrived = swap(jnp.where(first, high, low))
+    own_half, (x0, seg, cot) = gather_rows(jnp.where(first, low, arrived), (x0, seg, cot))
     other_half = swap(own_half)
 
     late = jnp.concatenate([w_in[0].astype(BF), w_back[0].T.astype(BF), w_out[0].T.astype(BF)], 1)
@@ -691,8 +697,7 @@
         return jnp.where(first, own[:half], other), jnp.where(first, other, own[half:])
 
     late0, late1 = halves(late)
-    early1 = halves(jnp.concatenate([qkv, gain_columns], 1))[1]
-    second = lax.all_gather(jnp.concatenate([late0, early1], 1), AXES, axis=0, tiled=True)
+    second = lax.all_gather(late0, AXES, axis=0, tiled=True)
     third = lax.all_gather(late1, AXES, axis=0, tiled=True)
 
     own_mix = jnp.concatenate([mix_logits, mix_weights], 0)
@@ -706,14 +711,16 @@
         return rows[0:1], rows[1:2]
 
     at_out = 2 * wide // width
-    end = 2 * wide + 4 * width
     qkv0 = (2, (section.astype(jnp.int32).reshape(1), own_half, other_half), ())
-    qkv1 = (3, (second,) * 3, (at_out + 1, at_out + 2, at_out + 3))
     weights0 = (gain_rows(own_half[:, middle:]), qkv0, second, (at_out, 0, 1))
-    weights1 = (gain_rows(second[:, end:]), qkv1, third, (at_out, 0, 1))
-
-    y0, kept0 = layer_forward(x0, seg, weights0, tables[0])
-    y1, kept1 = layer_forward(y0, seg, weights1, tables[1])
+
+    projected, own_half = gather_under(
+        jnp.where(first, arrived, high), lambda: project(x0, weights0[0][0], qkv0)
+    )
+    y0, kept0, own_half = layer_forward(x0, seg, weights0, tables[0], projected, own_half)
+    qkv1 = (2, (section.astype(jnp.int32).reshape(1), own_half, swap(own_half)), ())
+    weights1 = (gain_rows(own_half[:, middle:]), qkv1, third, (at_out, 0, 1))
+    y1, kept1, _ = layer_forward(y0, seg, weights1, tables[1], project(y0, weights1[0][0], qkv1), ())
 
     def back_feed(dy, kept, weights):
         slope, middle_rows = kept[11], kept[9]

time: 613 us -> 600 us (0.979)
  waiting for transfers between devices: 117 us -> 88.8 us
  starting transfers between devices: 86.7 us -> 108 us
    all_gather x1, waiting for transfers between devices: 25.5 us -> 0.01 us  [on_device(): second = lax.all_gather(late0, AXES, axis=0, tiled=True)]
    ppermute x10, starting transfers between devices: 23.1 us -> 41.3 us  [swap(): return lax.ppermute(x, 'section', [(0, 1), (1, 0)])]
    ppermute x28 -> x34, waiting for transfers between devices: 52.9 us -> 65.7 us  [partners(): lax.ppermute(x, 'dp', [(i, i ^ mask) for i in range(lax.axis_size('dp'))])]
    all_gather x1, waiting for transfers between devices: 32.2 us -> 19.9 us  [on_device(): third = lax.all_gather(late1, AXES, axis=0, tiled=True)]
    ppermute x28 -> x34, starting transfers between devices: 46.6 us -> 49.5 us  [partners(): lax.ppermute(x, 'dp', [(i, i ^ mask) for i in range(lax.axis_size('dp'))])]
  transfers between devices with their start and end apart: 47 -> 53, of which waited for: 18 -> 17; matrix products, arithmetic and copies ran while one was open for 8% -> 8% of each run, Pallas kernels for 46% -> 46%
where the time goes in v6:
time: 600 us; the launch traced here: 593 us
  Pallas kernels  320 us (53%)
  starting transfers between devices  108 us (18%)
  waiting for transfers between devices  88.8 us (15%)
  other arithmetic  35.1 us (6%)
  local copies, waits for them, and re-layouts  27.2 us (5%)
  between operations  14.9 us (2%)
    pallas_call x2, Pallas kernels, attend_back(): pl.pallas_call(functools.partial(attend_back_kernel, heads), grid_spec=pl...  77.9 us
    pallas_call x7, Pallas kernels, packed_grads(): pl.pallas_call(functools.partial(grads_kernel, [(columns, tiles) for _, _...  69.5 us
    ppermute x34, waiting for transfers between devices, partners(): lax.ppermute(x, 'dp', [(i, i ^ mask) for i in range(lax.axis_size('dp'))])  65.7 us
    ppermute x34, starting transfers between devices, partners(): lax.ppermute(x, 'dp', [(i, i ^ mask) for i in range(lax.axis_size('dp'))])  49.5 us
    pallas_call x2, Pallas kernels, attend(): pl.pallas_call(functools.partial(attend_kernel, heads), grid_spec=pltpu.P...  48.5 us
    pallas_call x2, Pallas kernels, feed(): pl.pallas_call(feed_kernel, grid=(steps,), in_specs=[all_rows, all_rows,...  43.7 us
    ppermute x10, starting transfers between devices, swap(): return lax.ppermute(x, 'section', [(0, 1), (1, 0)])  41.3 us
    pallas_call x2, Pallas kernels, feed_back(): pl.pallas_call(feed_back_kernel, grid=(steps,), in_specs=[all_rows, chunk...  41.2 us
  transfers between devices with their start and end apart: 53, of which 17 were waited for; matrix products, arithmetic and copies ran while one was open for 8% of the time, Pallas kernels for 46%

profile of v6, /device:TPU:1, one launch (start us, length us, event | category | flops | bytes accessed | tf_op | source)
XLA Modules:
  0.0 593.2 jit_solution(10195911357795430289)
XLA Ops:
  44.7 12.1 %collective-permute-done.10 = bf16[4,48,1280]{2,1,0:T(8,128)(2,1)S(1)} collective-permute-done((bf16[4,48,1280]{2,1,0:T(8,128)(2,1)S(1)}, bf16[4,48,1280]{2,1,0:T(8,128)(2,1)S(1)}, u32[]{:S(2)}, u32[]{:S(2)}) %collective-permute-start.10) | collective-permute-done | bytes 491552 | tf_op jit(solution)/shard_map/ppermute | solution.py:595
  56.8 12.7 %collective-permute-start.11 = (bf16[768,1280]{1,0:T(8,128)(2,1)S(1)}, bf16[768,1280]{1,0:T(8,128)(2,1)}, u32[]{:S(2)}, u32[]{:S(2)}) collective-permute-start(bf16[768,1280]{1,0:T(8,128)(2,1)S(1)} %bitcast.199), channel_id=1, source_target_pairs={{0,16},{16,0},{1,17},{17,1},{2,18},{18,2},{3,19},{19,3},{4,20},{20... | collective-permute-start | bytes 5898248 | tf_op jit(solution)/shard_map/ppermute | solution.py:591
  70.8 6.5 %collective-permute-start.5 = (bf16[1,48,1280]{2,1,0:T(8,128)(2,1)S(1)}, bf16[1,48,1280]{2,1,0:T(8,128)(2,1)S(1)}, u32[]{:S(2)}, u32[]{:S(2)}) collective-permute-start(bf16[1,48,1280]{2,1,0:T(8,128)(2,1)S(1)} %get-tuple-element.310), channel_id=1, source_target_pairs={{0,4},{1,5},{2,6},{3,7},{4,0},{5,1},{6,2},{7,3},{8,12},{9,13},{10,... | collective-permute-start | bytes 368648 | tf_op jit(solution)/shard_map/ppermute | solution.py:595
  83.3 7.8 %collective-permute-done.7 = bf16[1,48,1280]{2,1,0:T(8,128)(2,1)S(1)} collective-permute-done((bf16[1,48,1280]{2,1,0:T(8,128)(2,1)S(1)}, bf16[1,48,1280]{2,1,0:T(8,128)(2,1)S(1)}, u32[]{:S(2)}, u32[]{:S(2)}) %collective-permute-start.7) | collective-permute-done | bytes 122912 | tf_op jit(solution)/shard_map/ppermute | solution.py:595
  92.1 9.1 %project.2 = (bf16[1024,768]{1,0:T(8,128)(2,1)}, bf16[1024,768]{1,0:T(8,128)(2,1)}, bf16[1024,768]{1,0:T(8,128)(2,1)}, bf16[1024,768]{1,0:T(8,128)(2,1)}) custom-call(bf16[1024,768]{1,0:T(8,128)(2,1)} %get-tuple-element.142.refs_0_.x_ref, f32[1,768]{1,0:T(1,128)} %copy.133.refs_1_.gain_ref, s32[1]{0:T(128)} %bitcast.20.refs_2_.refs_0_.half_ref, ...), custom_call_target="tpu_custom_call" | custom-call | flops 3623878656 | bytes 12582912 | tf_op jit(solution)/shard_map/project/pallas_call | solution.py:92
  103.9 24.4 %attend.2 = (bf16[1024,768]{1,0:T(8,128)(2,1)}, bf16[8,1536,640]{2,1,0:T(8,128)(2,1)}, bf16[12,1024,768]{2,1,0:T(8,128)(2,1)}) custom-call(s32[8]{0:T(128)} %convert_reduce_fusion.start_ref, f32[12,768]{1,0:T(8,128)} %reshape.284.mwx_ref, f32[12,768]{1,0:T(8,128)} %broadcast_multiply_fusion.1.mlx_ref, bf16[1024,768]{1,0:T(8,128)(2,1)} %get-tuple-element.148.q_ref, ...), custom_call_target="tpu_custom_call" | custom-call | flops 24159191040 | bytes 41943040 | tf_op jit(solution)/shard_map/attend/pallas_call | solution.py:171
  140.0 21.9 %feed.2 = (bf16[1024,768]{1,0:T(8,128)(2,1)}, f32[1024,768]{1,0:T(8,128)}, bf16[1024,768]{1,0:T(8,128)(2,1)}, bf16[1024,3072]{1,0:T(8,128)(2,1)}, bf16[1024,3072]{1,0:T(8,128)(2,1)}) custom-call(bf16[1024,768]{1,0:T(8,128)(2,1)} %get-tuple-element.142.refs_0_.x_ref, bf16[1024,768]{1,0:T(8,128)(2,1)} %get-tuple-element.155.o_ref.refs_5_, ...), custom_call_target="tpu_custom_call" | custom-call | flops 10871635968 | bytes 31457280 | tf_op jit(solution)/shard_map/feed/pallas_call | solution.py:392
  161.9 9.2 %project.3 = (bf16[1024,768]{1,0:T(8,128)(2,1)}, bf16[1024,768]{1,0:T(8,128)(2,1)}, bf16[1024,768]{1,0:T(8,128)(2,1)}, bf16[1024,768]{1,0:T(8,128)(2,1)}) custom-call(bf16[1024,768]{1,0:T(8,128)(2,1)} %get-tuple-element.234.refs_0_.x_ref, f32[1,768]{1,0:T(1,128)} %copy.141.refs_1_.gain_ref, s32[1]{0:T(128)} %bitcast.20.refs_2_.refs_0_.half_ref, ...), custom_call_target="tpu_custom_call" | custom-call | flops 3623878656 | bytes 12582912 | tf_op jit(solution)/shard_map/project/pallas_call | solution.py:92
  171.1 24.1 %attend.3 = (bf16[1024,768]{1,0:T(8,128)(2,1)}, bf16[8,1536,640]{2,1,0:T(8,128)(2,1)}, bf16[12,1024,768]{2,1,0:T(8,128)(2,1)}) custom-call(s32[8]{0:T(128)} %convert_reduce_fusion.start_ref, f32[12,768]{1,0:T(8,128)} %reshape.288.mwx_ref, f32[12,768]{1,0:T(8,128)} %broadcast_multiply_fusion.mlx_ref, bf16[1024,768]{1,0:T(8,128)(2,1)} %get-tuple-element.158.q_ref, ...), custom_call_target="tpu_custom_call" | custom-call | flops 24159191040 | bytes 41943040 | tf_op jit(solution)/shard_map/attend/pallas_call | solution.py:171
  195.2 19.9 %all-gather.5.cloned.1.call-done.wo_ref.wi_ref.wb_ref = bf16[768,6912]{1,0:T(8,128)(2,1)} async-done(((bf16[24,6912]{1,0:T(8,128)(2,1)}), bf16[768,6912]{1,0:T(8,128)(2,1)}) %all-gather.5.cloned.1.call-update) | async-done | bytes 10616848 | tf_op jit(solution)/shard_map/all_gather | solution.py:701
  215.1 21.9 %feed.3 = (bf16[1024,768]{1,0:T(8,128)(2,1)}, f32[1024,768]{1,0:T(8,128)}, bf16[1024,768]{1,0:T(8,128)(2,1)}, bf16[1024,3072]{1,0:T(8,128)(2,1)}, bf16[1024,3072]{1,0:T(8,128)(2,1)}) custom-call(bf16[1024,768]{1,0:T(8,128)(2,1)} %get-tuple-element.234.refs_0_.x_ref, bf16[1024,768]{1,0:T(8,128)(2,1)} %get-tuple-element.162.o_ref.refs_5_, ...), custom_call_target="tpu_custom_call" | custom-call | flops 10871635968 | bytes 31457280 | tf_op jit(solution)/shard_map/feed/pallas_call | solution.py:392
  242.5 20.4 %feed_back.2 = (bf16[1024,3072]{1,0:T(8,128)(2,1)}, f32[1024,768]{1,0:T(8,128)}, bf16[1024,768]{1,0:T(8,128)(2,1)}, bf16[1024,768]{1,0:T(8,128)(2,1)}) custom-call(bf16[1024,768]{1,0:T(8,128)(2,1)} %get-tuple-element.159.dy_ref.refs_2_, bf16[1024,3072]{1,0:T(8,128)(2,1)} %get-tuple-element.163.slope_ref, f32[1024,768]{1,0:T(8,128)} %get-tuple-element.164.middle_ref, ...), custom_call_target="tpu_custom_call" | custom-call | flops 10871635968 | bytes 41943040 | tf_op jit(solution)/shard_map/feed_back/pallas_call | solution.py:455
  262.9 19.8 %grads_feed.1 = bf16[768,6912]{1,0:T(8,128)(2,1)} custom-call(s32[1]{0:T(128)} %constant.109.clone.1.half_ref, bf16[1024,768]{1,0:T(8,128)(2,1)} %get-tuple-element.171.refs_0_, bf16[1024,3072]{1,0:T(8,128)(2,1)} %get-tuple-element.172.refs_1_, bf16[1024,768]{1,0:T(8,128)(2,1)} %get-tuple-element.159.dy_ref.refs_2_, ...), custom_call_target="tpu_custom_call" | custom-call | flops 10871635968 | bytes 27525120 | tf_op jit(solution)/shard_map/grads_feed/pallas_call | solution.py:552
  282.7 39.1 %attend_back.2 = (bf16[1024,2304]{1,0:T(8,128)(2,1)}, f32[2,12,768]{2,1,0:T(8,128)}) custom-call(s32[8]{0:T(128)} %convert_reduce_fusion.start_ref, f32[12,768]{1,0:T(8,128)} %copy-done.24, f32[12,768]{1,0:T(8,128)} %reshape.288.mwx_ref, bf16[1024,768]{1,0:T(8,128)(2,1)} %get-tuple-element.158.q_ref, bf16[1024,768]{1,0:T(8,128)(2,1)} %get-tuple-element.175.do_ref, ...), custom_call_target="tpu_custom_call" | custom-call | flops 6039797760 | bytes 8388608 | tf_op jit(solution)/shard_map/attend_back/pallas_call | solution.py:304
  333.3 10.6 %project_back.2.dy_ref.refs_2_ = bf16[1024,768]{1,0:T(8,128)(2,1)} custom-call(bf16[1024,2304]{1,0:T(8,128)(2,1)} %get-tuple-element.178.dqkv_ref.refs_1_, bf16[1024,768]{1,0:T(8,128)(2,1)} %get-tuple-element.234.refs_0_.x_ref, f32[1024,768]{1,0:T(8,128)} %get-tuple-element.179.dmiddle_ref, f32[1,768]{1,0:T(1,128)} %copy.141.refs_1_.gain_ref, ...), custom_call_target="tpu_custom_call" | custom-call | flops 786432 | bytes 65536 | tf_op jit(solution)/shard_map/project_back/pallas_call | solution.py:501
  358.9 20.8 %feed_back.3 = (bf16[1024,3072]{1,0:T(8,128)(2,1)}, f32[1024,768]{1,0:T(8,128)}, bf16[1024,768]{1,0:T(8,128)(2,1)}, bf16[1024,768]{1,0:T(8,128)(2,1)}) custom-call(bf16[1024,768]{1,0:T(8,128)(2,1)} %project_back.2.dy_ref.refs_2_, bf16[1024,3072]{1,0:T(8,128)(2,1)} %get-tuple-element.182.slope_ref, f32[1024,768]{1,0:T(8,128)} %get-tuple-element.183.middle_ref, ...), custom_call_target="tpu_custom_call" | custom-call | flops 10871635968 | bytes 41943040 | tf_op jit(solution)/shard_map/feed_back/pallas_call | solution.py:455
  385.9 12.9 %grads_feed_away.1 = bf16[768,3456]{1,0:T(8,128)(2,1)} custom-call(s32[1]{0:T(128)S(6)} %sub.3.half_ref, bf16[1024,768]{1,0:T(8,128)(2,1)} %get-tuple-element.191.refs_0_, bf16[1024,3072]{1,0:T(8,128)(2,1)} %get-tuple-element.192.refs_1_, bf16[1024,768]{1,0:T(8,128)(2,1)} %project_back.2.dy_ref.refs_2_, bf16[1024,3072]{1,0:T(8,128)(2,1)} %get-tuple-element.193.refs_3_, ...), custom_call_target="tpu_custom_call" | custom-call | flops 5435817984 | bytes 15138816 | tf_op jit(solution)/shard_map/grads_feed_away/pallas_call | solution.py:552
  405.8 12.9 %grads_feed_here.1 = bf16[768,3456]{1,0:T(8,128)(2,1)} custom-call(s32[1]{0:T(128)} %bitcast.20.refs_2_.refs_0_.half_ref, bf16[1024,768]{1,0:T(8,128)(2,1)} %get-tuple-element.191.refs_0_, bf16[1024,3072]{1,0:T(8,128)(2,1)} %get-tuple-element.192.refs_1_, bf16[1024,768]{1,0:T(8,128)(2,1)} %project_back.2.dy_ref.refs_2_, ...), custom_call_target="tpu_custom_call" | custom-call | flops 5435817984 | bytes 15138816 | tf_op jit(solution)/shard_map/grads_feed_here/pallas_call | solution.py:552
  431.2 38.8 %attend_back.3 = (bf16[1024,2304]{1,0:T(8,128)(2,1)}, f32[2,12,768]{2,1,0:T(8,128)}) custom-call(s32[8]{0:T(128)} %convert_reduce_fusion.start_ref, f32[12,768]{1,0:T(8,128)} %copy-done.23, f32[12,768]{1,0:T(8,128)} %reshape.284.mwx_ref, bf16[1024,768]{1,0:T(8,128)(2,1)} %get-tuple-element.148.q_ref, bf16[1024,768]{1,0:T(8,128)(2,1)} %get-tuple-element.206.do_ref, ...), custom_call_target="tpu_custom_call" | custom-call | flops 6039797760 | bytes 8388608 | tf_op jit(solution)/shard_map/attend_back/pallas_call | solution.py:304
  471.4 9.3 %collective-permute-start.31 = (f32[2,2,12,12]{3,1,2,0:T(2,128)S(1)}, f32[2,2,12,12]{3,1,2,0:T(2,128)S(1)}, u32[]{:S(2)}, u32[]{:S(2)}) collective-permute-start(f32[2,2,12,12]{3,1,2,0:T(2,128)S(1)} %maximum_reduce_fusion), channel_id=1, source_target_pairs={{0,16},{16,0},{1,17},{17,1},{2,18},{18,2},{3,19},{19,3},{4,20},{20... | collective-permute-start | bytes 6920 | tf_op jit(solution)/shard_map/ppermute | solution.py:591
  481.7 8.1 %collective-permute-done.32 = f32[2,2,12,12]{3,1,2,0:T(2,128)S(1)} collective-permute-done((f32[2,2,12,12]{3,1,2,0:T(2,128)S(1)}, f32[2,2,12,12]{3,1,2,0:T(2,128)S(1)}, u32[]{:S(2)}, u32[]{:S(2)}) %collective-permute-start.32) | collective-permute-done | bytes 2336 | tf_op jit(solution)/shard_map/ppermute | solution.py:595
  522.7 9.8 %project_back.3 = bf16[1024,768]{1,0:T(8,128)(2,1)} custom-call(bf16[1024,2304]{1,0:T(8,128)(2,1)} %get-tuple-element.226.refs_1_.dqkv_ref, bf16[1024,768]{1,0:T(8,128)(2,1)} %get-tuple-element.142.refs_0_.x_ref, f32[1024,768]{1,0:T(8,128)} %get-tuple-element.227.dmiddle_ref, f32[1,768]{1,0:T(1,128)} %copy.133.refs_1_.gain_ref, ...), custom_call_target="tpu_custom_call" | custom-call | flops 786432 | bytes 65536 | tf_op jit(solution)/shard_map/project_back/pallas_call | solution.py:501
  535.8 9.0 %collective-permute-done.39 = bf16[1,48,3456]{2,1,0:T(8,128)(2,1)} collective-permute-done((bf16[1,48,3456]{2,1,0:T(8,128)(2,1)}, bf16[1,48,3456]{2,1,0:T(8,128)(2,1)}, u32[]{:S(2)}, u32[]{:S(2)}) %collective-permute-start.39) | collective-permute-done | bytes 331808 | tf_op jit(solution)/shard_map/ppermute | solution.py:595
  546.3 7.4 %collective-permute-start.41 = (bf16[1,48,1152]{2,1,0:T(8,128)(2,1)S(1)}, bf16[1,48,1152]{2,1,0:T(8,128)(2,1)S(1)}, u32[]{:S(2)}, u32[]{:S(2)}) collective-permute-start(bf16[1,48,1152]{2,1,0:T(8,128)(2,1)S(1)} %get-tuple-element.342), channel_id=1, source_target_pairs={{0,4},{1,5},{2,6},{3,7},{4,0},{5,1},{6,2},{7,3},{8,12},{9,13},{10,... | collective-permute-start | bytes 331784 | tf_op jit(solution)/shard_map/ppermute | solution.py:595
  (296 shorter events, 189.7 us)
Async XLA Ops:
  7.2 132.8 %all-gather.3.cloned.1.call-start = ((), (), s32[]{:S(2)}) async-start(), calls=%async_computation.1 | async-start | bytes 10948608 | tf_op jit(solution)/shard_map/all_gather | solution.py:700
  13.2 201.9 %all-gather.5.cloned.1.call-start = ((), (), s32[]{:S(2)}) async-start(), calls=%async_computation.2 | async-start | bytes 10948608 | tf_op jit(solution)/shard_map/all_gather | solution.py:701
  13.9 456.2 %reduce-scatter.2.cloned.1.call-start = ((), (), s32[]{:S(2)}) async-start(), calls=%async_computation.3 | async-start | bytes 10948608 | tf_op jit(solution)/shard_map/reduce_scatter | solution.py:766
  56.8 35.3 %collective-permute-start.11 = (bf16[768,1280]{1,0:T(8,128)(2,1)S(1)}, bf16[768,1280]{1,0:T(8,128)(2,1)}, u32[]{:S(2)}, u32[]{:S(2)}) collective-permute-start(bf16[768,1280]{1,0:T(8,128)(2,1)S(1)} %bitcast.199), channel_id=1, source_target_pairs={{0,16},{16,0},{1,17},{17,1},{2,18},{18,2},{3,19},{19,3},{4,20},{20... | collective-permute-start | bytes 5898248 | tf_op jit(solution)/shard_map/ppermute | solution.py:591
  101.3 27.3 %collective-permute-start.12 = (bf16[4,48,1280]{2,1,0:T(8,128)(2,1)S(1)}, bf16[4,48,1280]{2,1,0:T(8,128)(2,1)}, u32[]{:S(2)}, u32[]{:S(2)}) collective-permute-start(bf16[4,48,1280]{2,1,0:T(8,128)(2,1)S(1)} %constant_dynamic-update-slice_fusion), channel_id=1, source_target_pairs={{0,1},{1,0},{2,3},{3,2},{4,5},{5,4},{6,7},{7,6},{8,9},{9,8},{10,11... | collective-permute-start | bytes 1474568 | tf_op jit(solution)/shard_map/ppermute | solution.py:595
  102.6 27.1 %collective-permute-start.13 = (bf16[4,48,1280]{2,1,0:T(8,128)(2,1)S(1)}, bf16[4,48,1280]{2,1,0:T(8,128)(2,1)S(1)}, u32[]{:S(2)}, u32[]{:S(2)}) collective-permute-start(bf16[4,48,1280]{2,1,0:T(8,128)(2,1)S(1)} %constant_dynamic-update-slice_fusion), channel_id=1, source_target_pairs={{0,2},{1,3},{2,0},{3,1},{4,6},{5,7},{6,4},{7,5},{8,10},{9,11},{10,... | collective-permute-start | bytes 1474568 | tf_op jit(solution)/shard_map/ppermute | solution.py:595
  102.6 27.1 %collective-permute-start.14 = (bf16[4,48,1280]{2,1,0:T(8,128)(2,1)S(1)}, bf16[4,48,1280]{2,1,0:T(8,128)(2,1)S(1)}, u32[]{:S(2)}, u32[]{:S(2)}) collective-permute-start(bf16[4,48,1280]{2,1,0:T(8,128)(2,1)S(1)} %constant_dynamic-update-slice_fusion), channel_id=1, source_target_pairs={{0,3},{1,2},{2,1},{3,0},{4,7},{5,6},{6,5},{7,4},{8,11},{9,10},{10,... | collective-permute-start | bytes 1474568 | tf_op jit(solution)/shard_map/ppermute | solution.py:595
  129.8 32.1 %collective-permute-start.16 = (bf16[768,1280]{1,0:T(8,128)(2,1)S(1)}, bf16[768,1280]{1,0:T(8,128)(2,1)}, u32[]{:S(2)}, u32[]{:S(2)}) collective-permute-start(bf16[768,1280]{1,0:T(8,128)(2,1)S(1)} %bitcast.195), channel_id=1, source_target_pairs={{0,16},{16,0},{1,17},{17,1},{2,18},{18,2},{3,19},{19,3},{4,20},{20... | collective-permute-start | bytes 5898248 | tf_op jit(solution)/shard_map/ppermute | solution.py:591
  236.9 25.9 %collective-permute-start.18 = (bf16[1024,768]{1,0:T(8,128)(2,1)}, bf16[1024,768]{1,0:T(8,128)(2,1)S(1)}, u32[]{:S(2)}, u32[]{:S(2)}) collective-permute-start(bf16[1024,768]{1,0:T(8,128)(2,1)} %get-tuple-element.237), channel_id=1, source_target_pairs={{0,16},{1,17},{2,18},{3,19},{4,20},{5,21},{6,22},{7,23},{8,24},{9,... | collective-permute-start | bytes 4718600 | tf_op jit(solution)/shard_map/ppermute | solution.py:746
  238.2 24.7 %collective-permute-start.17 = (bf16[1024,768]{1,0:T(8,128)(2,1)S(1)}, bf16[1024,768]{1,0:T(8,128)(2,1)}, u32[]{:S(2)}, u32[]{:S(2)}) collective-permute-start(bf16[1024,768]{1,0:T(8,128)(2,1)S(1)} %copy-done.7), channel_id=1, source_target_pairs={{16,0},{17,1},{18,2},{19,3},{20,4},{21,5},{22,6},{23,7},{24,8},{25... | collective-permute-start | bytes 4718600 | tf_op jit(solution)/shard_map/ppermute | solution.py:743
  327.9 22.2 %collective-permute-start.19 = (bf16[768,1152]{1,0:T(8,128)(2,1)}, bf16[768,1152]{1,0:T(8,128)(2,1)S(1)}, u32[]{:S(2)}, u32[]{:S(2)}) collective-permute-start(bf16[768,1152]{1,0:T(8,128)(2,1)} %grads_project_away.2), channel_id=1, source_target_pairs={{0,16},{16,0},{1,17},{17,1},{2,18},{18,2},{3,19},{19,3},{4,20},{20... | collective-permute-start | bytes 5308424 | tf_op jit(solution)/shard_map/ppermute | solution.py:591
  350.0 35.8 %collective-permute-start.23 = (bf16[1024,768]{1,0:T(8,128)(2,1)S(1)}, bf16[1024,768]{1,0:T(8,128)(2,1)}, u32[]{:S(2)}, u32[]{:S(2)}) collective-permute-start(bf16[1024,768]{1,0:T(8,128)(2,1)S(1)} %copy-done.2), channel_id=1, source_target_pairs={{0,16},{1,17},{2,18},{3,19},{4,20},{5,21},{6,22},{7,23},{8,24},{9,... | collective-permute-start | bytes 4718600 | tf_op jit(solution)/shard_map/ppermute | solution.py:746
  356.2 24.7 %collective-permute-start.20 = (bf16[4,48,1152]{2,1,0:T(8,128)(2,1)}, bf16[4,48,1152]{2,1,0:T(8,128)(2,1)S(1)}, u32[]{:S(2)}, u32[]{:S(2)}) collective-permute-start(bf16[4,48,1152]{2,1,0:T(8,128)(2,1)} %get-tuple-element.319), channel_id=1, source_target_pairs={{0,1},{1,0},{2,3},{3,2},{4,5},{5,4},{6,7},{7,6},{8,9},{9,8},{10,11... | collective-permute-start | bytes 1327112 | tf_op jit(solution)/shard_map/ppermute | solution.py:595
  356.3 24.7 %collective-permute-start.21 = (bf16[4,48,1152]{2,1,0:T(8,128)(2,1)}, bf16[4,48,1152]{2,1,0:T(8,128)(2,1)S(1)}, u32[]{:S(2)}, u32[]{:S(2)}) collective-permute-start(bf16[4,48,1152]{2,1,0:T(8,128)(2,1)} %get-tuple-element.318), channel_id=1, source_target_pairs={{0,2},{1,3},{2,0},{3,1},{4,6},{5,7},{6,4},{7,5},{8,10},{9,11},{10,... | collective-permute-start | bytes 1327112 | tf_op jit(solution)/shard_map/ppermute | solution.py:595
  356.9 28.9 %collective-permute-start.22 = (bf16[4,48,1152]{2,1,0:T(8,128)(2,1)}, bf16[4,48,1152]{2,1,0:T(8,128)(2,1)S(1)}, u32[]{:S(2)}, u32[]{:S(2)}) collective-permute-start(bf16[4,48,1152]{2,1,0:T(8,128)(2,1)} %get-tuple-element.317), channel_id=1, source_target_pairs={{0,3},{1,2},{2,1},{3,0},{4,7},{5,6},{6,5},{7,4},{8,11},{9,10},{10,... | collective-permute-start | bytes 1327112 | tf_op jit(solution)/shard_map/ppermute | solution.py:595
  398.7 22.1 %collective-permute-start.24 = (bf16[768,3456]{1,0:T(8,128)(2,1)}, bf16[768,3456]{1,0:T(8,128)(2,1)}, u32[]{:S(2)}, u32[]{:S(2)}) collective-permute-start(bf16[768,3456]{1,0:T(8,128)(2,1)} %grads_feed_away.1), channel_id=1, source_target_pairs={{0,16},{16,0},{1,17},{17,1},{2,18},{18,2},{3,19},{19,3},{4,20},{20... | collective-permute-start | bytes 15925256 | tf_op jit(solution)/shard_map/ppermute | solution.py:591
  428.4 41.7 %collective-permute-start.28 = (bf16[4,48,3456]{2,1,0:T(8,128)(2,1)}, bf16[4,48,3456]{2,1,0:T(8,128)(2,1)S(1)}, u32[]{:S(2)}, u32[]{:S(2)}) collective-permute-start(bf16[4,48,3456]{2,1,0:T(8,128)(2,1)} %get-tuple-element.315), channel_id=1, source_target_pairs={{0,1},{1,0},{2,3},{3,2},{4,5},{5,4},{6,7},{7,6},{8,9},{9,8},{10,11... | collective-permute-start | bytes 3981320 | tf_op jit(solution)/shard_map/ppermute | solution.py:595
  428.9 63.7 %collective-permute-start.29 = (bf16[4,48,3456]{2,1,0:T(8,128)(2,1)}, bf16[4,48,3456]{2,1,0:T(8,128)(2,1)}, u32[]{:S(2)}, u32[]{:S(2)}) collective-permute-start(bf16[4,48,3456]{2,1,0:T(8,128)(2,1)} %get-tuple-element.314), channel_id=1, source_target_pairs={{0,2},{1,3},{2,0},{3,1},{4,6},{5,7},{6,4},{7,5},{8,10},{9,11},{10,... | collective-permute-start | bytes 3981320 | tf_op jit(solution)/shard_map/ppermute | solution.py:595
  429.1 63.6 %collective-permute-start.30 = (bf16[4,48,3456]{2,1,0:T(8,128)(2,1)}, bf16[4,48,3456]{2,1,0:T(8,128)(2,1)}, u32[]{:S(2)}, u32[]{:S(2)}) collective-permute-start(bf16[4,48,3456]{2,1,0:T(8,128)(2,1)} %get-tuple-element.313), channel_id=1, source_target_pairs={{0,3},{1,2},{2,1},{3,0},{4,7},{5,6},{6,5},{7,4},{8,11},{9,10},{10,... | collective-permute-start | bytes 3981320 | tf_op jit(solution)/shard_map/ppermute | solution.py:595
  516.8 27.9 %collective-permute-start.35 = (bf16[4,48,1152]{2,1,0:T(8,128)(2,1)}, bf16[4,48,1152]{2,1,0:T(8,128)(2,1)}, u32[]{:S(2)}, u32[]{:S(2)}) collective-permute-start(bf16[4,48,1152]{2,1,0:T(8,128)(2,1)} %get-tuple-element.324), channel_id=1, source_target_pairs={{0,1},{1,0},{2,3},{3,2},{4,5},{5,4},{6,7},{7,6},{8,9},{9,8},{10,11... | collective-permute-start | bytes 1327112 | tf_op jit(solution)/shard_map/ppermute | solution.py:595
  517.7 27.0 %collective-permute-start.36 = (bf16[4,48,1152]{2,1,0:T(8,128)(2,1)}, bf16[4,48,1152]{2,1,0:T(8,128)(2,1)}, u32[]{:S(2)}, u32[]{:S(2)}) collective-permute-start(bf16[4,48,1152]{2,1,0:T(8,128)(2,1)} %get-tuple-element.323), channel_id=1, source_target_pairs={{0,2},{1,3},{2,0},{3,1},{4,6},{5,7},{6,4},{7,5},{8,10},{9,11},{10,... | collective-permute-start | bytes 1327112 | tf_op jit(solution)/shard_map/ppermute | solution.py:595
  519.3 25.4 %collective-permute-start.37 = (bf16[4,48,1152]{2,1,0:T(8,128)(2,1)}, bf16[4,48,1152]{2,1,0:T(8,128)(2,1)}, u32[]{:S(2)}, u32[]{:S(2)}) collective-permute-start(bf16[4,48,1152]{2,1,0:T(8,128)(2,1)} %get-tuple-element.322), channel_id=1, source_target_pairs={{0,3},{1,2},{2,1},{3,0},{4,7},{5,6},{6,5},{7,4},{8,11},{9,10},{10,... | collective-permute-start | bytes 1327112 | tf_op jit(solution)/shard_map/ppermute | solution.py:595
  519.8 24.9 %collective-permute-start.39 = (bf16[1,48,3456]{2,1,0:T(8,128)(2,1)}, bf16[1,48,3456]{2,1,0:T(8,128)(2,1)}, u32[]{:S(2)}, u32[]{:S(2)}) collective-permute-start(bf16[1,48,3456]{2,1,0:T(8,128)(2,1)} %get-tuple-element.327), channel_id=1, source_target_pairs={{0,8},{1,9},{2,10},{3,11},{4,12},{5,13},{6,14},{7,15},{8,0},{9,1},... | collective-permute-start | bytes 995336 | tf_op jit(solution)/shard_map/ppermute | solution.py:595
  521.5 23.2 %collective-permute-start.40 = (bf16[1,48,3456]{2,1,0:T(8,128)(2,1)}, bf16[1,48,3456]{2,1,0:T(8,128)(2,1)}, u32[]{:S(2)}, u32[]{:S(2)}) collective-permute-start(bf16[1,48,3456]{2,1,0:T(8,128)(2,1)} %get-tuple-element.326), channel_id=1, source_target_pairs={{0,12},{1,13},{2,14},{3,15},{4,8},{5,9},{6,10},{7,11},{8,4},{9,5},... | collective-permute-start | bytes 995336 | tf_op jit(solution)/shard_map/ppermute | solution.py:595
  (70 other events, 857.4 us)
Sparse Core Ops, SparseCore 0:
  13.3 109.5 all-gather.2
  126.4 88.6 all-gather.4
  282.9 164.5 reduce-scatter.1
